TPU v7x, 256 devices: a whole 4x4x8 slice. The times are simulated.
256 devices in a mesh: bond: 32 (over z, y), mpo: 8 (over x, core).
Axes of the slice: x: 4, y: 4, z: 8, core: 2. Of those that a mesh axis runs over, the one named last changes fastest.
Arguments:
- wavefunction: bfloat16 [2048, 128, 128], P('bond'), may hold values from -6 to 6
- left_environment: bfloat16 [40, 512, 128, 128], P('mpo', 'bond'), may hold values from -0.5 to 0.5
- right_environment: bfloat16 [40, 512, 128, 128], P('mpo', 'bond'), may hold values from -0.078125 to 0.078125
- right_sector: int32 [2048], P('bond'), may hold values from 0 to 511, as said below
Outputs:
- product: bfloat16 [2048, 128, 128], P('bond', 'mpo')
Inputs may be any that keep to these rules, and one draw needn't show every extreme that they name: `right_sector`: sector s is owned by index s // 16 of bond. Among the blocks of one device (aligned runs of 64 blocks), at most 3 name right sectors of one owner; in every draw one owner receives exactly 3 from every run.
All inputs are finite; a program needn't handle non-finite values.
Results may differ from a plain program's by a relative error of at most 0.005.
Values may be sent and summed in bfloat16 or wider, within the bound.
No kernel may reach another device: no remote copies, remote signals or barrier semaphores. Data moves between devices by JAX's collectives and lax.ppermute only.
A program may use at most 128 MiB of HBM per device.

v0:
```python
import jax
import jax.numpy as jnp
from jax import lax
from jax.sharding import PartitionSpec as P


def on_device(wavefunction, left_environment, right_environment, right_sector):
    peers = lax.axis_size("bond")
    blocks_here = wavefunction.shape[0]
    width = wavefunction.shape[1]
    terms = left_environment.shape[0]
    owned = left_environment.shape[1]
    members = blocks_here // owned
    capacity = max(2, (3 * blocks_here + 2 * peers - 1) // (2 * peers))
    grouped = wavefunction.reshape(owned, members, width, width)
    mixed = jnp.einsum(
        "wsij,sgjk->sgwik", left_environment, grouped, preferred_element_type=jnp.float32
    )
    mixed = mixed.astype(jnp.bfloat16).reshape(blocks_here, terms, width, width)
    destination = right_sector // owned
    local_sector = right_sector % owned
    onehot = (destination[:, None] == jnp.arange(peers, dtype=jnp.int32)[None, :]).astype(jnp.int32)
    position = jnp.sum((jnp.cumsum(onehot, axis=0) - onehot) * onehot, axis=1)
    slot_index = destination * capacity + position
    outgoing = (
        jnp.zeros((peers * capacity, terms, width, width), jnp.bfloat16).at[slot_index].set(mixed)
    )
    outgoing = outgoing.reshape(peers, capacity, terms, width, width)
    sector_slots = jnp.zeros((peers * capacity,), jnp.int32).at[slot_index].set(local_sector)
    sector_slots = sector_slots.reshape(peers, capacity)
    arrived = lax.all_to_all(outgoing, "bond", split_axis=0, concat_axis=0, tiled=True)
    sectors = lax.all_to_all(sector_slots, "bond", split_axis=0, concat_axis=0, tiled=True)
    chosen = jnp.take(right_environment, sectors, axis=1)
    partial_value = jnp.einsum(
        "dnwil,wdnml->dnim", arrived, chosen, preferred_element_type=jnp.float32
    )
    returned = lax.all_to_all(partial_value, "bond", split_axis=0, concat_axis=0, tiled=True)
    flat = returned.reshape((peers * capacity,) + returned.shape[2:])
    gathered = flat[slot_index]
    return lax.psum_scatter(gathered, "mpo", scatter_dimension=1, tiled=True).astype(jnp.bfloat16)


def solution(mesh):
    placed = (
        P("bond", None, None),
        P("mpo", "bond", None, None),
        P("mpo", "bond", None, None),
        P("bond"),
    )
    return jax.shard_map(
        on_device, mesh=mesh, in_specs=placed, out_specs=P("bond", "mpo", None), check_vma=False
    )
```

profile of v0, /device:TPU:1, one launch (start us, length us, event | category | flops | bytes accessed | tf_op | source)
XLA Modules:
  0.0 682.1 jit_solution(6956023274518041595)
XLA Ops:
  6.5 0.0 copy-start
  6.5 0.8 and_select_fusion
  7.4 0.1 fusion.9
  7.4 0.1 reduce_window_sum.11
  7.5 0.2 select_reduce_fusion
  7.7 0.8 scatter_custom_fusion.1
  8.5 0.7 all_to_all.17
  9.2 12.0 %all-to-all-start.1 = ((s32[32,1,3]{2,1,0:T(1,128)}), s32[32,1,3]{2,1,0:T(1,128)S(1)}, u32[]{:S(2)}, u32[]{:S(2)}) async-start(s32[32,1,3]{2,1,0:T(1,128)} %bitcast.6), calls=%async_computation.1 | async-start | bytes 32768 | tf_op jit(solution)/shard_map/all_to_all | solution.py:32
  21.3 9.1 %convolution_convert_fusion = bf16[16,4,128,5,128]{4,2,3,1,0:T(8,128)(2,1)} fusion(bf16[16,4,128,128,1]{3,2,4,1,0:T(8,128)(2,1)} %bitcast.37, bf16[5,16,128,128]{3,2,1,0:T(8,128)(2,1)} %param.5), kind=kOutput, calls=%fused_computation.9 | convolution fusion | flops 1347420160 | bytes 15204352 | tf_op jit(solution)/shard_map/wsij,sgjk->sgwik/dot_general | solution.py:16
  30.4 15.3 %copy.20 = bf16[64,5,128,128]{3,2,1,0:T(8,128)(2,1)} copy(bf16[64,5,128,128]{2,3,1,0:T(8,128)(2,1)} %bitcast.35) | data formatting | bytes 20971520 | tf_op jit(solution)/shard_map/reshape | solution.py:19
  45.7 9.5 %broadcast_in_dim.23 = bf16[96,5,128,128]{3,2,1,0:T(8,128)(2,1)} broadcast(bf16[]{:T(256)} %constant.44.clone.1), dimensions={} | broadcast | bytes 15728642 | tf_op jit(solution)/shard_map/broadcast_in_dim | solution.py:26
  55.2 24.7 %scatter_fusion = bf16[96,5,128,128]{3,2,1,0:T(8,128)(2,1)} fusion(bf16[96,5,128,128]{3,2,1,0:T(8,128)(2,1)} %broadcast_in_dim.23, s32[64]{0:T(128)S(1)} %compare_select_fusion.2, bf16[64,5,128,128]{3,2,1,0:T(8,128)(2,1)} %copy.20), kind=kCustom, calls=%fused_computation.2 | custom fusion | bytes 31457536 | tf_op jit(solution)/shard_map/scatter | solution.py:26
  80.0 0.0 all-to-all-done.1
  80.0 9.3 %all-to-all-start = ((bf16[32,3,5,128,128]{4,3,2,1,0:T(8,128)(2,1)}), bf16[32,3,5,128,128]{4,3,2,1,0:T(8,128)(2,1)}, u32[]{:S(2)}, u32[]{:S(2)}) async-start(bf16[32,3,5,128,128]{4,3,2,1,0:T(8,128)(2,1)} %bitcast.34), calls=%async_computation | async-start | bytes 31457280 | tf_op jit(solution)/shard_map/all_to_all | solution.py:31
  89.2 0.1 copy.24
  89.3 0.1 copy.25
  89.4 0.1 reshape.57
  89.5 0.1 copy.22
  89.6 0.1 copy.23
  89.7 0.0 copy-done
  89.7 8.0 %gather_fusion = bf16[96,5,128,128]{3,2,1,0:T(8,128)(2,1)} fusion(bf16[5,16,128,128]{3,2,1,0:T(8,128)(2,1)S(1)} %copy-done, s32[1024]{0:T(1024)S(1)} %pad_clamp_fusion.1), kind=kCustom, calls=%fused_computation | custom fusion | bytes 31457664 | tf_op jit(solution)/shard_map/jit(_take)/gather | solution.py:33
  97.7 342.3 %all-to-all-done = bf16[32,3,5,128,128]{4,3,2,1,0:T(8,128)(2,1)} async-done(((bf16[32,3,5,128,128]{4,3,2,1,0:T(8,128)(2,1)}), bf16[32,3,5,128,128]{4,3,2,1,0:T(8,128)(2,1)}, u32[]{:S(2)}, u32[]{:S(2)}) %all-to-all-start) | async-done | bytes 15728672 | tf_op jit(solution)/shard_map/all_to_all | solution.py:31
  440.1 15.8 %fusion.5 = f32[32,3,128,128]{3,2,1,0:T(8,128)} fusion(bf16[32,3,5,128,128]{4,3,2,1,0:T(8,128)(2,1)} %all-to-all-done, bf16[32,3,5,128,128]{4,3,2,1,0:T(8,128)(2,1)} %bitcast.36, pred[32,3]{1,0:T(8,128)(4,1)S(1)} %copy.23), kind=kOutput, calls=%fused_computation.10 | convolution fusion | flops 2021130240 | bytes 37748832 | tf_op jit(solution)/shard_map/dnwil,wdnml->dnim/dot_general | solution.py:34
  455.8 30.0 %all-to-all-start.2 = ((f32[32,3,128,128]{3,2,1,0:T(8,128)}), f32[32,3,128,128]{3,2,1,0:T(8,128)}, u32[]{:S(2)}, u32[]{:S(2)}) async-start(f32[32,3,128,128]{3,2,1,0:T(8,128)} %fusion.5), calls=%async_computation.2 | async-start | bytes 12582912 | tf_op jit(solution)/shard_map/all_to_all | solution.py:37
  485.8 0.0 reduce-scatter.2.cloned.1.call-start
  485.9 136.5 %all-to-all-done.2 = f32[32,3,128,128]{3,2,1,0:T(8,128)} async-done(((f32[32,3,128,128]{3,2,1,0:T(8,128)}), f32[32,3,128,128]{3,2,1,0:T(8,128)}, u32[]{:S(2)}, u32[]{:S(2)}) %all-to-all-start.2) | async-done | bytes 6291488 | tf_op jit(solution)/shard_map/all_to_all | solution.py:37
  622.4 5.6 gather_fusion.1
  628.1 0.0 reduce-scatter.2.cloned.1.call-update
  628.1 45.4 %reduce-scatter.2.cloned.1.call-done = f32[64,16,128]{2,1,0:T(8,128)} async-done(((f32[64,128,128]{2,1,0:T(8,128)}), f32[64,16,128]{2,1,0:T(8,128)}) %reduce-scatter.2.cloned.1.call-update) | async-done | bytes 524304 | tf_op jit(solution)/shard_map/reduce_scatter | solution.py:40
  673.5 1.8 convert_element_type.15
  (5 shorter events, 0.0 us)
Async XLA Ops:
  6.5 83.2 %copy-start = (bf16[5,16,128,128]{3,2,1,0:T(8,128)(2,1)S(1)}, bf16[5,16,128,128]{3,2,1,0:T(8,128)(2,1)}, u32[]{:S(2)}) copy-start(bf16[5,16,128,128]{3,2,1,0:T(8,128)(2,1)} %param.6) | copy-start | bytes 7864324
  9.2 70.7 %all-to-all-start.1 = ((s32[32,1,3]{2,1,0:T(1,128)}), s32[32,1,3]{2,1,0:T(1,128)S(1)}, u32[]{:S(2)}, u32[]{:S(2)}) async-start(s32[32,1,3]{2,1,0:T(1,128)} %bitcast.6), calls=%async_computation.1 | async-start | bytes 32768 | tf_op jit(solution)/shard_map/all_to_all | solution.py:32
  80.0 360.1 %all-to-all-start = ((bf16[32,3,5,128,128]{4,3,2,1,0:T(8,128)(2,1)}), bf16[32,3,5,128,128]{4,3,2,1,0:T(8,128)(2,1)}, u32[]{:S(2)}, u32[]{:S(2)}) async-start(bf16[32,3,5,128,128]{4,3,2,1,0:T(8,128)(2,1)} %bitcast.34), calls=%async_computation | async-start | bytes 31457280 | tf_op jit(solution)/shard_map/all_to_all | solution.py:31
  455.8 166.6 %all-to-all-start.2 = ((f32[32,3,128,128]{3,2,1,0:T(8,128)}), f32[32,3,128,128]{3,2,1,0:T(8,128)}, u32[]{:S(2)}, u32[]{:S(2)}) async-start(f32[32,3,128,128]{3,2,1,0:T(8,128)} %fusion.5), calls=%async_computation.2 | async-start | bytes 12582912 | tf_op jit(solution)/shard_map/all_to_all | solution.py:37
  485.8 187.7 %reduce-scatter.2.cloned.1.call-start = ((), (), s32[]{:S(2)}) async-start(), calls=%async_computation.4 | async-start | bytes 4718592 | tf_op jit(solution)/shard_map/reduce_scatter | solution.py:40
Sparse Core Ops, SparseCore 0:
  628.2 45.2 reduce-scatter.1
where the time goes:
time: 685 us; the launch traced here: 682 us
  waiting for transfers between devices  524 us (76%)
  local copies, waits for them, and re-layouts  65.1 us (10%)
  starting transfers between devices  51.3 us (7%)
  matrix products  24.9 us (4%)
  between operations  13.5 us (2%)
    all_to_all x1, waiting for transfers between devices, on_device(): lax.all_to_all(outgoing, 'bond', split_axis=0, concat_axis=0, tiled=True)  342 us
    all_to_all x1, waiting for transfers between devices, on_device(): lax.all_to_all(partial_value, 'bond', split_axis=0, concat_axis=0, tiled=...  137 us
    reduce_scatter x1, waiting for transfers between devices, on_device(): lax.psum_scatter(gathered, 'mpo', scatter_dimension=1, tiled=True)  45.4 us
    all_to_all x1, starting transfers between devices, on_device(): lax.all_to_all(partial_value, 'bond', split_axis=0, concat_axis=0, tiled=...  30 us
    scatter x1, local copies, waits for them, and re-layouts, on_device(): jnp.zeros((peers * capacity, terms, width, width), jnp.bfloat16)  24.7 us
    dot_general x1, matrix products, on_device(): jnp.einsum('dnwil,wdnml->dnim', arrived, chosen, preferred_element_type=j...  15.8 us
    reshape x1, local copies, waits for them, and re-layouts, on_device(): mixed = mixed.astype(jnp.bfloat16).reshape(blocks_here, terms, width, width)  15.3 us
  transfers between devices with their start and end apart: 4, of which 3 were waited for; matrix products, arithmetic and copies ran while one was open for 10% of the time, Pallas kernels for 0%

commit v1 on v0

v1 whole, which is shorter than its diff:
```python
import functools

import jax
import jax.numpy as jnp
from jax import lax
from jax.experimental import pallas as pl
from jax.experimental.pallas import tpu as pltpu
from jax.sharding import Mesh, PartitionSpec as P

Z, Y, M = 8, 4, 8
CAP = 3
SLOTS = Z * CAP
OFFSETS = (0, -1, 1, -2, 2, -3, 3, 4)
RANK = tuple(OFFSETS.index(((d + 3) % Z) - 3) for d in range(Z))
RIGHT = [(i, (i + 1) % Z) for i in range(Z)]
LEFT = [(i, (i - 1) % Z) for i in range(Z)]


def multiply_kernel(places, per_place, info_ref, *refs):
    count = len(places)
    slots = count * CAP
    psi = refs[:count]
    left = refs[count : count + slots]
    right = refs[count + slots : count + slots + slots * per_place]
    out_ref = refs[-1]
    home = pl.program_id(0)
    terms = left[0].shape[1]
    width = left[0].shape[-1]
    for p in range(count):
        for c in range(CAP):
            s = p * CAP + c
            blocks = left[s][0, :, 0].reshape(terms * width, width)
            mixed = jnp.dot(blocks, psi[p][0, c], preferred_element_type=jnp.float32)
            mixed = mixed.astype(jnp.bfloat16)
            mixed = jnp.concatenate(
                [mixed[w * width : (w + 1) * width] for w in range(terms)], axis=1
            )
            if per_place == 1:
                chosen = right[s][:, 0]
            else:
                half = right[2 * s].shape[1]
                sector = info_ref[home * SLOTS + places[p] * CAP + c] % 16
                chosen = jnp.where(sector < 8, right[2 * s][:, 0], right[2 * s + 1][:, 0])
            chosen = jnp.concatenate([chosen[w] for w in range(terms)], axis=1)
            total = lax.dot_general(
                mixed, chosen, (((1,), (1,)), ((), ())), preferred_element_type=jnp.float32
            )
            out_ref[0, :, s] = total.astype(jnp.bfloat16).reshape(M, width // M, width)


def multiply(places, info, psi, left, rights):
    terms, width = left.shape[1], left.shape[-1]
    slots = len(places) * CAP
    per_place = 2 if isinstance(rights[0], tuple) else 1
    in_specs, operands = [], []
    for p in places:
        in_specs.append(pl.BlockSpec((1, CAP, width, width), lambda h, info, p=p: (h, p, 0, 0)))
        operands.append(psi)
    for p in places:
        for c in range(CAP):
            q = p * CAP + c
            in_specs.append(
                pl.BlockSpec(
                    (1, terms, 1, width, width),
                    lambda h, info, q=q: (h, 0, info[h * SLOTS + q] // 16, 0, 0),
                )
            )
            operands.append(left)
    for i, p in enumerate(places):
        for c in range(CAP):
            q = p * CAP + c
            if per_place == 1:
                in_specs.append(
                    pl.BlockSpec(
                        (terms, 1, width, width),
                        lambda h, info, q=q: (0, info[h * SLOTS + q] % 16, 0, 0),
                    )
                )
                operands.append(rights[i])
            else:
                low, high = rights[i]
                in_specs.append(
                    pl.BlockSpec(
                        (terms, 1, width, width),
                        lambda h, info, q=q: (0, jnp.minimum(info[h * SLOTS + q] % 16, 7), 0, 0),
                    )
                )
                in_specs.append(
                    pl.BlockSpec(
                        (terms, 1, width, width),
                        lambda h, info, q=q: (0, jnp.maximum(info[h * SLOTS + q] % 16, 8) - 8, 0, 0),
                    )
                )
                operands += [low, high]
    flops = 2 * 2 * Y * slots * terms * width**3
    moved = Y * slots * (2 * terms + 2) * width * width * 2
    return pl.pallas_call(
        functools.partial(multiply_kernel, tuple(places), per_place),
        out_shape=jax.ShapeDtypeStruct((Y, M, slots, width // M, width), jnp.bfloat16),
        grid_spec=pltpu.PrefetchScalarGridSpec(
            num_scalar_prefetch=1,
            grid=(Y,),
            in_specs=in_specs,
            out_specs=pl.BlockSpec(
                (1, M, slots, width // M, width), lambda h, info: (h, 0, 0, 0, 0)
            ),
        ),
        compiler_params=pltpu.CompilerParams(vmem_limit_bytes=40 * 1024 * 1024),
        cost_estimate=pl.CostEstimate(flops=flops, bytes_accessed=moved, transcendentals=0),
    )(info, *operands)


def on_device(wavefunction, left_environment, right_environment, right_sector):
    here = lax.axis_index("z")
    blocks = wavefunction.shape[0]
    owned = left_environment.shape[1]
    members = blocks // owned

    from_left, from_right = right_environment, right_environment
    arrived = [right_environment]
    for _ in range(3):
        from_left = lax.ppermute(from_left, "z", RIGHT)
        from_right = lax.ppermute(from_right, "z", LEFT)
        arrived += [from_left, from_right]
    half = owned // 2
    low = lax.ppermute(from_left[:, :half], "z", RIGHT)
    high = lax.ppermute(from_right[:, half:], "z", LEFT)
    arrived.append((low, high))

    lefts = lax.all_gather(left_environment, "y", axis=0, tiled=False)

    owner = right_sector // owned
    same = owner[:, None] == owner[None, :]
    index = jnp.arange(blocks, dtype=jnp.int32)
    place = jnp.sum((same & (index[None, :] < index[:, None])).astype(jnp.int32), axis=1)
    offset = (owner // Y - here) % Z
    rank = jnp.sum(
        jnp.where(offset[:, None] == jnp.arange(Z)[None, :], jnp.array(RANK, jnp.int32)[None, :], 0),
        axis=1,
    )
    slot = (owner % Y) * SLOTS + rank * CAP + place
    filled = slot[None, :] == jnp.arange(Y * SLOTS, dtype=jnp.int32)[:, None]
    source = jnp.sum(jnp.where(filled, index[None, :], 0), axis=1)
    detail = (index // members) * 16 + right_sector % owned
    detail = jnp.sum(jnp.where(filled, detail[None, :], 0), axis=1)
    outgoing = wavefunction.at[source].get(mode="promise_in_bounds").reshape((Y, SLOTS) + wavefunction.shape[1:])
    psi = lax.all_to_all(outgoing, "y", split_axis=0, concat_axis=0, tiled=True)
    info = lax.all_to_all(detail.reshape(Y, SLOTS), "y", split_axis=0, concat_axis=0, tiled=True)
    info = info.reshape(-1)

    picks = filled.T.astype(jnp.bfloat16).reshape(blocks, Y, SLOTS)
    total = jnp.zeros((), jnp.float32)
    for places in ((0, 1, 2, 3, 4), (5, 6), (7,)):
        part = multiply(places, info, psi, lefts, [arrived[p] for p in places])
        part = part.reshape((Y * M,) + part.shape[2:])
        part = lax.all_to_all(part, ("y", "mpo"), split_axis=0, concat_axis=0, tiled=True)
        part = part.reshape((Y, M) + part.shape[1:]).astype(jnp.float32).sum(axis=1)
        part = part.astype(jnp.bfloat16)
        pick = picks[:, :, places[0] * CAP : (places[-1] + 1) * CAP]
        total = total + jnp.einsum("kys,ysil->kil", pick, part, preferred_element_type=jnp.float32)
    return total.astype(jnp.bfloat16)


def solution(mesh):
    fine = Mesh(mesh.devices.reshape(Z, Y, M), ("z", "y", "mpo"))
    bond = ("z", "y")
    placed = (
        P(bond, None, None),
        P("mpo", bond, None, None),
        P("mpo", bond, None, None),
        P(bond),
    )
    return jax.shard_map(
        on_device, mesh=fine, in_specs=placed, out_specs=P(bond, "mpo", None), check_vma=False
    )
```

time: 685 us -> 326 us (0.48)
  waiting for transfers between devices: 524 us -> 202 us
  local copies, waits for them, and re-layouts: 65.1 us -> 20.2 us
  Pallas kernels: 0 us -> 35.8 us
  matrix products: 24.9 us -> 0.85 us
    all_to_all x3 -> x5, waiting for transfers between devices: 479 us -> 27.4 us  [the longest x3 25.9 us: on_device(): lax.all_to_all(part, ('y', 'mpo'), split_axis=0, concat_axis=0, tiled=True)]
    ppermute x0 -> x8, waiting for transfers between devices: none -> 174 us  [the longest x3 150 us: on_device(): from_left = lax.ppermute(from_left, 'z', RIGHT)]
    reduce_scatter x1 -> x0, waiting for transfers between devices: 45.4 us -> none  [on_device(): lax.psum_scatter(gathered, 'mpo', scatter_dimension=1, tiled=True)]
    pallas_call x0 -> x3, Pallas kernels: none -> 35.8 us  [multiply(): pl.pallas_call(functools.partial(multiply_kernel, tuple(places), per_plac...]
    scatter x2 -> x0, local copies, waits for them, and re-layouts: 25.5 us -> none  [the longest x1 24.7 us: on_device(): jnp.zeros((peers * capacity, terms, width, width), jnp.bfloat16)]
    dot_general x2 -> x3, matrix products: 24.9 us -> 0.85 us  [on_device(): jnp.einsum('kys,ysil->kil', pick, part, preferred_element_type=jnp.float32)]
    all_to_all x3 -> x5, starting transfers between devices: 51.3 us -> 34.2 us  [the longest x3 25.6 us: on_device(): lax.all_to_all(part, ('y', 'mpo'), split_axis=0, concat_axis=0, tiled=True)]
    ppermute x0 -> x8, starting transfers between devices: none -> 15.4 us  [the longest x3 10.2 us: on_device(): from_right = lax.ppermute(from_right, 'z', LEFT)]
  transfers between devices with their start and end apart: 4 -> 14, of which waited for: 3 -> 9; matrix products, arithmetic and copies ran while one was open for 10% -> 3% of each run, Pallas kernels for 0% -> 9%
where the time goes in v1:
time: 326 us; the launch traced here: 325 us
  waiting for transfers between devices  202 us (62%)
  starting transfers between devices  49.7 us (15%)
  Pallas kernels  35.8 us (11%)
  local copies, waits for them, and re-layouts  20.2 us (6%)
  between operations  13.5 us (4%)
    ppermute x3, waiting for transfers between devices, on_device(): from_left = lax.ppermute(from_left, 'z', RIGHT)  150 us
    pallas_call x3, Pallas kernels, multiply(): pl.pallas_call(functools.partial(multiply_kernel, tuple(places), per_plac...  35.8 us
    all_to_all x3, waiting for transfers between devices, on_device(): lax.all_to_all(part, ('y', 'mpo'), split_axis=0, concat_axis=0, tiled=True)  25.9 us
    all_to_all x3, starting transfers between devices, on_device(): lax.all_to_all(part, ('y', 'mpo'), split_axis=0, concat_axis=0, tiled=True)  25.6 us
    ppermute x1, waiting for transfers between devices, on_device(): low = lax.ppermute(from_left[:, :half], 'z', RIGHT)  22.2 us
    unnamed x20, local copies, waits for them, and re-layouts  10.3 us
    ppermute x3, starting transfers between devices, on_device(): from_right = lax.ppermute(from_right, 'z', LEFT)  10.2 us
  transfers between devices with their start and end apart: 14, of which 9 were waited for; matrix products, arithmetic and copies ran while one was open for 3% of the time, Pallas kernels for 9%

profile of v1, /device:TPU:1, one launch (start us, length us, event | category | flops | bytes accessed | tf_op | source)
XLA Modules:
  0.0 325.3 jit_solution(15325819531040402955)
XLA Ops:
  7.3 2.5 collective-permute-start
  9.8 4.0 %collective-permute-start.1 = (bf16[5,16,128,128]{3,2,1,0:T(8,128)(2,1)}, bf16[5,16,128,128]{3,2,1,0:T(8,128)(2,1)S(1)}, u32[]{:S(2)}, u32[]{:S(2)}) collective-permute-start(bf16[5,16,128,128]{3,2,1,0:T(8,128)(2,1)} %refs_22_.1), channel_id=1, source_target_pairs={{0,224},{32,0},{64,32},{96,64},{128,96},{160,128},{192,160},{224,1... | collective-permute-start | bytes 7864328 | tf_op jit(solution)/shard_map/ppermute | solution.py:123
  13.8 56.8 %collective-permute-done.refs_23_.refs_24_.refs_25_ = bf16[5,16,128,128]{3,2,1,0:T(8,128)(2,1)S(1)} collective-permute-done((bf16[5,16,128,128]{3,2,1,0:T(8,128)(2,1)}, bf16[5,16,128,128]{3,2,1,0:T(8,128)(2,1)S(1)}, u32[]{:S(2)}, u32[]{:S(2)}) %collective-permute-start) | collective-permute-done | bytes 2621472 | tf_op jit(solution)/shard_map/ppermute | solution.py:122
  70.7 1.5 copy-done.2
  72.1 2.7 collective-permute-start.3
  74.8 1.6 copy-done.4
  76.4 52.8 %collective-permute-done.2.refs_29_.refs_30_.refs_31_ = bf16[5,16,128,128]{3,2,1,0:T(8,128)(2,1)} collective-permute-done((bf16[5,16,128,128]{3,2,1,0:T(8,128)(2,1)S(1)}, bf16[5,16,128,128]{3,2,1,0:T(8,128)(2,1)}, u32[]{:S(2)}, u32[]{:S(2)}) %collective-permute-start.2) | collective-permute-done | bytes 2621472 | tf_op jit(solution)/shard_map/ppermute | solution.py:122
  129.6 3.5 %collective-permute-start.5 = (bf16[5,16,128,128]{3,2,1,0:T(8,128)(2,1)}, bf16[5,16,128,128]{3,2,1,0:T(8,128)(2,1)}, u32[]{:S(2)}, u32[]{:S(2)}) collective-permute-start(bf16[5,16,128,128]{3,2,1,0:T(8,128)(2,1)} %collective-permute-done.3.refs_32_.refs_33_.refs_34_), channel_id=1, source_target_pairs={{0,224},{32,0},{64,32},{96,64},{128,96},{160,128},{192,160},{224,1... | collective-permute-start | bytes 7864328 | tf_op jit(solution)/shard_map/ppermute | solution.py:123
  134.2 4.0 %all-to-all-start = ((s32[4,1,24]{2,1,0:T(1,128)}), s32[4,1,24]{2,1,0:T(1,128)S(1)}, u32[]{:S(2)}, u32[]{:S(2)}) async-start(s32[4,1,24]{2,1,0:T(1,128)} %bitcast.1), calls=%async_computation | async-start | bytes 4096 | tf_op jit(solution)/shard_map/all_to_all | solution.py:148
  138.2 2.7 gather_fusion
  140.9 1.4 all-to-all-done
  142.3 4.6 %all-to-all-start.1 = ((bf16[4,24,128,128]{3,2,1,0:T(8,128)(2,1)}), bf16[4,24,128,128]{3,2,1,0:T(8,128)(2,1)}, u32[]{:S(2)}, u32[]{:S(2)}) async-start(bf16[4,24,128,128]{3,2,1,0:T(8,128)(2,1)} %bitcast.66), calls=%async_computation.1 | async-start | bytes 6291456 | tf_op jit(solution)/shard_map/all_to_all | solution.py:147
  147.0 40.1 %collective-permute-done.4.refs_8_.refs_9_.refs_10_ = bf16[5,16,128,128]{3,2,1,0:T(8,128)(2,1)} collective-permute-done((bf16[5,16,128,128]{3,2,1,0:T(8,128)(2,1)}, bf16[5,16,128,128]{3,2,1,0:T(8,128)(2,1)}, u32[]{:S(2)}, u32[]{:S(2)}) %collective-permute-start.4) | collective-permute-done | bytes 2621472 | tf_op jit(solution)/shard_map/ppermute | solution.py:122
  187.0 2.6 slice.25
  189.6 2.5 slice.26
  192.1 2.7 collective-permute-start.7
  196.1 22.2 %collective-permute-done.6.refs_4_.refs_6_.refs_8_ = bf16[5,8,128,128]{3,2,1,0:T(8,128)(2,1)S(1)} collective-permute-done((bf16[5,8,128,128]{3,2,1,0:T(8,128)(2,1)}, bf16[5,8,128,128]{3,2,1,0:T(8,128)(2,1)S(1)}, u32[]{:S(2)}, u32[]{:S(2)}) %collective-permute-start.6) | collective-permute-done | bytes 1310752 | tf_op jit(solution)/shard_map/ppermute | solution.py:126
  218.3 1.6 collective-permute-done.7.refs_5_.refs_7_.refs_9_
  219.9 6.0 %shard_map.57 = bf16[4,8,3,16,128]{4,3,2,1,0:T(8,128)(2,1)S(1)} custom-call(s32[96]{0:T(128)S(1)} %reshape.63.info_ref, bf16[4,24,128,128]{3,2,1,0:T(8,128)(2,1)} %all-to-all-done.1.refs_0_.refs_1_.refs_2_.refs_3_.refs_4_, bf16[4,5,16,128,128]{4,3,2,1,0:T(8,128)(2,1)} %bitcast.42, bf16[4,5,16,128,128]{4,3,2,1,0:T(8,128)(2,1)} %bitcast.43, ...), custom_call_target="tpu_custom_call" | custom-call | flops 503316480 | bytes 4718592 | tf_op jit(solution)/shard_map/pallas_call | solution.py:97
  226.0 0.8 copy-done.7
  226.8 11.1 %all-to-all-start.4 = ((bf16[32,3,16,128]{3,2,1,0:T(8,128)(2,1)}), bf16[32,3,16,128]{3,2,1,0:T(8,128)(2,1)S(1)}, u32[]{:S(2)}, u32[]{:S(2)}) async-start(bf16[32,3,16,128]{3,2,1,0:T(8,128)(2,1)} %bitcast.41), calls=%async_computation.4 | async-start | bytes 786432 | tf_op jit(solution)/shard_map/all_to_all | solution.py:156
  237.8 9.8 %shard_map.56 = bf16[4,8,6,16,128]{4,3,2,1,0:T(8,128)(2,1)} custom-call(s32[96]{0:T(128)S(1)} %reshape.63.info_ref, bf16[4,24,128,128]{3,2,1,0:T(8,128)(2,1)} %all-to-all-done.1.refs_0_.refs_1_.refs_2_.refs_3_.refs_4_, bf16[4,24,128,128]{3,2,1,0:T(8,128)(2,1)} %all-to-all-done.1.refs_0_.refs_1_.refs_2_.refs_3_.refs_4_, ...), custom_call_target="tpu_custom_call" | custom-call | flops 1006632960 | bytes 9437184 | tf_op jit(solution)/shard_map/pallas_call | solution.py:97
  248.0 7.0 %all-to-all-start.3 = ((bf16[32,6,16,128]{3,2,1,0:T(8,128)(2,1)}), bf16[32,6,16,128]{3,2,1,0:T(8,128)(2,1)S(1)}, u32[]{:S(2)}, u32[]{:S(2)}) async-start(bf16[32,6,16,128]{3,2,1,0:T(8,128)(2,1)} %bitcast.11), calls=%async_computation.3 | async-start | bytes 1572864 | tf_op jit(solution)/shard_map/all_to_all | solution.py:156
  255.1 1.7 copy-done.1
  256.8 1.7 copy-done.3
  258.5 1.7 copy-done.5
  260.3 20.0 %shard_map.55 = bf16[4,8,15,16,128]{4,3,2,1,0:T(8,128)(2,1)S(1)} custom-call(s32[96]{0:T(128)S(1)} %reshape.63.info_ref, bf16[4,24,128,128]{3,2,1,0:T(8,128)(2,1)} %all-to-all-done.1.refs_0_.refs_1_.refs_2_.refs_3_.refs_4_, bf16[4,24,128,128]{3,2,1,0:T(8,128)(2,1)} %all-to-all-done.1.refs_0_.refs_1_.refs_2_.refs_3_.refs_4_, ...), custom_call_target="tpu_custom_call" | custom-call | flops 2516582400 | bytes 23592960 | tf_op jit(solution)/shard_map/pallas_call | solution.py:97
  280.3 1.3 copy-done.6
  281.5 7.5 %all-to-all-start.2 = ((bf16[32,15,16,128]{3,2,1,0:T(8,128)(2,1)}), bf16[32,15,16,128]{3,2,1,0:T(8,128)(2,1)}, u32[]{:S(2)}, u32[]{:S(2)}) async-start(bf16[32,15,16,128]{3,2,1,0:T(8,128)(2,1)} %bitcast.40), calls=%async_computation.2 | async-start | bytes 3932160 | tf_op jit(solution)/shard_map/all_to_all | solution.py:156
  289.9 25.5 %all-to-all-done.2 = bf16[32,15,16,128]{3,2,1,0:T(8,128)(2,1)} async-done(((bf16[32,15,16,128]{3,2,1,0:T(8,128)(2,1)}), bf16[32,15,16,128]{3,2,1,0:T(8,128)(2,1)}, u32[]{:S(2)}, u32[]{:S(2)}) %all-to-all-start.2) | async-done | bytes 1966112 | tf_op jit(solution)/shard_map/all_to_all | solution.py:156
  315.4 1.8 bitcast_reduce_fusion
  317.5 0.9 copy.18
  (43 shorter events, 4.9 us)
Async XLA Ops:
  6.5 131.7 %copy-start = (bf16[64,128,128]{2,1,0:T(8,128)(2,1)S(1)}, bf16[64,128,128]{2,1,0:T(8,128)(2,1)}, u32[]{:S(2)}) copy-start(bf16[64,128,128]{2,1,0:T(8,128)(2,1)} %param.5) | copy-start | bytes 6291460
  6.5 126.8 %copy-start.9 = (s32[8]{0:T(128)S(1)}, s32[8]{0:T(128)}, u32[]{:S(2)}) copy-start(s32[8]{0:T(128)} %constant.89.clone) | copy-start | bytes 100
  6.5 126.5 %copy-start.8 = (s32[64]{0:T(128)S(1)}, s32[64]{0:T(128)}, u32[]{:S(2)}) copy-start(s32[64]{0:T(128)} %param.8) | copy-start | bytes 772
  6.5 213.4 %all-gather.3.cloned.1.call-start = ((), (), s32[]{:S(2)}) async-start(), calls=%async_computation.5 | async-start | bytes 13107200 | tf_op jit(solution)/shard_map/all_gather | solution.py:130
  7.3 63.4 %collective-permute-start = (bf16[5,16,128,128]{3,2,1,0:T(8,128)(2,1)}, bf16[5,16,128,128]{3,2,1,0:T(8,128)(2,1)S(1)}, u32[]{:S(2)}, u32[]{:S(2)}) collective-permute-start(bf16[5,16,128,128]{3,2,1,0:T(8,128)(2,1)} %refs_22_.1), channel_id=1, source_target_pairs={{0,32},{32,64},{64,96},{96,128},{128,160},{160,192},{192,224},{224... | collective-permute-start | bytes 7864328 | tf_op jit(solution)/shard_map/ppermute | solution.py:122
  9.8 62.3 %collective-permute-start.1 = (bf16[5,16,128,128]{3,2,1,0:T(8,128)(2,1)}, bf16[5,16,128,128]{3,2,1,0:T(8,128)(2,1)S(1)}, u32[]{:S(2)}, u32[]{:S(2)}) collective-permute-start(bf16[5,16,128,128]{3,2,1,0:T(8,128)(2,1)} %refs_22_.1), channel_id=1, source_target_pairs={{0,224},{32,0},{64,32},{96,64},{128,96},{160,128},{192,160},{224,1... | collective-permute-start | bytes 7864328 | tf_op jit(solution)/shard_map/ppermute | solution.py:123
  70.7 58.5 %collective-permute-start.2 = (bf16[5,16,128,128]{3,2,1,0:T(8,128)(2,1)S(1)}, bf16[5,16,128,128]{3,2,1,0:T(8,128)(2,1)}, u32[]{:S(2)}, u32[]{:S(2)}) collective-permute-start(bf16[5,16,128,128]{3,2,1,0:T(8,128)(2,1)S(1)} %collective-permute-done.refs_23_.refs_24_.refs_25_), channel_id=1, source_target_pairs={{0,32},{32,64},{64,96},{96,128},{128,160},{160,192},{192,224},{224... | collective-permute-start | bytes 7864328 | tf_op jit(solution)/shard_map/ppermute | solution.py:122
  70.7 1.5 copy-start.2
  72.1 57.4 %collective-permute-start.3 = (bf16[5,16,128,128]{3,2,1,0:T(8,128)(2,1)S(1)}, bf16[5,16,128,128]{3,2,1,0:T(8,128)(2,1)}, u32[]{:S(2)}, u32[]{:S(2)}) collective-permute-start(bf16[5,16,128,128]{3,2,1,0:T(8,128)(2,1)S(1)} %collective-permute-done.1.refs_26_.refs_27_.refs_28_), channel_id=1, source_target_pairs={{0,224},{32,0},{64,32},{96,64},{128,96},{160,128},{192,160},{224,1... | collective-permute-start | bytes 7864328 | tf_op jit(solution)/shard_map/ppermute | solution.py:123
  74.8 1.6 copy-start.4
  129.2 57.8 %collective-permute-start.4 = (bf16[5,16,128,128]{3,2,1,0:T(8,128)(2,1)}, bf16[5,16,128,128]{3,2,1,0:T(8,128)(2,1)}, u32[]{:S(2)}, u32[]{:S(2)}) collective-permute-start(bf16[5,16,128,128]{3,2,1,0:T(8,128)(2,1)} %collective-permute-done.2.refs_29_.refs_30_.refs_31_), channel_id=1, source_target_pairs={{0,32},{32,64},{64,96},{96,128},{128,160},{160,192},{192,224},{224... | collective-permute-start | bytes 7864328 | tf_op jit(solution)/shard_map/ppermute | solution.py:122
  129.6 60.0 %collective-permute-start.5 = (bf16[5,16,128,128]{3,2,1,0:T(8,128)(2,1)}, bf16[5,16,128,128]{3,2,1,0:T(8,128)(2,1)}, u32[]{:S(2)}, u32[]{:S(2)}) collective-permute-start(bf16[5,16,128,128]{3,2,1,0:T(8,128)(2,1)} %collective-permute-done.3.refs_32_.refs_33_.refs_34_), channel_id=1, source_target_pairs={{0,224},{32,0},{64,32},{96,64},{128,96},{160,128},{192,160},{224,1... | collective-permute-start | bytes 7864328 | tf_op jit(solution)/shard_map/ppermute | solution.py:123
  134.2 8.1 %all-to-all-start = ((s32[4,1,24]{2,1,0:T(1,128)}), s32[4,1,24]{2,1,0:T(1,128)S(1)}, u32[]{:S(2)}, u32[]{:S(2)}) async-start(s32[4,1,24]{2,1,0:T(1,128)} %bitcast.1), calls=%async_computation | async-start | bytes 4096 | tf_op jit(solution)/shard_map/all_to_all | solution.py:148
  142.3 53.8 %all-to-all-start.1 = ((bf16[4,24,128,128]{3,2,1,0:T(8,128)(2,1)}), bf16[4,24,128,128]{3,2,1,0:T(8,128)(2,1)}, u32[]{:S(2)}, u32[]{:S(2)}) async-start(bf16[4,24,128,128]{3,2,1,0:T(8,128)(2,1)} %bitcast.66), calls=%async_computation.1 | async-start | bytes 6291456 | tf_op jit(solution)/shard_map/all_to_all | solution.py:147
  189.6 28.7 %collective-permute-start.6 = (bf16[5,8,128,128]{3,2,1,0:T(8,128)(2,1)}, bf16[5,8,128,128]{3,2,1,0:T(8,128)(2,1)S(1)}, u32[]{:S(2)}, u32[]{:S(2)}) collective-permute-start(bf16[5,8,128,128]{3,2,1,0:T(8,128)(2,1)} %slice.25), channel_id=1, source_target_pairs={{0,32},{32,64},{64,96},{96,128},{128,160},{160,192},{192,224},{224... | collective-permute-start | bytes 3932168 | tf_op jit(solution)/shard_map/ppermute | solution.py:126
  192.1 27.8 %collective-permute-start.7 = (bf16[5,8,128,128]{3,2,1,0:T(8,128)(2,1)}, bf16[5,8,128,128]{3,2,1,0:T(8,128)(2,1)}, u32[]{:S(2)}, u32[]{:S(2)}) collective-permute-start(bf16[5,8,128,128]{3,2,1,0:T(8,128)(2,1)} %slice.26), channel_id=1, source_target_pairs={{0,224},{32,0},{64,32},{96,64},{128,96},{160,128},{192,160},{224,1... | collective-permute-start | bytes 3932168 | tf_op jit(solution)/shard_map/ppermute | solution.py:127
  226.0 0.8 copy-start.7
  226.8 21.3 %all-to-all-start.4 = ((bf16[32,3,16,128]{3,2,1,0:T(8,128)(2,1)}), bf16[32,3,16,128]{3,2,1,0:T(8,128)(2,1)S(1)}, u32[]{:S(2)}, u32[]{:S(2)}) async-start(bf16[32,3,16,128]{3,2,1,0:T(8,128)(2,1)} %bitcast.41), calls=%async_computation.4 | async-start | bytes 786432 | tf_op jit(solution)/shard_map/all_to_all | solution.py:156
  248.0 33.5 %all-to-all-start.3 = ((bf16[32,6,16,128]{3,2,1,0:T(8,128)(2,1)}), bf16[32,6,16,128]{3,2,1,0:T(8,128)(2,1)S(1)}, u32[]{:S(2)}, u32[]{:S(2)}) async-start(bf16[32,6,16,128]{3,2,1,0:T(8,128)(2,1)} %bitcast.11), calls=%async_computation.3 | async-start | bytes 1572864 | tf_op jit(solution)/shard_map/all_to_all | solution.py:156
  255.0 1.7 copy-start.1
  256.8 1.7 copy-start.3
  258.5 1.7 copy-start.5
  280.2 1.3 copy-start.6
  281.5 33.9 %all-to-all-start.2 = ((bf16[32,15,16,128]{3,2,1,0:T(8,128)(2,1)}), bf16[32,15,16,128]{3,2,1,0:T(8,128)(2,1)}, u32[]{:S(2)}, u32[]{:S(2)}) async-start(bf16[32,15,16,128]{3,2,1,0:T(8,128)(2,1)} %bitcast.40), calls=%async_computation.2 | async-start | bytes 3932160 | tf_op jit(solution)/shard_map/all_to_all | solution.py:156
Sparse Core Ops, SparseCore 0:
  9.2 107.2 all-gather.2

commit v2 on v0

v2 whole, which is shorter than its diff:
```python
import functools

import jax
import jax.numpy as jnp
from jax import lax
from jax.experimental import pallas as pl
from jax.experimental.pallas import tpu as pltpu
from jax.sharding import Mesh, PartitionSpec as P

Z, Y, X, C = 8, 4, 4, 2
M = X * C
CAP = 3
SLOTS = Z * CAP
OFFSETS = (0, -1, 1, -2, 2, -3, 3, 4)
RANK = tuple(OFFSETS.index(((d + 3) % Z) - 3) for d in range(Z))
RIGHT = [(i, (i + 1) % Z) for i in range(Z)]
LEFT = [(i, (i - 1) % Z) for i in range(Z)]


def left_products(blocks, psi):
    terms, width = blocks.shape[0], blocks.shape[-1]
    mixed = jnp.dot(
        blocks.reshape(terms * width, width), psi, preferred_element_type=jnp.float32
    ).astype(jnp.bfloat16)
    return jnp.concatenate([mixed[w * width : (w + 1) * width] for w in range(terms)], axis=1)


def times_right(mixed, chosen):
    total = lax.dot_general(
        mixed,
        jnp.concatenate([chosen[w, 0] for w in range(chosen.shape[0])], axis=1),
        (((1,), (1,)), ((), ())),
        preferred_element_type=jnp.float32,
    )
    width = total.shape[0]
    return total.astype(jnp.bfloat16).reshape(M, width // M, width)


def near_kernel(count, info_ref, *refs):
    slots = count * CAP
    psi = refs[:count]
    left = refs[count : count + slots]
    right = refs[count + slots : -1]
    out_ref = refs[-1]
    for s in range(slots):
        mixed = left_products(left[s][0, :, 0], psi[s // CAP][0, s % CAP])
        out_ref[0, :, s] = times_right(mixed, right[s])


def prepare_kernel(counts, info_ref, *refs):
    count = sum(counts)
    psi = refs[:count]
    left = refs[count : count + count * CAP]
    outs = refs[count + count * CAP :]
    s = 0
    for out_ref, n in zip(outs, counts):
        for i in range(n * CAP):
            out_ref[0, i] = left_products(left[s][0, :, 0], psi[s // CAP][0, s % CAP])
            s += 1


def far_kernel(info_ref, mixed_ref, *refs):
    for s in range(mixed_ref.shape[1]):
        refs[-1][0, :, s] = times_right(mixed_ref[0, s], refs[s])


def end_kernel(low_mixed, high_mixed, low, high, out_ref):
    for s in range(CAP):
        out_ref[0, 0, :, s] = times_right(low_mixed[0, s], low[:, s : s + 1])
        out_ref[1, 0, :, s] = times_right(high_mixed[0, s], high[:, s : s + 1])


def fetch_kernel(low_index, high_index, low_ref, high_ref, low_out, high_out):
    low_out[...] = low_ref[...]
    high_out[...] = high_ref[...]


PARAMS = pltpu.CompilerParams(vmem_limit_bytes=60 * 1024 * 1024)


def cost(slots, matmuls, terms, width):
    return pl.CostEstimate(
        flops=2 * slots * matmuls * terms * width**3,
        bytes_accessed=slots * (matmuls * terms + 2) * width * width * 2,
        transcendentals=0,
    )


def psi_and_left(places, psi, left):
    terms, width = left.shape[1], left.shape[-1]
    specs, operands = [], []
    for p in places:
        side, at = divmod(p, Z // C)
        specs.append(pl.BlockSpec((1, CAP, width, width), lambda h, info, at=at: (h, at, 0, 0)))
        operands.append(psi[side])
    for p in places:
        for q in range(p * CAP, (p + 1) * CAP):
            specs.append(
                pl.BlockSpec(
                    (1, terms, 1, width, width),
                    lambda h, info, q=q: (h, 0, info[h * SLOTS + q] // 16, 0, 0),
                )
            )
            operands.append(left)
    return specs, operands


def rights(places, arrived):
    specs, operands = [], []
    for p in places:
        for q in range(p * CAP, (p + 1) * CAP):
            terms, _, rows, width = arrived[p].shape
            specs.append(
                pl.BlockSpec(
                    (terms, 1, rows, width),
                    lambda h, info, q=q: (0, info[h * SLOTS + q] % 16, 0, 0),
                )
            )
            operands.append(arrived[p])
    return specs, operands


def product_shape(slots, width):
    out = jax.ShapeDtypeStruct((Y, M, slots, width // M, width), jnp.bfloat16)
    spec = pl.BlockSpec((1, M, slots, width // M, width), lambda h, info: (h, 0, 0, 0, 0))
    return out, spec


def near_products(places, info, psi, left, arrived):
    terms, width = left.shape[1], left.shape[-1]
    slots = len(places) * CAP
    specs, operands = psi_and_left(places, psi, left)
    more_specs, more = rights(places, arrived)
    out, out_spec = product_shape(slots, width)
    return pl.pallas_call(
        functools.partial(near_kernel, len(places)),
        out_shape=out,
        grid_spec=pltpu.PrefetchScalarGridSpec(
            num_scalar_prefetch=1, grid=(Y,), in_specs=specs + more_specs, out_specs=out_spec
        ),
        compiler_params=PARAMS,
        cost_estimate=cost(Y * slots, 2, terms, width),
    )(info, *operands, *more)


def prepare(groups, info, psi, left):
    terms, width = left.shape[1], left.shape[-1]
    specs, operands = psi_and_left(sum(groups, ()), psi, left)
    counts = tuple(len(g) for g in groups)
    return pl.pallas_call(
        functools.partial(prepare_kernel, counts),
        out_shape=[
            jax.ShapeDtypeStruct((Y, n * CAP, width, terms * width), jnp.bfloat16) for n in counts
        ],
        grid_spec=pltpu.PrefetchScalarGridSpec(
            num_scalar_prefetch=1,
            grid=(Y,),
            in_specs=specs,
            out_specs=[
                pl.BlockSpec((1, n * CAP, width, terms * width), lambda h, info: (h, 0, 0, 0))
                for n in counts
            ],
        ),
        compiler_params=PARAMS,
        cost_estimate=cost(Y * sum(counts) * CAP, 1, terms, width),
    )(info, *operands)


def far_products(places, info, mixed, arrived):
    slots, width = mixed.shape[1:3]
    terms = mixed.shape[3] // width
    specs, operands = rights(places, arrived)
    out, out_spec = product_shape(slots, width)
    mixed_spec = pl.BlockSpec((1,) + mixed.shape[1:], lambda h, info: (h, 0, 0, 0))
    return pl.pallas_call(
        far_kernel,
        out_shape=out,
        grid_spec=pltpu.PrefetchScalarGridSpec(
            num_scalar_prefetch=1, grid=(Y,), in_specs=[mixed_spec] + specs, out_specs=out_spec
        ),
        compiler_params=PARAMS,
        cost_estimate=cost(Y * slots, 2, terms, width),
    )(info, mixed, *operands)


def end_products(mixed, sent):
    side = Y // 2
    slots, width = mixed.shape[1:3]
    low, high = sent
    terms = low.shape[0]
    part = pl.BlockSpec((terms, CAP) + low.shape[2:], lambda g: (0, g, 0, 0))
    out = pl.pallas_call(
        end_kernel,
        out_shape=jax.ShapeDtypeStruct((2, side, M, slots, width // M, width), jnp.bfloat16),
        grid=(side,),
        in_specs=[
            pl.BlockSpec((1,) + mixed.shape[1:], lambda g: (g, 0, 0, 0)),
            pl.BlockSpec((1,) + mixed.shape[1:], lambda g: (g + side, 0, 0, 0)),
            part,
            part,
        ],
        out_specs=pl.BlockSpec(
            (2, 1, M, slots, width // M, width), lambda g: (0, g, 0, 0, 0, 0)
        ),
        compiler_params=PARAMS,
        cost_estimate=cost(Y * slots, 2, terms, width),
    )(mixed, mixed, low, high)
    return out.reshape((Y,) + out.shape[2:])


def fetch(low, high, low_index, high_index):
    terms, _, rows, width = low.shape
    count = low_index.shape[0]
    block = (terms, 1, rows, width)
    out = jax.ShapeDtypeStruct((terms, count, rows, width), low.dtype)
    out_spec = pl.BlockSpec(block, lambda i, low_index, high_index: (0, i, 0, 0))
    return pl.pallas_call(
        fetch_kernel,
        out_shape=[out, out],
        grid_spec=pltpu.PrefetchScalarGridSpec(
            num_scalar_prefetch=2,
            grid=(count,),
            in_specs=[
                pl.BlockSpec(block, lambda i, low_index, high_index: (0, low_index[i], 0, 0)),
                pl.BlockSpec(block, lambda i, low_index, high_index: (0, high_index[i], 0, 0)),
            ],
            out_specs=[out_spec, out_spec],
        ),
        compiler_params=PARAMS,
        cost_estimate=pl.CostEstimate(
            flops=0, bytes_accessed=4 * terms * count * rows * width * 2, transcendentals=0
        ),
    )(low_index, high_index, low, high)


def exchange(part):
    part = part.reshape((Y * M,) + part.shape[2:])
    part = lax.all_to_all(part, ("y", "x", "c"), split_axis=0, concat_axis=0, tiled=True)
    return part.reshape((Y, M) + part.shape[1:])


def on_device(wavefunction, left_environment, right_environment, right_sector):
    z, y, core = (lax.axis_index(name) for name in ("z", "y", "c"))
    blocks, width = wavefunction.shape[:2]
    owned = left_environment.shape[1]
    members = blocks // owned
    tie = lax.optimization_barrier

    lefts = lax.all_gather(left_environment, "y", axis=0, tiled=False)
    beyond = lax.ppermute(right_sector, "z", LEFT)
    before = lax.ppermute(right_sector, "z", RIGHT)
    start, beyond, before = tie((right_environment, beyond, before))

    index = jnp.arange(blocks, dtype=jnp.int32)
    earlier = index[None, :] < index[:, None]

    def slots_of(sectors, plane):
        owner = sectors // owned
        same = owner[:, :, None] == owner[:, None, :]
        place = jnp.sum((same & earlier).astype(jnp.int32), axis=2)
        offset = (owner // Y - plane) % Z
        rank = sum(jnp.where(offset == d, RANK[d], 0) for d in range(Z))
        return owner % Y, rank * CAP + place

    def into(slots, values, count, start=0):
        hit = slots[:, None, :] == jnp.arange(start, start + count, dtype=jnp.int32)[None, :, None]
        return jnp.sum(jnp.where(hit, values[:, None, :], 0), axis=2)

    column, slot = slots_of(right_sector[None], z)
    slot = column * SLOTS + slot
    split = SLOTS // C
    mine = (slot // SLOTS) * split + jnp.where((slot % SLOTS) // split == core, slot % split, -Y * SLOTS)
    source = into(mine, index[None], Y * split)[0]
    outgoing = wavefunction.at[source].get(mode="promise_in_bounds")
    outgoing = outgoing.reshape((Y, split) + wavefunction.shape[1:])

    planes = jnp.broadcast_to(jnp.stack([right_sector, beyond, before]), (Y, 3, blocks))
    planes = lax.all_to_all(planes, "y", split_axis=0, concat_axis=0, tiled=True)

    def for_this_column(sectors, plane):
        column, slots = slots_of(sectors, plane)
        return jnp.where(column == y, slots, -1)

    info = into(
        for_this_column(planes[:, 0], z), (index // members) * 16 + planes[:, 0] % owned, SLOTS
    ).reshape(-1)
    low, high = planes[: Y // 2, 1], planes[Y // 2 :, 2]
    wanted = [
        into(for_this_column(low, z + 1), low % owned, CAP, SLOTS - CAP).reshape(-1),
        into(for_this_column(high, z - 1), high % owned, CAP, SLOTS - CAP).reshape(-1),
    ]

    def step(moving):
        return [lax.ppermute(moving[0], "z", RIGHT), lax.ppermute(moving[1], "z", LEFT)]

    first = step([start, start])
    psi = lax.all_to_all(outgoing, "y", split_axis=0, concat_axis=0, tiled=True)
    first, psi, info, wanted = tie((first, psi, info, wanted))
    second = step(first)
    other = lax.ppermute(psi, "c", [(0, 1), (1, 0)])
    psi = (jnp.where(core == 0, psi, other), jnp.where(core == 0, other, psi))
    second, psi = tie((second, psi))
    third = step(second)
    arrived = [start] + first + second + third
    near = near_products((0, 1, 2, 3, 4), info, psi, lefts, arrived)
    far_mixed, end_mixed = prepare(((5, 6), (7,)), info, psi, lefts)
    wanted, near, far_mixed, end_mixed = tie((wanted, near, far_mixed, end_mixed))
    fourth = step(fetch(*third, *wanted))
    near = exchange(near)
    far = far_products((5, 6), info, far_mixed, arrived)
    end_mixed, far, near = tie((end_mixed, far, near))
    far = exchange(far)
    end = exchange(end_products(end_mixed, fourth))

    def gather(part, start):
        where = jnp.arange(Y)[:, None, None] * SLOTS + start + jnp.arange(part.shape[2])
        where = jnp.broadcast_to(where, part.shape[:3])
        pick = (slot[0][:, None, None, None] == where).astype(jnp.bfloat16)
        return jnp.einsum("kyms,ymsil->kil", pick, part, preferred_element_type=jnp.float32)

    total = gather(near, 0) + gather(far, 5 * CAP) + gather(end, 7 * CAP)
    return total.astype(jnp.bfloat16)


def solution(mesh):
    fine = Mesh(mesh.devices.reshape(Z, Y, X, C), ("z", "y", "x", "c"))
    bond = ("z", "y")
    placed = (
        P(bond, None, None),
        P(("x", "c"), bond, None, None),
        P(("x", "c"), bond, None, None),
        P(bond),
    )
    return jax.shard_map(
        on_device, mesh=fine, in_specs=placed, out_specs=P(bond, ("x", "c"), None), check_vma=False
    )
```

time: 685 us -> 252 us (0.37)
  waiting for transfers between devices: 524 us -> 122 us
  local copies, waits for them, and re-layouts: 65.1 us -> 6.2 us
  Pallas kernels: 0 us -> 43.8 us
  matrix products: 24.9 us -> 2.92 us
    all_to_all x3 -> x5, waiting for transfers between devices: 479 us -> 53.2 us  [the longest x1 32.4 us: on_device(): psi = lax.all_to_all(outgoing, 'y', split_axis=0, concat_axis=0, tiled=True)]
    ppermute x0 -> x11, waiting for transfers between devices: none -> 67.8 us  [the longest x4 61.2 us: step(): lax.ppermute(moving[0], 'z', RIGHT)]
    reduce_scatter x1 -> x0, waiting for transfers between devices: 45.4 us -> none  [on_device(): lax.psum_scatter(gathered, 'mpo', scatter_dimension=1, tiled=True)]
    pallas_call x0 -> x5, Pallas kernels: none -> 43.8 us  [the longest x1 20.9 us: near_products(): pl.pallas_call(functools.partial(near_kernel, len(places)), out_shape=out...]
    scatter x2 -> x0, local copies, waits for them, and re-layouts: 25.5 us -> none  [the longest x1 24.7 us: on_device(): jnp.zeros((peers * capacity, terms, width, width), jnp.bfloat16)]
    dot_general x2 -> x3, matrix products: 24.9 us -> 2.92 us  [gather(): jnp.einsum('kyms,ymsil->kil', pick, part, preferred_element_type=jnp.floa...]
    ppermute x0 -> x11, starting transfers between devices: none -> 20.7 us  [the longest x4 10.7 us: step(): lax.ppermute(moving[1], 'z', LEFT)]
    all_to_all x3 -> x5, starting transfers between devices: 51.3 us -> 36.5 us  [the longest x3 27.9 us: exchange(): lax.all_to_all(part, ('y', 'x', 'c'), split_axis=0, concat_axis=0, tiled=...]
  transfers between devices with their start and end apart: 4 -> 17, of which waited for: 3 -> 10; matrix products, arithmetic and copies ran while one was open for 10% -> 5% of each run, Pallas kernels for 0% -> 17%
where the time goes in v2:
time: 252 us; the launch traced here: 251 us
  waiting for transfers between devices  122 us (48%)
  starting transfers between devices  57.2 us (23%)
  Pallas kernels  43.8 us (17%)
  between operations  13.6 us (5%)
  local copies, waits for them, and re-layouts  6.2 us (2%)
  other arithmetic  5.98 us (2%)
  matrix products  2.92 us (1%)
    ppermute x4, waiting for transfers between devices, step(): lax.ppermute(moving[0], 'z', RIGHT)  61.2 us
    all_to_all x1, waiting for transfers between devices, on_device(): psi = lax.all_to_all(outgoing, 'y', split_axis=0, concat_axis=0, tiled=True)  32.4 us
    all_to_all x3, starting transfers between devices, exchange(): lax.all_to_all(part, ('y', 'x', 'c'), split_axis=0, concat_axis=0, tiled=...  27.9 us
    pallas_call x1, Pallas kernels, near_products(): pl.pallas_call(functools.partial(near_kernel, len(places)), out_shape=out...  20.9 us
    all_to_all x3, waiting for transfers between devices, exchange(): lax.all_to_all(part, ('y', 'x', 'c'), split_axis=0, concat_axis=0, tiled=...  18.5 us
    ppermute x4, starting transfers between devices, step(): lax.ppermute(moving[1], 'z', LEFT)  10.7 us
    pallas_call x1, Pallas kernels, prepare(): pl.pallas_call(functools.partial(prepare_kernel, counts), out_shape=[jax....  7.75 us
    ppermute x1, starting transfers between devices, on_device(): beyond = lax.ppermute(right_sector, 'z', LEFT)  6.41 us
  transfers between devices with their start and end apart: 17, of which 10 were waited for; matrix products, arithmetic and copies ran while one was open for 5% of the time, Pallas kernels for 17%

profile of v2, /device:TPU:1, one launch (start us, length us, event | category | flops | bytes accessed | tf_op | source)
XLA Modules:
  0.0 251.3 jit_solution(9809158673667639765)
XLA Ops:
  6.5 0.7 all-gather.3.cloned.1.call-update
  7.3 6.4 %collective-permute-start = (s32[64]{0:T(128)S(1)}, s32[64]{0:T(128)S(1)}, u32[]{:S(2)}, u32[]{:S(2)}) collective-permute-start(s32[64]{0:T(128)S(1)} %copy-done.1), channel_id=1, source_target_pairs={{0,224},{32,0},{64,32},{96,64},{128,96},{160,128},{192,160},{224,1... | collective-permute-start | bytes 776 | tf_op jit(solution)/shard_map/ppermute | solution.py:250
  14.5 2.9 %collective-permute-done.1 = s32[64]{0:T(128)S(1)} collective-permute-done((s32[64]{0:T(128)S(1)}, s32[64]{0:T(128)S(1)}, u32[]{:S(2)}, u32[]{:S(2)}) %collective-permute-start.1) | collective-permute-done | bytes 288 | tf_op jit(solution)/shard_map/ppermute | solution.py:251
  17.4 2.7 %collective-permute-start.3 = (bf16[5,16,128,128]{3,2,1,0:T(8,128)(2,1)}, bf16[5,16,128,128]{3,2,1,0:T(8,128)(2,1)}, u32[]{:S(2)}, u32[]{:S(2)}) collective-permute-start(bf16[5,16,128,128]{3,2,1,0:T(8,128)(2,1)} %refs_22_), channel_id=1, source_target_pairs={{0,224},{32,0},{64,32},{96,64},{128,96},{160,128},{192,160},{224,1... | collective-permute-start | bytes 7864328 | tf_op jit(solution)/shard_map/ppermute | solution.py:294
  20.1 0.7 reshape.474
  20.7 4.2 %all-to-all-start.1 = ((s32[4,1,192]{2,1,0:T(1,128)}), s32[4,1,192]{2,1,0:T(1,128)S(1)}, u32[]{:S(2)}, u32[]{:S(2)}) async-start(s32[4,1,192]{2,1,0:T(1,128)} %reshape.474), calls=%async_computation.1 | async-start | bytes 8192 | tf_op jit(solution)/shard_map/all_to_all | solution.py:278
  24.9 2.0 gather_fusion
  26.9 2.3 all-to-all-done.1
  29.2 4.4 %all-to-all-start = ((bf16[4,12,128,128]{3,2,1,0:T(8,128)(2,1)}), bf16[4,12,128,128]{3,2,1,0:T(8,128)(2,1)}, u32[]{:S(2)}, u32[]{:S(2)}) async-start(bf16[4,12,128,128]{3,2,1,0:T(8,128)(2,1)} %bitcast.116), calls=%async_computation | async-start | bytes 3145728 | tf_op jit(solution)/shard_map/all_to_all | solution.py:297
  34.1 0.7 reduce.2
  37.8 32.4 %all-to-all-done = bf16[4,12,128,128]{3,2,1,0:T(8,128)(2,1)} async-done(((bf16[4,12,128,128]{3,2,1,0:T(8,128)(2,1)}), bf16[4,12,128,128]{3,2,1,0:T(8,128)(2,1)}, u32[]{:S(2)}, u32[]{:S(2)}) %all-to-all-start) | async-done | bytes 1572896 | tf_op jit(solution)/shard_map/all_to_all | solution.py:297
  70.2 4.9 %collective-permute-done.2.refs_23_.refs_24_.refs_25_ = bf16[5,16,128,128]{3,2,1,0:T(8,128)(2,1)} collective-permute-done((bf16[5,16,128,128]{3,2,1,0:T(8,128)(2,1)}, bf16[5,16,128,128]{3,2,1,0:T(8,128)(2,1)}, u32[]{:S(2)}, u32[]{:S(2)}) %collective-permute-start.2) | collective-permute-done | bytes 2621472 | tf_op jit(solution)/shard_map/ppermute | solution.py:294
  75.1 2.7 %collective-permute-start.5 = (bf16[5,16,128,128]{3,2,1,0:T(8,128)(2,1)}, bf16[5,16,128,128]{3,2,1,0:T(8,128)(2,1)}, u32[]{:S(2)}, u32[]{:S(2)}) collective-permute-start(bf16[5,16,128,128]{3,2,1,0:T(8,128)(2,1)} %collective-permute-done.3.refs_26_.refs_27_.refs_28_), channel_id=1, source_target_pairs={{0,224},{32,0},{64,32},{96,64},{128,96},{160,128},{192,160},{224,1... | collective-permute-start | bytes 7864328 | tf_op jit(solution)/shard_map/ppermute | solution.py:294
  77.8 3.6 %collective-permute-start.6 = (bf16[4,12,128,128]{3,2,1,0:T(8,128)(2,1)}, bf16[4,12,128,128]{3,2,1,0:T(8,128)(2,1)}, u32[]{:S(2)}, u32[]{:S(2)}) collective-permute-start(bf16[4,12,128,128]{3,2,1,0:T(8,128)(2,1)} %all-to-all-done), channel_id=1, source_target_pairs={{0,1},{1,0},{2,3},{3,2},{4,5},{5,4},{6,7},{7,6},{8,9},{9,8},{10,11... | collective-permute-start | bytes 4718600 | tf_op jit(solution)/shard_map/ppermute | solution.py:300
  81.4 3.4 %collective-permute-done.6 = bf16[4,12,128,128]{3,2,1,0:T(8,128)(2,1)} collective-permute-done((bf16[4,12,128,128]{3,2,1,0:T(8,128)(2,1)}, bf16[4,12,128,128]{3,2,1,0:T(8,128)(2,1)}, u32[]{:S(2)}, u32[]{:S(2)}) %collective-permute-start.6) | collective-permute-done | bytes 1572896 | tf_op jit(solution)/shard_map/ppermute | solution.py:300
  84.8 3.8 %broadcast_select_fusion = (bf16[4,12,128,128]{3,2,1,0:T(8,128)(2,1)}, bf16[4,12,128,128]{3,2,1,0:T(8,128)(2,1)}) fusion(bf16[4,12,128,128]{3,2,1,0:T(8,128)(2,1)} %collective-permute-done.6, bf16[4,12,128,128]{3,2,1,0:T(8,128)(2,1)} %all-to-all-done, pred[]{:T(512)S(6)} %eq.404), kind=kLoop, calls=%fused_computation.3 | loop fusion | flops 1572864 | bytes 6291457 | tf_op jit(solution)/shard_map/jit(_where)/select_n | solution.py:301
  88.6 43.4 %collective-permute-done.4.refs_29_.refs_30_.refs_31_ = bf16[5,16,128,128]{3,2,1,0:T(8,128)(2,1)} collective-permute-done((bf16[5,16,128,128]{3,2,1,0:T(8,128)(2,1)}, bf16[5,16,128,128]{3,2,1,0:T(8,128)(2,1)}, u32[]{:S(2)}, u32[]{:S(2)}) %collective-permute-start.4) | collective-permute-done | bytes 2621472 | tf_op jit(solution)/shard_map/ppermute | solution.py:294
  132.0 2.7 %collective-permute-start.8 = (bf16[5,16,128,128]{3,2,1,0:T(8,128)(2,1)}, bf16[5,16,128,128]{3,2,1,0:T(8,128)(2,1)}, u32[]{:S(2)}, u32[]{:S(2)}) collective-permute-start(bf16[5,16,128,128]{3,2,1,0:T(8,128)(2,1)} %collective-permute-done.5.refs_32_.refs_33_.refs_34_), channel_id=1, source_target_pairs={{0,224},{32,0},{64,32},{96,64},{128,96},{160,128},{192,160},{224,1... | collective-permute-start | bytes 7864328 | tf_op jit(solution)/shard_map/ppermute | solution.py:294
  134.7 7.8 %shard_map.47 = (bf16[4,6,128,640]{3,2,1,0:T(8,128)(2,1)}, bf16[4,3,128,640]{3,2,1,0:T(8,128)(2,1)}) custom-call(s32[96]{0:T(128)} %reshape.451.info_ref, bf16[4,12,128,128]{3,2,1,0:T(8,128)(2,1)} %get-tuple-element.40.refs_4_.refs_0_.refs_1_.refs_2_, bf16[4,12,128,128]{3,2,1,0:T(8,128)(2,1)} %get-tuple-element.40.refs_4_.refs_0_.refs_1_.refs_2_, ...), custom_call_target="tpu_custom_call" | custom-call | flops 754974720 | bytes 8257536 | tf_op jit(solution)/shard_map/pallas_call | solution.py:150
  142.4 20.9 %shard_map.46 = bf16[4,8,15,16,128]{4,3,2,1,0:T(8,128)(2,1)} custom-call(s32[96]{0:T(128)} %reshape.451.info_ref, bf16[4,12,128,128]{3,2,1,0:T(8,128)(2,1)} %get-tuple-element.39.refs_0_.refs_1_.refs_2_.refs_3_, bf16[4,12,128,128]{3,2,1,0:T(8,128)(2,1)} %get-tuple-element.39.refs_0_.refs_1_.refs_2_.refs_3_, ...), custom_call_target="tpu_custom_call" | custom-call | flops 2516582400 | bytes 23592960 | tf_op jit(solution)/shard_map/pallas_call | solution.py:135
  163.3 11.7 %all-to-all-start.2 = ((bf16[32,15,16,128]{3,2,1,0:T(8,128)(2,1)}), bf16[32,15,16,128]{3,2,1,0:T(8,128)(2,1)}, u32[]{:S(2)}, u32[]{:S(2)}) async-start(bf16[32,15,16,128]{3,2,1,0:T(8,128)(2,1)} %bitcast.115), calls=%async_computation.2 | async-start | bytes 3932160 | tf_op jit(solution)/shard_map/all_to_all | solution.py:238
  175.0 12.9 %collective-permute-done.7.refs_0_.refs_1_.refs_2_.low_ref = bf16[5,16,128,128]{3,2,1,0:T(8,128)(2,1)} collective-permute-done((bf16[5,16,128,128]{3,2,1,0:T(8,128)(2,1)}, bf16[5,16,128,128]{3,2,1,0:T(8,128)(2,1)}, u32[]{:S(2)}, u32[]{:S(2)}) %collective-permute-start.7) | collective-permute-done | bytes 2621472 | tf_op jit(solution)/shard_map/ppermute | solution.py:294
  187.9 5.6 %shard_map.49 = (bf16[5,6,128,128]{3,2,1,0:T(8,128)(2,1)}, bf16[5,6,128,128]{3,2,1,0:T(8,128)(2,1)}) custom-call(s32[6]{0:T(128)} %reshape.452.low_index, s32[6]{0:T(128)} %reshape.453.high_index, bf16[5,16,128,128]{3,2,1,0:T(8,128)(2,1)} %collective-permute-done.7.refs_0_.refs_1_.refs_2_.low_ref, ...), custom_call_target="tpu_custom_call" | custom-call | bytes 3932160 | tf_op jit(solution)/shard_map/pallas_call | solution.py:217
  193.5 2.7 %collective-permute-start.10 = (bf16[5,6,128,128]{3,2,1,0:T(8,128)(2,1)}, bf16[5,6,128,128]{3,2,1,0:T(8,128)(2,1)}, u32[]{:S(2)}, u32[]{:S(2)}) collective-permute-start(bf16[5,6,128,128]{3,2,1,0:T(8,128)(2,1)} %get-tuple-element.54), channel_id=1, source_target_pairs={{0,224},{32,0},{64,32},{96,64},{128,96},{160,128},{192,160},{224,1... | collective-permute-start | bytes 2949128 | tf_op jit(solution)/shard_map/ppermute | solution.py:294
  196.2 6.3 %shard_map.48 = bf16[4,8,6,16,128]{4,3,2,1,0:T(8,128)(2,1)} custom-call(s32[96]{0:T(128)} %reshape.451.info_ref, bf16[4,6,128,640]{3,2,1,0:T(8,128)(2,1)} %get-tuple-element.46.mixed_ref, bf16[5,16,128,128]{3,2,1,0:T(8,128)(2,1)} %collective-permute-done.7.refs_0_.refs_1_.refs_2_.low_ref, ...), custom_call_target="tpu_custom_call" | custom-call | flops 1006632960 | bytes 9437184 | tf_op jit(solution)/shard_map/pallas_call | solution.py:175
  202.5 12.2 %all-to-all-start.3 = ((bf16[32,6,16,128]{3,2,1,0:T(8,128)(2,1)}), bf16[32,6,16,128]{3,2,1,0:T(8,128)(2,1)S(1)}, u32[]{:S(2)}, u32[]{:S(2)}) async-start(bf16[32,6,16,128]{3,2,1,0:T(8,128)(2,1)} %bitcast.117), calls=%async_computation.3 | async-start | bytes 1572864 | tf_op jit(solution)/shard_map/all_to_all | solution.py:238
  214.7 3.3 %shard_map.50 = bf16[2,2,8,3,16,128]{5,4,3,2,1,0:T(8,128)(2,1)} custom-call(bf16[4,3,128,640]{3,2,1,0:T(8,128)(2,1)} %get-tuple-element.50.low_mixed.high_mixed, bf16[4,3,128,640]{3,2,1,0:T(8,128)(2,1)} %get-tuple-element.50.low_mixed.high_mixed, bf16[5,6,128,128]{3,2,1,0:T(8,128)(2,1)} %collective-permute-done.9.low, ...), custom_call_target="tpu_custom_call" | custom-call | flops 503316480 | bytes 4718592 | tf_op jit(solution)/shard_map/pallas_call | solution.py:192
  218.0 10.8 %all-to-all-done.3 = bf16[32,6,16,128]{3,2,1,0:T(8,128)(2,1)S(1)} async-done(((bf16[32,6,16,128]{3,2,1,0:T(8,128)(2,1)}), bf16[32,6,16,128]{3,2,1,0:T(8,128)(2,1)S(1)}, u32[]{:S(2)}, u32[]{:S(2)}) %all-to-all-start.3) | async-done | bytes 786464 | tf_op jit(solution)/shard_map/all_to_all | solution.py:238
  228.9 4.1 %all-to-all-start.4 = ((bf16[32,3,16,128]{3,2,1,0:T(8,128)(2,1)}), bf16[32,3,16,128]{3,2,1,0:T(8,128)(2,1)S(1)}, u32[]{:S(2)}, u32[]{:S(2)}) async-start(bf16[32,3,16,128]{3,2,1,0:T(8,128)(2,1)} %bitcast.118), calls=%async_computation.4 | async-start | bytes 786432 | tf_op jit(solution)/shard_map/all_to_all | solution.py:238
  233.4 2.2 fusion.6
  235.6 7.7 %all-to-all-done.4 = bf16[32,3,16,128]{3,2,1,0:T(8,128)(2,1)S(1)} async-done(((bf16[32,3,16,128]{3,2,1,0:T(8,128)(2,1)}), bf16[32,3,16,128]{3,2,1,0:T(8,128)(2,1)S(1)}, u32[]{:S(2)}, u32[]{:S(2)}) %all-to-all-start.4) | async-done | bytes 393248 | tf_op jit(solution)/shard_map/all_to_all | solution.py:238
  243.6 0.9 copy.26
  (58 shorter events, 5.3 us)
Async XLA Ops:
  6.5 18.4 %copy-start = (bf16[64,128,128]{2,1,0:T(8,128)(2,1)S(1)}, bf16[64,128,128]{2,1,0:T(8,128)(2,1)}, u32[]{:S(2)}) copy-start(bf16[64,128,128]{2,1,0:T(8,128)(2,1)} %param.4) | copy-start | bytes 6291460
  6.5 0.8 copy-start.1
  6.5 128.1 %all-gather.3.cloned.1.call-start = ((), (), s32[]{:S(2)}) async-start(), calls=%async_computation.5 | async-start | bytes 13107200 | tf_op jit(solution)/shard_map/all_gather | solution.py:249
  7.3 7.1 %collective-permute-start = (s32[64]{0:T(128)S(1)}, s32[64]{0:T(128)S(1)}, u32[]{:S(2)}, u32[]{:S(2)}) collective-permute-start(s32[64]{0:T(128)S(1)} %copy-done.1), channel_id=1, source_target_pairs={{0,224},{32,0},{64,32},{96,64},{128,96},{160,128},{192,160},{224,1... | collective-permute-start | bytes 776 | tf_op jit(solution)/shard_map/ppermute | solution.py:250
  13.8 3.6 %collective-permute-start.1 = (s32[64]{0:T(128)S(1)}, s32[64]{0:T(128)S(1)}, u32[]{:S(2)}, u32[]{:S(2)}) collective-permute-start(s32[64]{0:T(128)S(1)} %copy-done.1), channel_id=1, source_target_pairs={{0,32},{32,64},{64,96},{96,128},{128,160},{160,192},{192,224},{224... | collective-permute-start | bytes 776 | tf_op jit(solution)/shard_map/ppermute | solution.py:251
  17.4 57.8 %collective-permute-start.2 = (bf16[5,16,128,128]{3,2,1,0:T(8,128)(2,1)}, bf16[5,16,128,128]{3,2,1,0:T(8,128)(2,1)}, u32[]{:S(2)}, u32[]{:S(2)}) collective-permute-start(bf16[5,16,128,128]{3,2,1,0:T(8,128)(2,1)} %refs_22_), channel_id=1, source_target_pairs={{0,32},{32,64},{64,96},{96,128},{128,160},{160,192},{192,224},{224... | collective-permute-start | bytes 7864328 | tf_op jit(solution)/shard_map/ppermute | solution.py:294
  17.4 57.8 %collective-permute-start.3 = (bf16[5,16,128,128]{3,2,1,0:T(8,128)(2,1)}, bf16[5,16,128,128]{3,2,1,0:T(8,128)(2,1)}, u32[]{:S(2)}, u32[]{:S(2)}) collective-permute-start(bf16[5,16,128,128]{3,2,1,0:T(8,128)(2,1)} %refs_22_), channel_id=1, source_target_pairs={{0,224},{32,0},{64,32},{96,64},{128,96},{160,128},{192,160},{224,1... | collective-permute-start | bytes 7864328 | tf_op jit(solution)/shard_map/ppermute | solution.py:294
  20.7 8.4 %all-to-all-start.1 = ((s32[4,1,192]{2,1,0:T(1,128)}), s32[4,1,192]{2,1,0:T(1,128)S(1)}, u32[]{:S(2)}, u32[]{:S(2)}) async-start(s32[4,1,192]{2,1,0:T(1,128)} %reshape.474), calls=%async_computation.1 | async-start | bytes 8192 | tf_op jit(solution)/shard_map/all_to_all | solution.py:278
  29.2 41.1 %all-to-all-start = ((bf16[4,12,128,128]{3,2,1,0:T(8,128)(2,1)}), bf16[4,12,128,128]{3,2,1,0:T(8,128)(2,1)}, u32[]{:S(2)}, u32[]{:S(2)}) async-start(bf16[4,12,128,128]{3,2,1,0:T(8,128)(2,1)} %bitcast.116), calls=%async_computation | async-start | bytes 3145728 | tf_op jit(solution)/shard_map/all_to_all | solution.py:297
  75.1 56.9 %collective-permute-start.4 = (bf16[5,16,128,128]{3,2,1,0:T(8,128)(2,1)}, bf16[5,16,128,128]{3,2,1,0:T(8,128)(2,1)}, u32[]{:S(2)}, u32[]{:S(2)}) collective-permute-start(bf16[5,16,128,128]{3,2,1,0:T(8,128)(2,1)} %collective-permute-done.2.refs_23_.refs_24_.refs_25_), channel_id=1, source_target_pairs={{0,32},{32,64},{64,96},{96,128},{128,160},{160,192},{192,224},{224... | collective-permute-start | bytes 7864328 | tf_op jit(solution)/shard_map/ppermute | solution.py:294
  75.1 56.9 %collective-permute-start.5 = (bf16[5,16,128,128]{3,2,1,0:T(8,128)(2,1)}, bf16[5,16,128,128]{3,2,1,0:T(8,128)(2,1)}, u32[]{:S(2)}, u32[]{:S(2)}) collective-permute-start(bf16[5,16,128,128]{3,2,1,0:T(8,128)(2,1)} %collective-permute-done.3.refs_26_.refs_27_.refs_28_), channel_id=1, source_target_pairs={{0,224},{32,0},{64,32},{96,64},{128,96},{160,128},{192,160},{224,1... | collective-permute-start | bytes 7864328 | tf_op jit(solution)/shard_map/ppermute | solution.py:294
  77.8 7.0 %collective-permute-start.6 = (bf16[4,12,128,128]{3,2,1,0:T(8,128)(2,1)}, bf16[4,12,128,128]{3,2,1,0:T(8,128)(2,1)}, u32[]{:S(2)}, u32[]{:S(2)}) collective-permute-start(bf16[4,12,128,128]{3,2,1,0:T(8,128)(2,1)} %all-to-all-done), channel_id=1, source_target_pairs={{0,1},{1,0},{2,3},{3,2},{4,5},{5,4},{6,7},{7,6},{8,9},{9,8},{10,11... | collective-permute-start | bytes 4718600 | tf_op jit(solution)/shard_map/ppermute | solution.py:300
  132.0 55.9 %collective-permute-start.7 = (bf16[5,16,128,128]{3,2,1,0:T(8,128)(2,1)}, bf16[5,16,128,128]{3,2,1,0:T(8,128)(2,1)}, u32[]{:S(2)}, u32[]{:S(2)}) collective-permute-start(bf16[5,16,128,128]{3,2,1,0:T(8,128)(2,1)} %collective-permute-done.4.refs_29_.refs_30_.refs_31_), channel_id=1, source_target_pairs={{0,32},{32,64},{64,96},{96,128},{128,160},{160,192},{192,224},{224... | collective-permute-start | bytes 7864328 | tf_op jit(solution)/shard_map/ppermute | solution.py:294
  132.0 55.9 %collective-permute-start.8 = (bf16[5,16,128,128]{3,2,1,0:T(8,128)(2,1)}, bf16[5,16,128,128]{3,2,1,0:T(8,128)(2,1)}, u32[]{:S(2)}, u32[]{:S(2)}) collective-permute-start(bf16[5,16,128,128]{3,2,1,0:T(8,128)(2,1)} %collective-permute-done.5.refs_32_.refs_33_.refs_34_), channel_id=1, source_target_pairs={{0,224},{32,0},{64,32},{96,64},{128,96},{160,128},{192,160},{224,1... | collective-permute-start | bytes 7864328 | tf_op jit(solution)/shard_map/ppermute | solution.py:294
  163.3 39.1 %all-to-all-start.2 = ((bf16[32,15,16,128]{3,2,1,0:T(8,128)(2,1)}), bf16[32,15,16,128]{3,2,1,0:T(8,128)(2,1)}, u32[]{:S(2)}, u32[]{:S(2)}) async-start(bf16[32,15,16,128]{3,2,1,0:T(8,128)(2,1)} %bitcast.115), calls=%async_computation.2 | async-start | bytes 3932160 | tf_op jit(solution)/shard_map/all_to_all | solution.py:238
  193.5 21.2 %collective-permute-start.9 = (bf16[5,6,128,128]{3,2,1,0:T(8,128)(2,1)}, bf16[5,6,128,128]{3,2,1,0:T(8,128)(2,1)}, u32[]{:S(2)}, u32[]{:S(2)}) collective-permute-start(bf16[5,6,128,128]{3,2,1,0:T(8,128)(2,1)} %get-tuple-element.53), channel_id=1, source_target_pairs={{0,32},{32,64},{64,96},{96,128},{128,160},{160,192},{192,224},{224... | collective-permute-start | bytes 2949128 | tf_op jit(solution)/shard_map/ppermute | solution.py:294
  193.5 21.2 %collective-permute-start.10 = (bf16[5,6,128,128]{3,2,1,0:T(8,128)(2,1)}, bf16[5,6,128,128]{3,2,1,0:T(8,128)(2,1)}, u32[]{:S(2)}, u32[]{:S(2)}) collective-permute-start(bf16[5,6,128,128]{3,2,1,0:T(8,128)(2,1)} %get-tuple-element.54), channel_id=1, source_target_pairs={{0,224},{32,0},{64,32},{96,64},{128,96},{160,128},{192,160},{224,1... | collective-permute-start | bytes 2949128 | tf_op jit(solution)/shard_map/ppermute | solution.py:294
  202.5 26.4 %all-to-all-start.3 = ((bf16[32,6,16,128]{3,2,1,0:T(8,128)(2,1)}), bf16[32,6,16,128]{3,2,1,0:T(8,128)(2,1)S(1)}, u32[]{:S(2)}, u32[]{:S(2)}) async-start(bf16[32,6,16,128]{3,2,1,0:T(8,128)(2,1)} %bitcast.117), calls=%async_computation.3 | async-start | bytes 1572864 | tf_op jit(solution)/shard_map/all_to_all | solution.py:238
  228.9 14.4 %all-to-all-start.4 = ((bf16[32,3,16,128]{3,2,1,0:T(8,128)(2,1)}), bf16[32,3,16,128]{3,2,1,0:T(8,128)(2,1)S(1)}, u32[]{:S(2)}, u32[]{:S(2)}) async-start(bf16[32,3,16,128]{3,2,1,0:T(8,128)(2,1)} %bitcast.118), calls=%async_computation.4 | async-start | bytes 786432 | tf_op jit(solution)/shard_map/all_to_all | solution.py:238
Sparse Core Ops, SparseCore 0:
  9.2 124.0 all-gather.2

commit v3 on v0

v3 whole, which is shorter than its diff:
```python
import functools

import jax
import jax.numpy as jnp
from jax import lax
from jax.experimental import pallas as pl
from jax.experimental.pallas import tpu as pltpu
from jax.sharding import Mesh, PartitionSpec as P

Z, Y, X, C = 8, 4, 4, 2
M = X * C
CAP = 3
SLOTS = Z * CAP
OFFSETS = (0, -1, 1, -2, 2, -3, 3, 4)
RANK = tuple(OFFSETS.index(((d + 3) % Z) - 3) for d in range(Z))
RIGHT = [(i, (i + 1) % Z) for i in range(Z)]
LEFT = [(i, (i - 1) % Z) for i in range(Z)]
UP = [(i, (i + 1) % Y) for i in range(Y)]
DOWN = [(i, (i - 1) % Y) for i in range(Y)]


def left_products(blocks, psi):
    terms, width = blocks.shape[0], blocks.shape[-1]
    mixed = jnp.dot(
        blocks.reshape(terms * width, width), psi, preferred_element_type=jnp.float32
    ).astype(jnp.bfloat16)
    return jnp.concatenate([mixed[w * width : (w + 1) * width] for w in range(terms)], axis=1)


def times_right(mixed, chosen):
    total = lax.dot_general(
        mixed,
        jnp.concatenate([chosen[w, 0] for w in range(chosen.shape[0])], axis=1),
        (((1,), (1,)), ((), ())),
        preferred_element_type=jnp.float32,
    )
    width = total.shape[0]
    return total.astype(jnp.bfloat16).reshape(M, width // M, width)


def left_products_turned(blocks, psi):
    terms, width = blocks.shape[0], blocks.shape[-1]
    mixed = jnp.dot(
        blocks.reshape(terms * width, width), psi, preferred_element_type=jnp.float32
    )
    turned = [mixed[w * width : (w + 1) * width].T for w in range(terms)]
    return jnp.concatenate(turned, axis=0).astype(jnp.bfloat16)


def right_times(chosen, turned):
    wide = jnp.concatenate([chosen[w, 0] for w in range(chosen.shape[0])], axis=1)
    total = jnp.dot(wide, turned, preferred_element_type=jnp.float32).T
    width = total.shape[0]
    return total.astype(jnp.bfloat16).reshape(M, width // M, width)


def middle_kernel(near, info_ref, low_psi, high_psi, *refs):
    own, above, low_far, high_far, below = refs[:5]
    rights = refs[5 : 5 + near]
    near_ref, far_ref, end_ref, left, right, left_sems, right_sems = refs[5 + near :]
    home = pl.program_id(0)
    owned = own.shape[1]
    far = far_ref.shape[1] // CAP

    def left_copy(source, sector, i):
        return pltpu.make_async_copy(source.at[:, pl.ds(sector, 1)], left.at[i], left_sems.at[i])

    def right_copy(source, sector, i):
        return pltpu.make_async_copy(source.at[:, pl.ds(sector, 1)], right.at[i], right_sems.at[i])

    def start_home(h, carry):
        apart = (h + Y - info_ref[Y * SLOTS]) % Y

        def start_lefts(pick):
            for q in range(SLOTS):
                pick(info_ref[h * SLOTS + q] // 16, h * SLOTS + q)

        def both_halves(sector, i):
            @pl.when(sector < owned // 2)
            def _():
                left_copy(low_far, sector, i).start()

            @pl.when(sector >= owned // 2)
            def _():
                left_copy(high_far, sector - owned // 2, i).start()

        for n, source in ((0, own), (1, above), (3, below)):

            @pl.when(apart == n)
            def _(source=source):
                start_lefts(lambda sector, i: left_copy(source, sector, i).start())

        @pl.when(apart == 2)
        def _():
            start_lefts(both_halves)

        for q in range(near * CAP):
            sector = info_ref[h * SLOTS + q] % 16
            right_copy(rights[q // CAP], sector, h * near * CAP + q).start()
        return carry

    @pl.when(home == 0)
    def _():
        lax.fori_loop(0, Y, start_home, 0)

    for q in range(SLOTS):
        left_copy(own, 0, home * SLOTS + q).wait()
    for q in range(near * CAP):
        right_copy(rights[0], 0, home * near * CAP + q).wait()
    half = SLOTS // C
    for q in range(SLOTS):
        psi = low_psi[0, q] if q < half else high_psi[0, q - half]
        blocks = left[home * SLOTS + q, :, 0]
        if q < near * CAP:
            chosen = right[home * near * CAP + q]
            near_ref[0, :, q] = times_right(left_products(blocks, psi), chosen)
        elif q < (near + far) * CAP:
            far_ref[0, q - near * CAP] = left_products_turned(blocks, psi)
        else:
            end_ref[0, q - (near + far) * CAP] = left_products_turned(blocks, psi)


def far_kernel(count, info_ref, mixed_ref, *refs):
    rights, (out_ref, held, sems) = refs[:count], refs[count:]
    copies = []
    for h in range(Y):
        for s in range(count * CAP):
            place = s // CAP
            sector = info_ref[h * SLOTS + (Z - 1 - count) * CAP + s] % 16
            copies.append(
                pltpu.make_async_copy(
                    rights[place].at[:, pl.ds(sector, 1)],
                    held.at[h * count * CAP + s],
                    sems.at[h * count * CAP + s],
                )
            )
    for copy in copies:
        copy.start()
    for h in range(Y):
        slots = range(h * count * CAP, (h + 1) * count * CAP)
        for i in slots:
            copies[i].wait()
        for s, i in enumerate(slots):
            out_ref[h, :, s] = right_times(held[i], mixed_ref[h, s])


def end_kernel(mixed_ref, low, high, out_ref):
    for h in range(Y):
        side, first = (low, h * CAP) if h < Y // 2 else (high, (h - Y // 2) * CAP)
        for s in range(CAP):
            chosen = side[:, first + s : first + s + 1]
            out_ref[h, :, s] = right_times(chosen, mixed_ref[h, s])


def fetch_kernel(low_index, high_index, low_ref, high_ref, low_out, high_out, sems):
    count = low_out.shape[1]
    copies = []
    for i in range(count):
        for n, (index, source, out) in enumerate(
            ((low_index, low_ref, low_out), (high_index, high_ref, high_out))
        ):
            copies.append(
                pltpu.make_async_copy(
                    source.at[:, pl.ds(index[i], 1)], out.at[:, pl.ds(i, 1)], sems.at[2 * i + n]
                )
            )
    for copy in copies:
        copy.start()
    for copy in copies:
        copy.wait()


PARAMS = pltpu.CompilerParams(vmem_limit_bytes=60 * 1024 * 1024)


def cost(slots, matmuls, terms, width):
    return pl.CostEstimate(
        flops=2 * slots * matmuls * terms * width**3,
        bytes_accessed=slots * (matmuls * terms + 2) * width * width * 2,
        transcendentals=0,
    )


def middle_products(info, psi, lefts, rights):
    terms, _, width, _ = lefts[0].shape
    near, far = len(rights), Z - 1 - len(rights)
    one = (terms, 1, width, width)
    turned = [
        jax.ShapeDtypeStruct((Y, n * CAP, terms * width, width), jnp.bfloat16) for n in (far, 1)
    ]
    out = jax.ShapeDtypeStruct((Y, M, near * CAP, width // M, width), jnp.bfloat16)
    per_home = lambda shape: pl.BlockSpec(
        (1,) + shape[1:], lambda h, info: (h,) + (0,) * (len(shape) - 1)
    )
    return pl.pallas_call(
        functools.partial(middle_kernel, near),
        out_shape=[out] + turned,
        grid_spec=pltpu.PrefetchScalarGridSpec(
            num_scalar_prefetch=1,
            grid=(Y,),
            in_specs=[per_home(p.shape) for p in psi]
            + [pl.BlockSpec(memory_space=pl.ANY)] * (len(lefts) + near),
            out_specs=[per_home(o.shape) for o in [out] + turned],
            scratch_shapes=[
                pltpu.VMEM((Y * SLOTS,) + one, jnp.bfloat16),
                pltpu.VMEM((Y * near * CAP,) + one, jnp.bfloat16),
                pltpu.SemaphoreType.DMA((Y * SLOTS,)),
                pltpu.SemaphoreType.DMA((Y * near * CAP,)),
            ],
        ),
        compiler_params=PARAMS,
        cost_estimate=cost(Y * SLOTS, 2, terms, width),
    )(info, *psi, *lefts, *rights)


SMALL = pltpu.CompilerParams(vmem_limit_bytes=24 * 1024 * 1024)
IN_VMEM = pl.BlockSpec(memory_space=pltpu.VMEM)
ANYWHERE = pl.BlockSpec(memory_space=pl.ANY)


def far_products(info, mixed, arrived):
    slots, width = mixed.shape[1], mixed.shape[3]
    terms = mixed.shape[2] // width
    return pl.pallas_call(
        functools.partial(far_kernel, len(arrived)),
        out_shape=jax.ShapeDtypeStruct((Y, M, slots, width // M, width), jnp.bfloat16),
        in_specs=[pl.BlockSpec(memory_space=pltpu.SMEM), IN_VMEM] + [ANYWHERE] * len(arrived),
        out_specs=IN_VMEM,
        scratch_shapes=[
            pltpu.VMEM((Y * slots, terms, 1, width, width), jnp.bfloat16),
            pltpu.SemaphoreType.DMA((Y * slots,)),
        ],
        compiler_params=SMALL,
        cost_estimate=cost(Y * slots, 2, terms, width),
    )(info, mixed, *arrived)


def end_products(mixed, sent):
    slots, width = mixed.shape[1], mixed.shape[3]
    return pl.pallas_call(
        end_kernel,
        out_shape=jax.ShapeDtypeStruct((Y, M, slots, width // M, width), jnp.bfloat16),
        in_specs=[IN_VMEM] * 3,
        out_specs=IN_VMEM,
        compiler_params=SMALL,
        cost_estimate=cost(Y * slots, 2, mixed.shape[2] // width, width),
    )(mixed, *sent)


def fetch(low, high, low_index, high_index):
    count = low_index.shape[0]
    out = jax.ShapeDtypeStruct((low.shape[0], count) + low.shape[2:], low.dtype)
    return pl.pallas_call(
        fetch_kernel,
        out_shape=[out, out],
        in_specs=[pl.BlockSpec(memory_space=pltpu.SMEM)] * 2 + [ANYWHERE] * 2,
        out_specs=[IN_VMEM] * 2,
        scratch_shapes=[pltpu.SemaphoreType.DMA((2 * count,))],
        compiler_params=SMALL,
        cost_estimate=pl.CostEstimate(
            flops=0, bytes_accessed=4 * out.size * 2, transcendentals=0
        ),
    )(low_index, high_index, low, high)


def exchange(part):
    part = part.reshape((Y * M,) + part.shape[2:])
    part = lax.all_to_all(part, ("y", "x", "c"), split_axis=0, concat_axis=0, tiled=True)
    return part.reshape((Y, M) + part.shape[1:])


def on_device(wavefunction, left_environment, right_environment, right_sector):
    z, y, core = (lax.axis_index(name) for name in ("z", "y", "c"))
    blocks, width = wavefunction.shape[:2]
    owned = left_environment.shape[1]
    members = blocks // owned
    tie = lax.optimization_barrier

    def step(moving, axis="z"):
        to_next, to_last = (RIGHT, LEFT) if axis == "z" else (UP, DOWN)
        return [lax.ppermute(moving[0], axis, to_next), lax.ppermute(moving[1], axis, to_last)]

    first = step([right_environment] * 2)

    index = jnp.arange(blocks, dtype=jnp.int32)
    earlier = index[None, :] < index[:, None]

    def slots_of(sectors, plane):
        owner = sectors // owned
        same = owner[:, :, None] == owner[:, None, :]
        place = jnp.sum((same & earlier).astype(jnp.int32), axis=2)
        offset = (owner // Y - plane) % Z
        rank = sum(jnp.where(offset == d, RANK[d], 0) for d in range(Z))
        return owner % Y, rank * CAP + place

    def into(slots, values, count):
        hit = slots[:, None, :] == jnp.arange(count, dtype=jnp.int32)[None, :, None]
        return jnp.sum(jnp.where(hit, values[:, None, :], 0), axis=2)

    column, slot = slots_of(right_sector[None], z)
    slot = column * SLOTS + slot
    split = SLOTS // C
    mine = (slot // SLOTS) * split + jnp.where((slot % SLOTS) // split == core, slot % split, -Y * SLOTS)
    source = into(mine, index[None], Y * split)[0]
    outgoing = wavefunction.at[source].get(mode="promise_in_bounds")
    outgoing = outgoing.reshape((Y, split) + wavefunction.shape[1:])

    sectors = jnp.broadcast_to(right_sector, (Y, blocks))
    sectors = lax.all_to_all(sectors, "y", split_axis=0, concat_axis=0, tiled=True)
    left_environment, sectors = tie((left_environment, sectors))
    near_left = step([left_environment] * 2, "y")
    column, here = slots_of(sectors, z)
    here = jnp.where(column == y, here, -1)
    info = into(here, (index // members) * 16 + sectors % owned, SLOTS)
    info = jnp.concatenate([info.reshape(-1), y[None].astype(jnp.int32)])

    last = info[: Y * SLOTS].reshape(Y, SLOTS)[:, SLOTS - CAP :] % owned
    wanted = [
        lax.ppermute(last[: Y // 2].reshape(-1), "z", LEFT),
        lax.ppermute(last[Y // 2 :].reshape(-1), "z", RIGHT),
    ]
    first, outgoing, wanted = tie((first, outgoing, wanted))
    psi = lax.all_to_all(outgoing, "y", split_axis=0, concat_axis=0, tiled=True)
    second = step(first)
    far_left = step([near_left[0][:, : owned // 2], near_left[1][:, owned // 2 :]], "y")
    other = lax.ppermute(psi, "c", [(0, 1), (1, 0)])
    psi = (jnp.where(core == 0, psi, other), jnp.where(core == 0, other, psi))
    second, psi, far_left = tie((second, psi, far_left))
    third = step(second)
    lefts = (left_environment, near_left[1], far_left[0], far_left[1], near_left[0])
    arrived = [right_environment] + first + second
    near, far_mixed, end_mixed = middle_products(info, psi, lefts, arrived)
    wanted, near, far_mixed, end_mixed = tie((wanted, near, far_mixed, end_mixed))
    fourth = step(fetch(*third, *wanted))
    near = exchange(near)
    far = far_products(info, far_mixed, third)
    end_mixed, far, near = tie((end_mixed, far, near))
    far = exchange(far)
    end = exchange(end_products(end_mixed, fourth))

    def gather(part, start):
        where = jnp.arange(Y)[:, None, None] * SLOTS + start + jnp.arange(part.shape[2])
        where = jnp.broadcast_to(where, part.shape[:3])
        pick = (slot[0][:, None, None, None] == where).astype(jnp.bfloat16)
        return jnp.einsum("kyms,ymsil->kil", pick, part, preferred_element_type=jnp.float32)

    total = gather(near, 0) + gather(far, 5 * CAP) + gather(end, 7 * CAP)
    return total.astype(jnp.bfloat16)


def solution(mesh):
    fine = Mesh(mesh.devices.reshape(Z, Y, X, C), ("z", "y", "x", "c"))
    bond = ("z", "y")
    placed = (
        P(bond, None, None),
        P(("x", "c"), bond, None, None),
        P(("x", "c"), bond, None, None),
        P(bond),
    )
    return jax.shard_map(
        on_device, mesh=fine, in_specs=placed, out_specs=P(bond, ("x", "c"), None), check_vma=False
    )
```

time: 685 us -> 242 us (0.35)
  waiting for transfers between devices: 524 us -> 129 us
  local copies, waits for them, and re-layouts: 65.1 us -> 11 us
  Pallas kernels: 0 us -> 33.8 us
  matrix products: 24.9 us -> 4.05 us
  between operations: 13.5 us -> 0.21 us
    all_to_all x3 -> x5, waiting for transfers between devices: 479 us -> 30.9 us  [the longest x1 18.4 us: on_device(): psi = lax.all_to_all(outgoing, 'y', split_axis=0, concat_axis=0, tiled=True)]
    ppermute x0 -> x15, waiting for transfers between devices: none -> 98.5 us  [the longest x6 50.3 us: step(): lax.ppermute(moving[0], axis, to_next)]
    reduce_scatter x1 -> x0, waiting for transfers between devices: 45.4 us -> none  [on_device(): lax.psum_scatter(gathered, 'mpo', scatter_dimension=1, tiled=True)]
    pallas_call x0 -> x4, Pallas kernels: none -> 33.8 us  [the longest x1 22.5 us: middle_products(): pl.pallas_call(functools.partial(middle_kernel, near), out_shape=[out] +...]
    scatter x2 -> x0, local copies, waits for them, and re-layouts: 25.5 us -> none  [the longest x1 24.7 us: on_device(): jnp.zeros((peers * capacity, terms, width, width), jnp.bfloat16)]
    ppermute x0 -> x15, starting transfers between devices: none -> 23.2 us  [the longest x6 15.5 us: step(): lax.ppermute(moving[1], axis, to_last)]
    dot_general x2 -> x3, matrix products: 24.9 us -> 4.05 us  [gather(): jnp.einsum('kyms,ymsil->kil', pick, part, preferred_element_type=jnp.floa...]
    all_to_all x3 -> x5, starting transfers between devices: 51.3 us -> 33.4 us  [the longest x3 24.9 us: exchange(): lax.all_to_all(part, ('y', 'x', 'c'), split_axis=0, concat_axis=0, tiled=...]
  transfers between devices with their start and end apart: 4 -> 20, of which waited for: 3 -> 10; matrix products, arithmetic and copies ran while one was open for 10% -> 8% of each run, Pallas kernels for 0% -> 14%
where the time goes in v3:
time: 242 us
  waiting for transfers between devices  129 us (53%)
  starting transfers between devices  56.7 us (23%)
  Pallas kernels  33.8 us (14%)
  local copies, waits for them, and re-layouts  11 us (5%)
  other arithmetic  6.63 us (3%)
  matrix products  4.05 us (2%)
    ppermute x6, waiting for transfers between devices, step(): lax.ppermute(moving[0], axis, to_next)  50.3 us
    ppermute x1, waiting for transfers between devices, on_device(): lax.ppermute(last[:Y // 2].reshape(-1), 'z', LEFT)  41.6 us
    all_to_all x3, starting transfers between devices, exchange(): lax.all_to_all(part, ('y', 'x', 'c'), split_axis=0, concat_axis=0, tiled=...  24.9 us
    pallas_call x1, Pallas kernels, middle_products(): pl.pallas_call(functools.partial(middle_kernel, near), out_shape=[out] +...  22.5 us
    all_to_all x1, waiting for transfers between devices, on_device(): psi = lax.all_to_all(outgoing, 'y', split_axis=0, concat_axis=0, tiled=True)  18.4 us
    ppermute x6, starting transfers between devices, step(): lax.ppermute(moving[1], axis, to_last)  15.5 us
    all_to_all x3, waiting for transfers between devices, exchange(): lax.all_to_all(part, ('y', 'x', 'c'), split_axis=0, concat_axis=0, tiled=...  12 us
    pallas_call x1, Pallas kernels, far_products(): pl.pallas_call(functools.partial(far_kernel, len(arrived)), out_shape=jax...  4.95 us
  transfers between devices with their start and end apart: 20, of which 10 were waited for; matrix products, arithmetic and copies ran while one was open for 8% of the time, Pallas kernels for 14%

profile of v3, /device:TPU:1, one launch (start us, length us, event | category | flops | bytes accessed | tf_op | source)
XLA Modules:
  0.0 241.7 jit_solution(1647052629685748137)
XLA Ops:
  0.0 2.5 %collective-permute-start = (bf16[5,16,128,128]{3,2,1,0:T(8,128)(2,1)}, bf16[5,16,128,128]{3,2,1,0:T(8,128)(2,1)}, u32[]{:S(2)}, u32[]{:S(2)}) collective-permute-start(bf16[5,16,128,128]{3,2,1,0:T(8,128)(2,1)} %refs_5_.1), channel_id=1, source_target_pairs={{0,32},{32,64},{64,96},{96,128},{128,160},{160,192},{192,224},{224... | collective-permute-start | bytes 7864328 | tf_op jit(solution)/shard_map/ppermute | solution.py:281
  2.5 4.0 %collective-permute-start.1 = (bf16[5,16,128,128]{3,2,1,0:T(8,128)(2,1)}, bf16[5,16,128,128]{3,2,1,0:T(8,128)(2,1)}, u32[]{:S(2)}, u32[]{:S(2)}) collective-permute-start(bf16[5,16,128,128]{3,2,1,0:T(8,128)(2,1)} %refs_5_.1), channel_id=1, source_target_pairs={{0,224},{32,0},{64,32},{96,64},{128,96},{160,128},{192,160},{224,1... | collective-permute-start | bytes 7864328 | tf_op jit(solution)/shard_map/ppermute | solution.py:281
  7.7 4.2 %all-to-all-start = ((s32[4,1,64]{2,1,0:T(1,128)}), s32[4,1,64]{2,1,0:T(1,128)S(1)}, u32[]{:S(2)}, u32[]{:S(2)}) async-start(s32[4,1,64]{2,1,0:T(1,128)} %broadcast_in_dim.102), calls=%async_computation | async-start | bytes 4096 | tf_op jit(solution)/shard_map/all_to_all | solution.py:309
  13.6 1.9 gather_fusion
  17.1 1.7 collective-permute-start.9
  20.8 41.6 %collective-permute-done.2.low_index = s32[6]{0:T(128)S(1)} collective-permute-done((s32[6]{0:T(128)S(1)}, s32[6]{0:T(128)S(1)}, u32[]{:S(2)}, u32[]{:S(2)}) %collective-permute-start.2) | collective-permute-done | bytes 56 | tf_op jit(solution)/shard_map/ppermute | solution.py:319
  62.3 4.7 %collective-permute-done.3.high_index = s32[6]{0:T(128)S(1)} collective-permute-done((s32[6]{0:T(128)S(1)}, s32[6]{0:T(128)S(1)}, u32[]{:S(2)}, u32[]{:S(2)}) %collective-permute-start.3) | collective-permute-done | bytes 56 | tf_op jit(solution)/shard_map/ppermute | solution.py:320
  67.1 4.3 %all-to-all-start.1 = ((bf16[4,12,128,128]{3,2,1,0:T(8,128)(2,1)}), bf16[4,12,128,128]{3,2,1,0:T(8,128)(2,1)}, u32[]{:S(2)}, u32[]{:S(2)}) async-start(bf16[4,12,128,128]{3,2,1,0:T(8,128)(2,1)} %bitcast.50), calls=%async_computation.1 | async-start | bytes 3145728 | tf_op jit(solution)/shard_map/all_to_all | solution.py:323
  71.5 2.7 %collective-permute-start.5 = (bf16[5,16,128,128]{3,2,1,0:T(8,128)(2,1)}, bf16[5,16,128,128]{3,2,1,0:T(8,128)(2,1)}, u32[]{:S(2)}, u32[]{:S(2)}) collective-permute-start(bf16[5,16,128,128]{3,2,1,0:T(8,128)(2,1)} %collective-permute-done.1.refs_7_), channel_id=1, source_target_pairs={{0,224},{32,0},{64,32},{96,64},{128,96},{160,128},{192,160},{224,1... | collective-permute-start | bytes 7864328 | tf_op jit(solution)/shard_map/ppermute | solution.py:281
  74.2 18.4 %all-to-all-done.1 = bf16[4,12,128,128]{3,2,1,0:T(8,128)(2,1)} async-done(((bf16[4,12,128,128]{3,2,1,0:T(8,128)(2,1)}), bf16[4,12,128,128]{3,2,1,0:T(8,128)(2,1)}, u32[]{:S(2)}, u32[]{:S(2)}) %all-to-all-start.1) | async-done | bytes 1572896 | tf_op jit(solution)/shard_map/all_to_all | solution.py:323
  92.6 1.8 collective-permute-start.6
  94.4 2.6 %slice.22 = bf16[5,8,128,128]{3,2,1,0:T(8,128)(2,1)} slice(bf16[5,16,128,128]{3,2,1,0:T(8,128)(2,1)} %collective-permute-done.7.refs_4_), slice={[0:5], [0:8], [0:128], [0:128]} | slice | bytes 2621440 | tf_op jit(solution)/shard_map/slice | solution.py:325
  97.9 2.5 %slice.23 = bf16[5,8,128,128]{3,2,1,0:T(8,128)(2,1)} slice(bf16[5,16,128,128]{3,2,1,0:T(8,128)(2,1)} %collective-permute-done.9.refs_1_), slice={[0:5], [8:16], [0:128], [0:128]} | slice | bytes 2621440 | tf_op jit(solution)/shard_map/slice | solution.py:325
  100.4 1.8 collective-permute-start.10
  102.2 3.8 %broadcast_select_fusion = (bf16[4,12,128,128]{3,2,1,0:T(8,128)(2,1)}, bf16[4,12,128,128]{3,2,1,0:T(8,128)(2,1)}) fusion(bf16[4,12,128,128]{3,2,1,0:T(8,128)(2,1)} %collective-permute-done.6, bf16[4,12,128,128]{3,2,1,0:T(8,128)(2,1)} %all-to-all-done.1, pred[]{:T(512)S(6)} %eq.223), kind=kLoop, calls=%fused_computation.3 | loop fusion | flops 1572864 | bytes 6291457 | tf_op jit(solution)/shard_map/jit(_where)/select_n | solution.py:327
  106.0 23.0 %collective-permute-done.8.refs_2_ = bf16[5,8,128,128]{3,2,1,0:T(8,128)(2,1)S(1)} collective-permute-done((bf16[5,8,128,128]{3,2,1,0:T(8,128)(2,1)}, bf16[5,8,128,128]{3,2,1,0:T(8,128)(2,1)S(1)}, u32[]{:S(2)}, u32[]{:S(2)}) %collective-permute-start.8) | collective-permute-done | bytes 1310752 | tf_op jit(solution)/shard_map/ppermute | solution.py:281
  128.9 1.9 collective-permute-done.10.refs_3_
  130.8 2.7 %collective-permute-start.12 = (bf16[5,16,128,128]{3,2,1,0:T(8,128)(2,1)}, bf16[5,16,128,128]{3,2,1,0:T(8,128)(2,1)}, u32[]{:S(2)}, u32[]{:S(2)}) collective-permute-start(bf16[5,16,128,128]{3,2,1,0:T(8,128)(2,1)} %collective-permute-done.5.refs_9_), channel_id=1, source_target_pairs={{0,224},{32,0},{64,32},{96,64},{128,96},{160,128},{192,160},{224,1... | collective-permute-start | bytes 7864328 | tf_op jit(solution)/shard_map/ppermute | solution.py:281
  134.2 22.5 %shard_map.46 = (bf16[4,8,15,16,128]{4,3,2,1,0:T(8,128)(2,1)}, bf16[4,6,640,128]{3,2,1,0:T(8,128)(2,1)}, bf16[4,3,640,128]{3,2,1,0:T(8,128)(2,1)}) custom-call(s32[97]{0:T(128)} %pad_add_fusion.info_ref, bf16[4,12,128,128]{3,2,1,0:T(8,128)(2,1)} %get-tuple-element.38.low_psi, bf16[4,12,128,128]{3,2,1,0:T(8,128)(2,1)} %get-tuple-element.39.high_psi, ...), custom_call_target="tpu_custom_call" | custom-call | flops 4026531840 | bytes 37748736 | tf_op jit(solution)/shard_map/pallas_call | solution.py:195
  156.7 9.4 %all-to-all-start.2 = ((bf16[32,15,16,128]{3,2,1,0:T(8,128)(2,1)}), bf16[32,15,16,128]{3,2,1,0:T(8,128)(2,1)}, u32[]{:S(2)}, u32[]{:S(2)}) async-start(bf16[32,15,16,128]{3,2,1,0:T(8,128)(2,1)} %bitcast.51), calls=%async_computation.2 | async-start | bytes 3932160 | tf_op jit(solution)/shard_map/all_to_all | solution.py:268
  166.2 23.0 %collective-permute-done.11.refs_0_.low_ref = bf16[5,16,128,128]{3,2,1,0:T(8,128)(2,1)} collective-permute-done((bf16[5,16,128,128]{3,2,1,0:T(8,128)(2,1)}, bf16[5,16,128,128]{3,2,1,0:T(8,128)(2,1)}, u32[]{:S(2)}, u32[]{:S(2)}) %collective-permute-start.11) | collective-permute-done | bytes 2621472 | tf_op jit(solution)/shard_map/ppermute | solution.py:281
  189.2 3.6 %shard_map.48 = (bf16[5,6,128,128]{3,2,1,0:T(8,128)(2,1)}, bf16[5,6,128,128]{3,2,1,0:T(8,128)(2,1)}) custom-call(s32[6]{0:T(128)S(1)} %collective-permute-done.2.low_index, s32[6]{0:T(128)S(1)} %collective-permute-done.3.high_index, bf16[5,16,128,128]{3,2,1,0:T(8,128)(2,1)} %collective-permute-done.11.refs_0_.low_ref, ...), custom_call_target="tpu_custom_call" | custom-call | bytes 3932160 | tf_op jit(solution)/shard_map/pallas_call | solution.py:253
  192.9 2.7 %collective-permute-start.14 = (bf16[5,6,128,128]{3,2,1,0:T(8,128)(2,1)}, bf16[5,6,128,128]{3,2,1,0:T(8,128)(2,1)}, u32[]{:S(2)}, u32[]{:S(2)}) collective-permute-start(bf16[5,6,128,128]{3,2,1,0:T(8,128)(2,1)} %get-tuple-element.56), channel_id=1, source_target_pairs={{0,224},{32,0},{64,32},{96,64},{128,96},{160,128},{192,160},{224,1... | collective-permute-start | bytes 2949128 | tf_op jit(solution)/shard_map/ppermute | solution.py:281
  195.5 5.0 %shard_map.47 = bf16[4,8,6,16,128]{4,3,2,1,0:T(8,128)(2,1)} custom-call(s32[97]{0:T(128)S(1)} %copy-done.3, bf16[4,6,640,128]{3,2,1,0:T(8,128)(2,1)S(1)} %copy-done.1, bf16[5,16,128,128]{3,2,1,0:T(8,128)(2,1)} %collective-permute-done.11.refs_0_.low_ref, bf16[5,16,128,128]{3,2,1,0:T(8,128)(2,1)} %collective-permute-done.12.refs_1_.high_ref), custom_call_target="tpu_custom_call" | custom-call | flops 1006632960 | bytes 9437184 | tf_op jit(solution)/shard_map/pallas_call | solution.py:224
  200.5 10.2 %all-to-all-start.3 = ((bf16[32,6,16,128]{3,2,1,0:T(8,128)(2,1)}), bf16[32,6,16,128]{3,2,1,0:T(8,128)(2,1)}, u32[]{:S(2)}, u32[]{:S(2)}) async-start(bf16[32,6,16,128]{3,2,1,0:T(8,128)(2,1)} %bitcast.13), calls=%async_computation.3 | async-start | bytes 1572864 | tf_op jit(solution)/shard_map/all_to_all | solution.py:268
  210.9 4.3 %collective-permute-done.13.low = bf16[5,6,128,128]{3,2,1,0:T(8,128)(2,1)S(1)} collective-permute-done((bf16[5,6,128,128]{3,2,1,0:T(8,128)(2,1)}, bf16[5,6,128,128]{3,2,1,0:T(8,128)(2,1)S(1)}, u32[]{:S(2)}, u32[]{:S(2)}) %collective-permute-start.13) | collective-permute-done | bytes 983072 | tf_op jit(solution)/shard_map/ppermute | solution.py:281
  216.8 2.8 %shard_map.49 = bf16[4,8,3,16,128]{4,3,2,1,0:T(8,128)(2,1)} custom-call(bf16[4,3,640,128]{3,2,1,0:T(8,128)(2,1)S(1)} %copy-done.2, bf16[5,6,128,128]{3,2,1,0:T(8,128)(2,1)S(1)} %collective-permute-done.13.low, bf16[5,6,128,128]{3,2,1,0:T(8,128)(2,1)} %collective-permute-done.14.high), custom_call_target="tpu_custom_call" | custom-call | flops 503316480 | bytes 4718592 | tf_op jit(solution)/shard_map/pallas_call | solution.py:240
  219.5 5.5 %all-to-all-done.3 = bf16[32,6,16,128]{3,2,1,0:T(8,128)(2,1)} async-done(((bf16[32,6,16,128]{3,2,1,0:T(8,128)(2,1)}), bf16[32,6,16,128]{3,2,1,0:T(8,128)(2,1)}, u32[]{:S(2)}, u32[]{:S(2)}) %all-to-all-start.3) | async-done | bytes 786464 | tf_op jit(solution)/shard_map/all_to_all | solution.py:268
  225.0 5.2 %all-to-all-start.4 = ((bf16[32,3,16,128]{3,2,1,0:T(8,128)(2,1)}), bf16[32,3,16,128]{3,2,1,0:T(8,128)(2,1)S(1)}, u32[]{:S(2)}, u32[]{:S(2)}) async-start(bf16[32,3,16,128]{3,2,1,0:T(8,128)(2,1)} %bitcast.19), calls=%async_computation.4 | async-start | bytes 786432 | tf_op jit(solution)/shard_map/all_to_all | solution.py:268
  230.3 1.6 convolution_bitcast_fusion.1
  231.8 2.1 fusion.6
  234.0 6.5 %all-to-all-done.4 = bf16[32,3,16,128]{3,2,1,0:T(8,128)(2,1)S(1)} async-done(((bf16[32,3,16,128]{3,2,1,0:T(8,128)(2,1)}), bf16[32,3,16,128]{3,2,1,0:T(8,128)(2,1)S(1)}, u32[]{:S(2)}, u32[]{:S(2)}) %all-to-all-start.4) | async-done | bytes 393248 | tf_op jit(solution)/shard_map/all_to_all | solution.py:268
  (55 shorter events, 11.1 us)
Async XLA Ops:
  0.0 13.6 %copy-start = (bf16[64,128,128]{2,1,0:T(8,128)(2,1)S(1)}, bf16[64,128,128]{2,1,0:T(8,128)(2,1)}, u32[]{:S(2)}) copy-start(bf16[64,128,128]{2,1,0:T(8,128)(2,1)} %param.4) | copy-start | bytes 6291460
  0.0 67.1 %collective-permute-start = (bf16[5,16,128,128]{3,2,1,0:T(8,128)(2,1)}, bf16[5,16,128,128]{3,2,1,0:T(8,128)(2,1)}, u32[]{:S(2)}, u32[]{:S(2)}) collective-permute-start(bf16[5,16,128,128]{3,2,1,0:T(8,128)(2,1)} %refs_5_.1), channel_id=1, source_target_pairs={{0,32},{32,64},{64,96},{96,128},{128,160},{160,192},{192,224},{224... | collective-permute-start | bytes 7864328 | tf_op jit(solution)/shard_map/ppermute | solution.py:281
  2.5 64.6 %collective-permute-start.1 = (bf16[5,16,128,128]{3,2,1,0:T(8,128)(2,1)}, bf16[5,16,128,128]{3,2,1,0:T(8,128)(2,1)}, u32[]{:S(2)}, u32[]{:S(2)}) collective-permute-start(bf16[5,16,128,128]{3,2,1,0:T(8,128)(2,1)} %refs_5_.1), channel_id=1, source_target_pairs={{0,224},{32,0},{64,32},{96,64},{128,96},{160,128},{192,160},{224,1... | collective-permute-start | bytes 7864328 | tf_op jit(solution)/shard_map/ppermute | solution.py:281
  7.7 8.3 %all-to-all-start = ((s32[4,1,64]{2,1,0:T(1,128)}), s32[4,1,64]{2,1,0:T(1,128)S(1)}, u32[]{:S(2)}, u32[]{:S(2)}) async-start(s32[4,1,64]{2,1,0:T(1,128)} %broadcast_in_dim.102), calls=%async_computation | async-start | bytes 4096 | tf_op jit(solution)/shard_map/all_to_all | solution.py:309
  16.0 78.4 %collective-permute-start.7 = (bf16[5,16,128,128]{3,2,1,0:T(8,128)(2,1)}, bf16[5,16,128,128]{3,2,1,0:T(8,128)(2,1)}, u32[]{:S(2)}, u32[]{:S(2)}) collective-permute-start(bf16[5,16,128,128]{3,2,1,0:T(8,128)(2,1)} %refs_0_), channel_id=1, source_target_pairs={{0,8},{8,16},{16,24},{24,0},{1,9},{9,17},{17,25},{25,1},{2,10},{10... | collective-permute-start | bytes 7864328 | tf_op jit(solution)/shard_map/ppermute | solution.py:281
  17.1 80.8 %collective-permute-start.9 = (bf16[5,16,128,128]{3,2,1,0:T(8,128)(2,1)}, bf16[5,16,128,128]{3,2,1,0:T(8,128)(2,1)}, u32[]{:S(2)}, u32[]{:S(2)}) collective-permute-start(bf16[5,16,128,128]{3,2,1,0:T(8,128)(2,1)} %refs_0_), channel_id=1, source_target_pairs={{0,24},{8,0},{16,8},{24,16},{1,25},{9,1},{17,9},{25,17},{2,26},{10... | collective-permute-start | bytes 7864328 | tf_op jit(solution)/shard_map/ppermute | solution.py:281
  19.3 43.0 %collective-permute-start.2 = (s32[6]{0:T(128)S(1)}, s32[6]{0:T(128)S(1)}, u32[]{:S(2)}, u32[]{:S(2)}) collective-permute-start(s32[6]{0:T(128)S(1)} %reshape.365), channel_id=1, source_target_pairs={{0,224},{32,0},{64,32},{96,64},{128,96},{160,128},{192,160},{224,1... | collective-permute-start | bytes 80 | tf_op jit(solution)/shard_map/ppermute | solution.py:319
  62.3 4.7 %collective-permute-start.3 = (s32[6]{0:T(128)S(1)}, s32[6]{0:T(128)S(1)}, u32[]{:S(2)}, u32[]{:S(2)}) collective-permute-start(s32[6]{0:T(128)S(1)} %reshape.366), channel_id=1, source_target_pairs={{0,32},{32,64},{64,96},{96,128},{128,160},{160,192},{192,224},{224... | collective-permute-start | bytes 80 | tf_op jit(solution)/shard_map/ppermute | solution.py:320
  67.1 25.5 %all-to-all-start.1 = ((bf16[4,12,128,128]{3,2,1,0:T(8,128)(2,1)}), bf16[4,12,128,128]{3,2,1,0:T(8,128)(2,1)}, u32[]{:S(2)}, u32[]{:S(2)}) async-start(bf16[4,12,128,128]{3,2,1,0:T(8,128)(2,1)} %bitcast.50), calls=%async_computation.1 | async-start | bytes 3145728 | tf_op jit(solution)/shard_map/all_to_all | solution.py:323
  71.4 59.4 %collective-permute-start.4 = (bf16[5,16,128,128]{3,2,1,0:T(8,128)(2,1)}, bf16[5,16,128,128]{3,2,1,0:T(8,128)(2,1)}, u32[]{:S(2)}, u32[]{:S(2)}) collective-permute-start(bf16[5,16,128,128]{3,2,1,0:T(8,128)(2,1)} %collective-permute-done.refs_6_), channel_id=1, source_target_pairs={{0,32},{32,64},{64,96},{96,128},{128,160},{160,192},{192,224},{224... | collective-permute-start | bytes 7864328 | tf_op jit(solution)/shard_map/ppermute | solution.py:281
  71.5 59.3 %collective-permute-start.5 = (bf16[5,16,128,128]{3,2,1,0:T(8,128)(2,1)}, bf16[5,16,128,128]{3,2,1,0:T(8,128)(2,1)}, u32[]{:S(2)}, u32[]{:S(2)}) collective-permute-start(bf16[5,16,128,128]{3,2,1,0:T(8,128)(2,1)} %collective-permute-done.1.refs_7_), channel_id=1, source_target_pairs={{0,224},{32,0},{64,32},{96,64},{128,96},{160,128},{192,160},{224,1... | collective-permute-start | bytes 7864328 | tf_op jit(solution)/shard_map/ppermute | solution.py:281
  92.6 9.6 %collective-permute-start.6 = (bf16[4,12,128,128]{3,2,1,0:T(8,128)(2,1)}, bf16[4,12,128,128]{3,2,1,0:T(8,128)(2,1)}, u32[]{:S(2)}, u32[]{:S(2)}) collective-permute-start(bf16[4,12,128,128]{3,2,1,0:T(8,128)(2,1)} %all-to-all-done.1), channel_id=1, source_target_pairs={{0,1},{1,0},{2,3},{3,2},{4,5},{5,4},{6,7},{7,6},{8,9},{9,8},{10,11... | collective-permute-start | bytes 4718600 | tf_op jit(solution)/shard_map/ppermute | solution.py:326
  97.0 31.9 %collective-permute-start.8 = (bf16[5,8,128,128]{3,2,1,0:T(8,128)(2,1)}, bf16[5,8,128,128]{3,2,1,0:T(8,128)(2,1)S(1)}, u32[]{:S(2)}, u32[]{:S(2)}) collective-permute-start(bf16[5,8,128,128]{3,2,1,0:T(8,128)(2,1)} %slice.22), channel_id=1, source_target_pairs={{0,8},{8,16},{16,24},{24,0},{1,9},{9,17},{17,25},{25,1},{2,10},{10... | collective-permute-start | bytes 3932168 | tf_op jit(solution)/shard_map/ppermute | solution.py:281
  100.4 30.4 %collective-permute-start.10 = (bf16[5,8,128,128]{3,2,1,0:T(8,128)(2,1)}, bf16[5,8,128,128]{3,2,1,0:T(8,128)(2,1)}, u32[]{:S(2)}, u32[]{:S(2)}) collective-permute-start(bf16[5,8,128,128]{3,2,1,0:T(8,128)(2,1)} %slice.23), channel_id=1, source_target_pairs={{0,24},{8,0},{16,8},{24,16},{1,25},{9,1},{17,9},{25,17},{2,26},{10... | collective-permute-start | bytes 3932168 | tf_op jit(solution)/shard_map/ppermute | solution.py:281
  128.9 5.2 %copy-start.4 = (bf16[5,8,128,128]{3,2,1,0:T(8,128)(2,1)}, bf16[5,8,128,128]{3,2,1,0:T(8,128)(2,1)S(1)}, u32[]{:S(2)}) copy-start(bf16[5,8,128,128]{3,2,1,0:T(8,128)(2,1)S(1)} %collective-permute-done.8.refs_2_) | copy-start | bytes 3932164
  130.8 58.4 %collective-permute-start.11 = (bf16[5,16,128,128]{3,2,1,0:T(8,128)(2,1)}, bf16[5,16,128,128]{3,2,1,0:T(8,128)(2,1)}, u32[]{:S(2)}, u32[]{:S(2)}) collective-permute-start(bf16[5,16,128,128]{3,2,1,0:T(8,128)(2,1)} %collective-permute-done.4.refs_8_), channel_id=1, source_target_pairs={{0,32},{32,64},{64,96},{96,128},{128,160},{160,192},{192,224},{224... | collective-permute-start | bytes 7864328 | tf_op jit(solution)/shard_map/ppermute | solution.py:281
  130.8 58.4 %collective-permute-start.12 = (bf16[5,16,128,128]{3,2,1,0:T(8,128)(2,1)}, bf16[5,16,128,128]{3,2,1,0:T(8,128)(2,1)}, u32[]{:S(2)}, u32[]{:S(2)}) collective-permute-start(bf16[5,16,128,128]{3,2,1,0:T(8,128)(2,1)} %collective-permute-done.5.refs_9_), channel_id=1, source_target_pairs={{0,224},{32,0},{64,32},{96,64},{128,96},{160,128},{192,160},{224,1... | collective-permute-start | bytes 7864328 | tf_op jit(solution)/shard_map/ppermute | solution.py:281
  156.7 43.8 %all-to-all-start.2 = ((bf16[32,15,16,128]{3,2,1,0:T(8,128)(2,1)}), bf16[32,15,16,128]{3,2,1,0:T(8,128)(2,1)}, u32[]{:S(2)}, u32[]{:S(2)}) async-start(bf16[32,15,16,128]{3,2,1,0:T(8,128)(2,1)} %bitcast.51), calls=%async_computation.2 | async-start | bytes 3932160 | tf_op jit(solution)/shard_map/all_to_all | solution.py:268
  166.1 29.4 %copy-start.1 = (bf16[4,6,640,128]{3,2,1,0:T(8,128)(2,1)S(1)}, bf16[4,6,640,128]{3,2,1,0:T(8,128)(2,1)}, u32[]{:S(2)}) copy-start(bf16[4,6,640,128]{3,2,1,0:T(8,128)(2,1)} %get-tuple-element.48.mixed_ref) | copy-start | bytes 11796484
  166.1 29.4 %copy-start.3 = (s32[97]{0:T(128)S(1)}, s32[97]{0:T(128)}, u32[]{:S(2)}) copy-start(s32[97]{0:T(128)} %pad_add_fusion.info_ref) | copy-start | bytes 1168
  192.8 22.4 %collective-permute-start.13 = (bf16[5,6,128,128]{3,2,1,0:T(8,128)(2,1)}, bf16[5,6,128,128]{3,2,1,0:T(8,128)(2,1)S(1)}, u32[]{:S(2)}, u32[]{:S(2)}) collective-permute-start(bf16[5,6,128,128]{3,2,1,0:T(8,128)(2,1)} %get-tuple-element.55), channel_id=1, source_target_pairs={{0,32},{32,64},{64,96},{96,128},{128,160},{160,192},{192,224},{224... | collective-permute-start | bytes 2949128 | tf_op jit(solution)/shard_map/ppermute | solution.py:281
  192.9 22.3 %collective-permute-start.14 = (bf16[5,6,128,128]{3,2,1,0:T(8,128)(2,1)}, bf16[5,6,128,128]{3,2,1,0:T(8,128)(2,1)}, u32[]{:S(2)}, u32[]{:S(2)}) collective-permute-start(bf16[5,6,128,128]{3,2,1,0:T(8,128)(2,1)} %get-tuple-element.56), channel_id=1, source_target_pairs={{0,224},{32,0},{64,32},{96,64},{128,96},{160,128},{192,160},{224,1... | collective-permute-start | bytes 2949128 | tf_op jit(solution)/shard_map/ppermute | solution.py:281
  200.5 24.5 %all-to-all-start.3 = ((bf16[32,6,16,128]{3,2,1,0:T(8,128)(2,1)}), bf16[32,6,16,128]{3,2,1,0:T(8,128)(2,1)}, u32[]{:S(2)}, u32[]{:S(2)}) async-start(bf16[32,6,16,128]{3,2,1,0:T(8,128)(2,1)} %bitcast.13), calls=%async_computation.3 | async-start | bytes 1572864 | tf_op jit(solution)/shard_map/all_to_all | solution.py:268
  215.2 1.5 copy-start.2
  225.0 15.4 %all-to-all-start.4 = ((bf16[32,3,16,128]{3,2,1,0:T(8,128)(2,1)}), bf16[32,3,16,128]{3,2,1,0:T(8,128)(2,1)S(1)}, u32[]{:S(2)}, u32[]{:S(2)}) async-start(bf16[32,3,16,128]{3,2,1,0:T(8,128)(2,1)} %bitcast.19), calls=%async_computation.4 | async-start | bytes 786432 | tf_op jit(solution)/shard_map/all_to_all | solution.py:268

commit v4 on v3

v4 whole, which is shorter than its diff:
```python
import functools

import jax
import jax.numpy as jnp
from jax import lax
from jax.experimental import pallas as pl
from jax.experimental.pallas import tpu as pltpu
from jax.sharding import Mesh, PartitionSpec as P

Z, Y, X, C = 8, 4, 4, 2
M = X * C
CAP = 3
SLOTS = Z * CAP
OFFSETS = (0, -1, 1, -2, 2, -3, 3, 4)
RANK = tuple(OFFSETS.index(((d + 3) % Z) - 3) for d in range(Z))
TILE = 16
MIRROR = tuple(OFFSETS.index(-d if -d in OFFSETS else d) for d in OFFSETS)
PSI_ORDER = (0, 1, 2, 7, 3, 4, 5, 6)


def ring(size, way):
    return [
        (i * C + c, (i + (way if c == 0 else -way)) % size * C + c)
        for i in range(size)
        for c in range(C)
    ]


def left_products(blocks, psi):
    terms, width = blocks.shape[0], blocks.shape[-1]
    mixed = jnp.dot(
        blocks.reshape(terms * width, width), psi, preferred_element_type=jnp.float32
    ).astype(jnp.bfloat16)
    return jnp.concatenate([mixed[w * width : (w + 1) * width] for w in range(terms)], axis=1)


def times_right(mixed, chosen):
    total = lax.dot_general(
        mixed,
        jnp.concatenate([chosen[w, 0] for w in range(chosen.shape[0])], axis=1),
        (((1,), (1,)), ((), ())),
        preferred_element_type=jnp.float32,
    )
    width = total.shape[0]
    return total.astype(jnp.bfloat16).reshape(M, width // M, width)


def left_products_turned(blocks, psi):
    terms, width = blocks.shape[0], blocks.shape[-1]
    mixed = jnp.dot(
        blocks.reshape(terms * width, width), psi, preferred_element_type=jnp.float32
    )
    turned = [mixed[w * width : (w + 1) * width].T for w in range(terms)]
    return jnp.concatenate(turned, axis=0).astype(jnp.bfloat16)


def right_times(chosen, turned):
    wide = jnp.concatenate([chosen[w, 0] for w in range(chosen.shape[0])], axis=1)
    total = jnp.dot(wide, turned, preferred_element_type=jnp.float32).T
    width = total.shape[0]
    return total.astype(jnp.bfloat16).reshape(M, width // M, width)


def middle_kernel(near, info_ref, *refs):
    psi, lefts, rights = refs[:C], refs[C : C + Y], refs[C + Y : C + Y + near]
    near_ref, far_ref, low_ref, high_ref, left, right, left_sems, right_sems = refs[C + Y + near :]
    home = pl.program_id(0)
    far = far_ref.shape[1] // CAP

    def left_copy(source, sector, i):
        return pltpu.make_async_copy(source.at[:, pl.ds(sector, 1)], left.at[i], left_sems.at[i])

    def right_copy(source, sector, i):
        return pltpu.make_async_copy(source.at[:, pl.ds(sector, 1)], right.at[i], right_sems.at[i])

    def start_home(h, carry):
        apart = (Y + info_ref[Y * SLOTS + 1] * (h - info_ref[Y * SLOTS])) % Y
        for n, source in enumerate(lefts):

            @pl.when(apart == n)
            def _(source=source):
                for q in range(SLOTS):
                    left_copy(source, info_ref[h * SLOTS + q] // 16, h * SLOTS + q).start()

        for q in range(near * CAP):
            sector = info_ref[h * SLOTS + q] % 16
            right_copy(rights[q // CAP], sector, h * near * CAP + q).start()
        return carry

    @pl.when(home == 0)
    def _():
        lax.fori_loop(0, Y, start_home, 0)

    for q in range(SLOTS):
        left_copy(lefts[0], 0, home * SLOTS + q).wait()
    for q in range(near * CAP):
        right_copy(rights[0], 0, home * near * CAP + q).wait()
    half = Z // C
    flipped = (1 - info_ref[Y * SLOTS + 1]) // 2
    for q in range(SLOTS):
        p, c = divmod(q, CAP)
        part, at = divmod(PSI_ORDER.index(p), half)
        shift = PSI_ORDER.index(MIRROR[p]) % half - at
        blocks = left[home * SLOTS + q, :, 0]
        mine = psi[part][0, at * CAP + c + flipped * (shift * CAP)]
        if q < near * CAP:
            chosen = right[home * near * CAP + q]
            to = q + flipped * ((MIRROR[p] - p) * CAP)
            near_ref[0, :, pl.ds(to, 1)] = times_right(left_products(blocks, mine), chosen)[:, None]
        elif q < (near + far) * CAP:
            far_ref[0, q - near * CAP] = left_products_turned(blocks, mine)
        else:
            turned = left_products_turned(blocks, mine)
            sector = info_ref[home * SLOTS + q] % 16
            tile = jnp.full((TILE, turned.shape[1]), sector, jnp.int32).astype(jnp.float32)
            turned = jnp.concatenate([turned, tile.astype(jnp.bfloat16)], axis=0)

            @pl.when(home < Y // 2)
            def _(turned=turned, i=q - (near + far) * CAP):
                low_ref[0, i] = turned

            @pl.when(home >= Y // 2)
            def _(turned=turned, i=q - (near + far) * CAP):
                high_ref[0, i] = turned


def far_kernel(count, info_ref, mixed_ref, *refs):
    rights, (out_ref, held, held_mixed, sems, mixed_sems) = refs[:count], refs[count:]
    flipped = (1 - info_ref[Y * SLOTS + 1]) // 2
    copies = []
    mixed_copies = [
        pltpu.make_async_copy(mixed_ref.at[h], held_mixed.at[h], mixed_sems.at[h])
        for h in range(Y)
    ]
    for h in range(Y):
        for s in range(count * CAP):
            place = s // CAP
            sector = info_ref[h * SLOTS + (Z - 1 - count) * CAP + s] % 16
            copies.append(
                pltpu.make_async_copy(
                    rights[place].at[:, pl.ds(sector, 1)],
                    held.at[h * count * CAP + s],
                    sems.at[h * count * CAP + s],
                )
            )
    for h in range(Y):
        mixed_copies[h].start()
        for copy in copies[h * count * CAP : (h + 1) * count * CAP]:
            copy.start()
    for h in range(Y):
        slots = range(h * count * CAP, (h + 1) * count * CAP)
        mixed_copies[h].wait()
        for i in slots:
            copies[i].wait()
        for s, i in enumerate(slots):
            to = s + flipped * (CAP if s < CAP else -CAP)
            out_ref[h, :, pl.ds(to, 1)] = right_times(held[i], held_mixed[h, s])[:, None]


def guest_kernel(
    info_ref, low_index, high_index, low_ref, high_ref, one_ref, other_ref,
    out_ref, held, guests, sems, guest_sems,
):
    half = Y // 2 * CAP
    rows = low_ref.shape[2] - TILE
    sides = [
        pltpu.make_async_copy(side, guests.at[pl.ds(n * (Y // 2), Y // 2)], guest_sems.at[n])
        for n, side in enumerate((low_ref, high_ref))
    ]
    for side in sides:
        side.start()

    def start(low_source, high_source):
        for i in range(Y * CAP):
            source = low_source if i < half else high_source
            index = low_index if i < half else high_index
            sector = index[i % half // CAP, i % CAP]
            pltpu.make_async_copy(
                source.at[:, pl.ds(sector, 1)], held.at[i], sems.at[i]
            ).start()

    @pl.when(info_ref[Y * SLOTS + 1] == 1)
    def _():
        start(other_ref, one_ref)

    @pl.when(info_ref[Y * SLOTS + 1] != 1)
    def _():
        start(one_ref, other_ref)

    for h in range(Y):
        if h % (Y // 2) == 0:
            sides[h // (Y // 2)].wait()
        slots = range(h * CAP, (h + 1) * CAP)
        for i in slots:
            pltpu.make_async_copy(one_ref.at[:, pl.ds(0, 1)], held.at[i], sems.at[i]).wait()
        for s, i in enumerate(slots):
            out_ref[h, :, s] = right_times(held[i], guests[h, s, :rows])


LARGE = pltpu.CompilerParams(vmem_limit_bytes=60 * 1024 * 1024)


def cost(slots, matmuls, terms, width):
    return pl.CostEstimate(
        flops=2 * slots * matmuls * terms * width**3,
        bytes_accessed=slots * (matmuls * terms + 2) * width * width * 2,
        transcendentals=0,
    )


def middle_products(info, psi, lefts, rights):
    terms, _, width, _ = lefts[0].shape
    near, far = len(rights), Z - 1 - len(rights)
    one = (terms, 1, width, width)
    turned = jax.ShapeDtypeStruct((Y, far * CAP, terms * width, width), jnp.bfloat16)
    guest = jax.ShapeDtypeStruct((Y // 2, CAP, terms * width + TILE, width), jnp.bfloat16)
    out = jax.ShapeDtypeStruct((Y, M, near * CAP, width // M, width), jnp.bfloat16)
    per_home = lambda shape: pl.BlockSpec(
        (1,) + shape[1:], lambda h, info: (h,) + (0,) * (len(shape) - 1)
    )
    return pl.pallas_call(
        functools.partial(middle_kernel, near),
        out_shape=[out, turned, guest, guest],
        grid_spec=pltpu.PrefetchScalarGridSpec(
            num_scalar_prefetch=1,
            grid=(Y,),
            in_specs=[per_home(p.shape) for p in psi]
            + [pl.BlockSpec(memory_space=pl.ANY)] * (len(lefts) + near),
            out_specs=[
                per_home(out.shape),
                per_home(turned.shape),
                pl.BlockSpec(
                    (1,) + guest.shape[1:],
                    lambda h, info: (jnp.minimum(h, Y // 2 - 1), 0, 0, 0),
                ),
                pl.BlockSpec(
                    (1,) + guest.shape[1:],
                    lambda h, info: (jnp.maximum(h - Y // 2, 0), 0, 0, 0),
                ),
            ],
            scratch_shapes=[
                pltpu.VMEM((Y * SLOTS,) + one, jnp.bfloat16),
                pltpu.VMEM((Y * near * CAP,) + one, jnp.bfloat16),
                pltpu.SemaphoreType.DMA((Y * SLOTS,)),
                pltpu.SemaphoreType.DMA((Y * near * CAP,)),
            ],
        ),
        compiler_params=LARGE,
        cost_estimate=cost(Y * SLOTS, 2, terms, width),
    )(info, *psi, *lefts, *rights)


SMALL = pltpu.CompilerParams(vmem_limit_bytes=24 * 1024 * 1024)
IN_VMEM = pl.BlockSpec(memory_space=pltpu.VMEM)
IN_HBM = pl.BlockSpec(memory_space=pltpu.HBM)


def far_products(info, mixed, arrived):
    slots, width = mixed.shape[1], mixed.shape[3]
    terms = mixed.shape[2] // width
    return pl.pallas_call(
        functools.partial(far_kernel, len(arrived)),
        out_shape=jax.ShapeDtypeStruct((Y, M, slots, width // M, width), jnp.bfloat16),
        in_specs=[pl.BlockSpec(memory_space=pltpu.SMEM)] + [IN_HBM] * (1 + len(arrived)),
        out_specs=IN_VMEM,
        scratch_shapes=[
            pltpu.VMEM((Y * slots, terms, 1, width, width), jnp.bfloat16),
            pltpu.VMEM(mixed.shape, jnp.bfloat16),
            pltpu.SemaphoreType.DMA((Y * slots,)),
            pltpu.SemaphoreType.DMA((Y,)),
        ],
        compiler_params=LARGE,
        cost_estimate=cost(Y * slots, 2, terms, width),
    )(info, mixed, *arrived)


def guest_products(info, low_index, high_index, low, high, arrived):
    terms, _, width, _ = arrived[0].shape
    return pl.pallas_call(
        guest_kernel,
        out_shape=jax.ShapeDtypeStruct((Y, M, CAP, width // M, width), jnp.bfloat16),
        in_specs=[pl.BlockSpec(memory_space=pltpu.SMEM)] * 3 + [IN_HBM] * 4,
        out_specs=IN_VMEM,
        scratch_shapes=[
            pltpu.VMEM((Y * CAP, terms, 1, width, width), jnp.bfloat16),
            pltpu.VMEM((Y,) + low.shape[1:], jnp.bfloat16),
            pltpu.SemaphoreType.DMA((Y * CAP,)),
            pltpu.SemaphoreType.DMA((2,)),
        ],
        compiler_params=LARGE,
        cost_estimate=cost(Y * CAP, 2, terms, width),
    )(info, low_index, high_index, low, high, *arrived)


def settle_kernel(place_ref, *refs):
    parts, out_ref = refs[:-1], refs[-1]
    starts = [0]
    for part in parts:
        starts.append(starts[-1] + part.shape[0])
    for k in range(out_ref.shape[0]):
        place = place_ref[k]
        for n, part in enumerate(parts):

            @pl.when((place >= starts[n]) & (place < starts[n + 1]))
            def _(k=k, part=part, start=starts[n], place=place):
                out_ref[k] = part[place - start]


def settle(place, parts):
    return pl.pallas_call(
        settle_kernel,
        out_shape=jax.ShapeDtypeStruct(place.shape + parts[0].shape[1:], parts[0].dtype),
        in_specs=[pl.BlockSpec(memory_space=pltpu.SMEM)] + [IN_VMEM] * len(parts),
        out_specs=IN_VMEM,
        compiler_params=SMALL,
    )(place, *parts)


def exchange(part):
    part = part.reshape((Y * M,) + part.shape[2:])
    part = lax.all_to_all(part, ("y", "x", "c"), split_axis=0, concat_axis=0, tiled=True)
    return part.reshape((Y, M) + part.shape[1:])


def add_up(part):
    return part.astype(jnp.float32).sum(axis=1).astype(jnp.bfloat16)


def on_device(wavefunction, left_environment, right_environment, right_sector):
    z, y, core = (lax.axis_index(name) for name in ("z", "y", "c"))
    blocks, width = wavefunction.shape[:2]
    owned = left_environment.shape[1]
    members = blocks // owned
    tie = lax.optimization_barrier

    way = 1 - 2 * core

    def hop(moved, axis, direction):
        size = Z if axis == "z" else Y
        return lax.ppermute(moved, (axis, "c"), ring(size, direction))

    def step(moving, axis="z"):
        return [hop(moving[0], axis, 1), hop(moving[1], axis, -1)]

    first = step([right_environment] * 2)

    index = jnp.arange(blocks, dtype=jnp.int32)
    earlier = index[None, :] < index[:, None]

    def slots_of(sectors, direction):
        owner = sectors // owned
        same = owner[:, :, None] == owner[:, None, :]
        place = jnp.sum((same & earlier).astype(jnp.int32), axis=2)
        offset = (direction * (owner // Y - z)) % Z
        rank = sum(jnp.where(offset == d, RANK[d], 0) for d in range(Z))
        return owner % Y, rank * CAP + place

    def into(slots, values, count):
        hit = slots[:, None, :] == jnp.arange(count, dtype=jnp.int32)[None, :, None]
        return jnp.sum(jnp.where(hit, values[:, None, :], 0), axis=2)

    column, slot = slots_of(right_sector[None], 1)
    slot = column * SLOTS + slot
    split = SLOTS // C
    rank = (slot % SLOTS) // CAP
    position = sum(jnp.where(rank == p, n, 0) for n, p in enumerate(PSI_ORDER)) * CAP + slot % CAP
    mine = column * split + jnp.where(position // split == core, position % split, -Y * SLOTS)
    source = into(mine, index[None], Y * split)[0]
    outgoing = wavefunction.at[source].get(mode="promise_in_bounds")
    outgoing = outgoing.reshape((Y, split) + wavefunction.shape[1:])

    sectors = jnp.broadcast_to(right_sector, (Y, blocks))
    sectors = lax.all_to_all(sectors, "y", split_axis=0, concat_axis=0, tiled=True)
    left_environment, sectors = tie((left_environment, sectors))
    near_left = step([left_environment] * 2, "y")
    column, here = slots_of(sectors, way)
    here = jnp.where(column == y, here, -1)
    info = into(here, (index // members) * 16 + sectors % owned, SLOTS)
    info = jnp.concatenate([info.reshape(-1), jnp.stack([y, way]).astype(jnp.int32)])

    second = step(first)
    psi = lax.all_to_all(outgoing, "y", split_axis=0, concat_axis=0, tiled=True)
    far_left = hop(near_left[0], "y", 1)
    other = lax.ppermute(psi, "c", [(0, 1), (1, 0)])
    psi = (jnp.where(core == 0, psi, other), jnp.where(core == 0, other, psi))
    second, psi = tie((second, psi))
    third = step(second)
    lefts = (left_environment, near_left[1], far_left, near_left[0])
    arrived = [right_environment] + first + second
    near, far_mixed, low, high = middle_products(info, psi, lefts, arrived)
    low = lax.ppermute(low, "z", [(i, (i + 1) % Z) for i in range(Z)])
    high = lax.ppermute(high, "z", [(i, (i - 1) % Z) for i in range(Z)])
    far = far_products(info, far_mixed, third)
    far, near = tie((far, exchange(near)))
    sectors = [g[:, :, -1, 0].astype(jnp.int32) for g in (low, high)]
    guests = guest_products(info, *sectors, low, high, third)
    guests, far = tie((guests, exchange(far)))
    guests = add_up(exchange(guests))
    flat = lambda part: part.reshape((-1,) + part.shape[2:])
    column, at = slot[0] // SLOTS, slot[0] % SLOTS
    first_far, first_end = 5 * CAP, 7 * CAP
    near, far = flat(add_up(near)), flat(add_up(far))
    place = jnp.where(
        at < first_far,
        column * first_far + at,
        near.shape[0] + column * (first_end - first_far) + at - first_far,
    )
    settled = settle(jnp.where(at < first_end, place, -1), (near, far))
    guests, settled = tie((guests, settled))
    home = [
        (i * Y + j, (i + (-1 if j < Y // 2 else 1)) % Z * Y + j) for i in range(Z) for j in range(Y)
    ]
    end = lax.ppermute(guests, ("z", "y"), home)

    end = flat(end)
    place = jnp.where(at < first_end, end.shape[0] + index, column * CAP + at - first_end)
    return settle(place, (end, settled))


def solution(mesh):
    fine = Mesh(mesh.devices.reshape(Z, Y, X, C), ("z", "y", "x", "c"))
    bond = ("z", "y")
    placed = (
        P(bond, None, None),
        P(("x", "c"), bond, None, None),
        P(("x", "c"), bond, None, None),
        P(bond),
    )
    return jax.shard_map(
        on_device, mesh=fine, in_specs=placed, out_specs=P(bond, ("x", "c"), None), check_vma=False
    )
```

time: 242 us -> 239 us (0.988)
  starting transfers between devices: 56.7 us -> 46.8 us
  local copies, waits for them, and re-layouts: 11 us -> 2.7 us
  blocking collectives: 0 us -> 8.18 us
  other arithmetic: 6.63 us -> 13.1 us
  Pallas kernels: 33.8 us -> 40 us
  matrix products: 4.05 us -> 0 us
    all_to_all x1, waiting for transfers between devices: 18.4 us -> 0.01 us  [on_device(): psi = lax.all_to_all(outgoing, 'y', split_axis=0, concat_axis=0, tiled=True)]
    ppermute x14 -> x12, waiting for transfers between devices: 98.5 us -> 117 us  [the longest x9 106 us: hop(): return lax.ppermute(moved, (axis, 'c'), ring(size, direction))]
    all_to_all x0 -> x1, blocking collectives: none -> 8.18 us  [on_device(): lax.all_to_all(sectors, 'y', split_axis=0, concat_axis=0, tiled=True)]
    all_to_all x3, waiting for transfers between devices: 12 us -> 6.84 us  [exchange(): lax.all_to_all(part, ('y', 'x', 'c'), split_axis=0, concat_axis=0, tiled=...]
    slice x3 -> x0, local copies, waits for them, and re-layouts: 5.11 us -> none  [the longest x1 2.56 us: on_device(): near_left[0][:, :owned // 2]]
    pallas_call x3 -> x4, Pallas kernels: 28.8 us -> 33.9 us  [the longest x1 25.3 us: middle_products(): pl.pallas_call(functools.partial(middle_kernel, near), out_shape=[out, tu...]
    all_to_all x1 -> x0, starting transfers between devices: 4.18 us -> none  [on_device(): lax.all_to_all(sectors, 'y', split_axis=0, concat_axis=0, tiled=True)]
    dot_general x3 -> x0, matrix products: 4.05 us -> none  [gather(): jnp.einsum('kyms,ymsil->kil', pick, part, preferred_element_type=jnp.floa...]
  transfers between devices with their start and end apart: 20 -> 17, of which waited for: 10 -> 9; matrix products, arithmetic and copies ran while one was open for 8% -> 6% of each run, Pallas kernels for 14% -> 16%
where the time goes in v4:
time: 239 us; the launch traced here: 238 us
  waiting for transfers between devices  127 us (53%)
  starting transfers between devices  46.8 us (20%)
  Pallas kernels  40 us (17%)
  other arithmetic  13.1 us (5%)
  blocking collectives  8.18 us (3%)
  local copies, waits for them, and re-layouts  2.7 us (1%)
    ppermute x9, waiting for transfers between devices, hop(): return lax.ppermute(moved, (axis, 'c'), ring(size, direction))  106 us
    pallas_call x1, Pallas kernels, middle_products(): pl.pallas_call(functools.partial(middle_kernel, near), out_shape=[out, tu...  25.3 us
    all_to_all x3, starting transfers between devices, exchange(): lax.all_to_all(part, ('y', 'x', 'c'), split_axis=0, concat_axis=0, tiled=...  22.5 us
    ppermute x9, starting transfers between devices, hop(): return lax.ppermute(moved, (axis, 'c'), ring(size, direction))  14.9 us
    all_to_all x1, blocking collectives, on_device(): lax.all_to_all(sectors, 'y', split_axis=0, concat_axis=0, tiled=True)  8.18 us
    ppermute x1, waiting for transfers between devices, on_device(): low = lax.ppermute(low, 'z', [(i, (i + 1) % Z) for i in range(Z)])  7.63 us
    all_to_all x3, waiting for transfers between devices, exchange(): lax.all_to_all(part, ('y', 'x', 'c'), split_axis=0, concat_axis=0, tiled=...  6.84 us
    pallas_call x1, Pallas kernels, far_products(): pl.pallas_call(functools.partial(far_kernel, len(arrived)), out_shape=jax...  6.18 us
  transfers between devices with their start and end apart: 17, of which 9 were waited for; matrix products, arithmetic and copies ran while one was open for 6% of the time, Pallas kernels for 16%

profile of v4, /device:TPU:1, one launch (start us, length us, event | category | flops | bytes accessed | tf_op | source)
XLA Modules:
  0.0 237.8 jit_solution(6661460780182742589)
XLA Ops:
  0.0 6.4 %collective-permute-start = (bf16[5,16,128,128]{3,2,1,0:T(8,128)(2,1)}, bf16[5,16,128,128]{3,2,1,0:T(8,128)(2,1)}, u32[]{:S(2)}, u32[]{:S(2)}) collective-permute-start(bf16[5,16,128,128]{3,2,1,0:T(8,128)(2,1)} %refs_6_.1), channel_id=1, source_target_pairs={{0,32},{1,225},{32,64},{33,1},{64,96},{65,33},{96,128},{97,65},{12... | collective-permute-start | bytes 7864328 | tf_op jit(solution)/shard_map/ppermute | solution.py:340
  7.1 8.2 %all_to_all.29 = s32[4,1,64]{2,1,0:T(1,128)S(1)} all-to-all(s32[4,1,64]{2,1,0:T(1,128)S(1)} %broadcast_in_dim.108), channel_id=1, replica_groups=mesh['z'=8,'y'=4,'x'=4,'c'=2] {'y'}, dimensions={0} | all-to-all | bytes 2048 | tf_op jit(solution)/shard_map/all_to_all | solution.py:373
  18.4 2.0 gather_fusion
  20.4 4.4 %all-to-all-start.1 = ((bf16[4,12,128,128]{3,2,1,0:T(8,128)(2,1)}), bf16[4,12,128,128]{3,2,1,0:T(8,128)(2,1)}, u32[]{:S(2)}, u32[]{:S(2)}) async-start(bf16[4,12,128,128]{3,2,1,0:T(8,128)(2,1)} %bitcast.21), calls=%async_computation.1 | async-start | bytes 3145728 | tf_op jit(solution)/shard_map/all_to_all | solution.py:382
  24.8 37.4 %collective-permute-done.refs_7_ = bf16[5,16,128,128]{3,2,1,0:T(8,128)(2,1)} collective-permute-done((bf16[5,16,128,128]{3,2,1,0:T(8,128)(2,1)}, bf16[5,16,128,128]{3,2,1,0:T(8,128)(2,1)}, u32[]{:S(2)}, u32[]{:S(2)}) %collective-permute-start) | collective-permute-done | bytes 2621472 | tf_op jit(solution)/shard_map/ppermute | solution.py:340
  62.2 3.4 %collective-permute-start.1 = (bf16[5,16,128,128]{3,2,1,0:T(8,128)(2,1)}, bf16[5,16,128,128]{3,2,1,0:T(8,128)(2,1)}, u32[]{:S(2)}, u32[]{:S(2)}) collective-permute-start(bf16[5,16,128,128]{3,2,1,0:T(8,128)(2,1)} %collective-permute-done.refs_7_), channel_id=1, source_target_pairs={{0,32},{1,225},{32,64},{33,1},{64,96},{65,33},{96,128},{97,65},{12... | collective-permute-start | bytes 7864328 | tf_op jit(solution)/shard_map/ppermute | solution.py:340
  65.6 1.3 collective-permute-start.5
  66.9 1.5 collective-permute-start.7
  68.4 2.2 collective-permute-start.4
  70.9 3.1 %collective-permute-done.4 = bf16[4,12,128,128]{3,2,1,0:T(8,128)(2,1)} collective-permute-done((bf16[4,12,128,128]{3,2,1,0:T(8,128)(2,1)}, bf16[4,12,128,128]{3,2,1,0:T(8,128)(2,1)}, u32[]{:S(2)}, u32[]{:S(2)}) %collective-permute-start.4) | collective-permute-done | bytes 1572896 | tf_op jit(solution)/shard_map/ppermute | solution.py:384
  74.0 3.7 %broadcast_select_fusion = (bf16[4,12,128,128]{3,2,1,0:T(8,128)(2,1)}, bf16[4,12,128,128]{3,2,1,0:T(8,128)(2,1)}) fusion(bf16[4,12,128,128]{3,2,1,0:T(8,128)(2,1)} %collective-permute-done.4, bf16[4,12,128,128]{3,2,1,0:T(8,128)(2,1)} %all-to-all-done.1, pred[]{:T(512)S(6)} %eq.212), kind=kLoop, calls=%fused_computation.1 | loop fusion | flops 1572864 | bytes 6291457 | tf_op jit(solution)/shard_map/jit(_where)/select_n | solution.py:385
  77.7 42.7 %collective-permute-done.1.refs_9_ = bf16[5,16,128,128]{3,2,1,0:T(8,128)(2,1)} collective-permute-done((bf16[5,16,128,128]{3,2,1,0:T(8,128)(2,1)}, bf16[5,16,128,128]{3,2,1,0:T(8,128)(2,1)}, u32[]{:S(2)}, u32[]{:S(2)}) %collective-permute-start.1) | collective-permute-done | bytes 2621472 | tf_op jit(solution)/shard_map/ppermute | solution.py:340
  120.4 4.2 %collective-permute-done.3.refs_10_ = bf16[5,16,128,128]{3,2,1,0:T(8,128)(2,1)} collective-permute-done((bf16[5,16,128,128]{3,2,1,0:T(8,128)(2,1)}, bf16[5,16,128,128]{3,2,1,0:T(8,128)(2,1)}, u32[]{:S(2)}, u32[]{:S(2)}) %collective-permute-start.3) | collective-permute-done | bytes 2621472 | tf_op jit(solution)/shard_map/ppermute | solution.py:340
  124.7 1.5 collective-permute-start.11
  127.0 25.3 %shard_map.46 = (bf16[4,8,15,16,128]{4,3,2,1,0:T(8,128)(2,1)}, bf16[4,6,640,128]{3,2,1,0:T(8,128)(2,1)}, bf16[2,3,656,128]{3,2,1,0:T(8,128)(2,1)}, bf16[2,3,656,128]{3,2,1,0:T(8,128)(2,1)}) custom-call(s32[98]{0:T(128)} %pad_add_fusion.info_ref, bf16[4,12,128,128]{3,2,1,0:T(8,128)(2,1)} %get-tuple-element.22.refs_0_, ...), custom_call_target="tpu_custom_call" | custom-call | flops 4026531840 | bytes 37748736 | tf_op jit(solution)/shard_map/pallas_call | solution.py:221
  152.3 7.9 %all-to-all-start.2 = ((bf16[32,15,16,128]{3,2,1,0:T(8,128)(2,1)}), bf16[32,15,16,128]{3,2,1,0:T(8,128)(2,1)}, u32[]{:S(2)}, u32[]{:S(2)}) async-start(bf16[32,15,16,128]{3,2,1,0:T(8,128)(2,1)} %bitcast.24), calls=%async_computation.2 | async-start | bytes 3932160 | tf_op jit(solution)/shard_map/all_to_all | solution.py:321
  160.3 2.7 %collective-permute-start.9 = (bf16[2,3,656,128]{3,2,1,0:T(8,128)(2,1)}, bf16[2,3,656,128]{3,2,1,0:T(8,128)(2,1)}, u32[]{:S(2)}, u32[]{:S(2)}) collective-permute-start(bf16[2,3,656,128]{3,2,1,0:T(8,128)(2,1)} %get-tuple-element.28), channel_id=1, source_target_pairs={{0,224},{32,0},{64,32},{96,64},{128,96},{160,128},{192,160},{224,1... | collective-permute-start | bytes 3022856 | tf_op jit(solution)/shard_map/ppermute | solution.py:392
  163.0 20.8 %collective-permute-done.10.one_ref.refs_0_ = bf16[5,16,128,128]{3,2,1,0:T(8,128)(2,1)} collective-permute-done((bf16[5,16,128,128]{3,2,1,0:T(8,128)(2,1)}, bf16[5,16,128,128]{3,2,1,0:T(8,128)(2,1)}, u32[]{:S(2)}, u32[]{:S(2)}) %collective-permute-start.10) | collective-permute-done | bytes 2621472 | tf_op jit(solution)/shard_map/ppermute | solution.py:340
  183.8 1.2 collective-permute-done.11.other_ref.refs_1_
  185.0 6.2 %shard_map.48 = bf16[4,8,6,16,128]{4,3,2,1,0:T(8,128)(2,1)} custom-call(s32[98]{0:T(128)} %pad_add_fusion.info_ref, bf16[4,6,640,128]{3,2,1,0:T(8,128)(2,1)} %get-tuple-element.29.mixed_ref, bf16[5,16,128,128]{3,2,1,0:T(8,128)(2,1)} %collective-permute-done.10.one_ref.refs_0_, bf16[5,16,128,128]{3,2,1,0:T(8,128)(2,1)} %collective-permute-done.11.other_ref.refs_1_), custom_call_target="tpu_custom_call" | custom-call | flops 1006632960 | bytes 9437184 | tf_op jit(solution)/shard_map/pallas_call | solution.py:261
  191.2 7.2 %all-to-all-start.3 = ((bf16[32,6,16,128]{3,2,1,0:T(8,128)(2,1)}), bf16[32,6,16,128]{3,2,1,0:T(8,128)(2,1)S(1)}, u32[]{:S(2)}, u32[]{:S(2)}) async-start(bf16[32,6,16,128]{3,2,1,0:T(8,128)(2,1)} %bitcast.22), calls=%async_computation.3 | async-start | bytes 1572864 | tf_op jit(solution)/shard_map/all_to_all | solution.py:321
  198.4 7.6 %collective-permute-done.8.low_ref = bf16[2,3,656,128]{3,2,1,0:T(8,128)(2,1)} collective-permute-done((bf16[2,3,656,128]{3,2,1,0:T(8,128)(2,1)}, bf16[2,3,656,128]{3,2,1,0:T(8,128)(2,1)}, u32[]{:S(2)}, u32[]{:S(2)}) %collective-permute-start.8) | collective-permute-done | bytes 1007648 | tf_op jit(solution)/shard_map/ppermute | solution.py:391
  206.0 1.5 fusion.2.low_index
  207.5 1.5 fusion.1.high_index
  209.0 5.0 %shard_map.47 = bf16[4,8,3,16,128]{4,3,2,1,0:T(8,128)(2,1)} custom-call(s32[98]{0:T(128)} %pad_add_fusion.info_ref, s32[2,3]{1,0:T(2,128)} %fusion.2.low_index, s32[2,3]{1,0:T(2,128)} %fusion.1.high_index, bf16[2,3,656,128]{3,2,1,0:T(8,128)(2,1)} %collective-permute-done.8.low_ref, bf16[2,3,656,128]{3,2,1,0:T(8,128)(2,1)} %collective-permute-done.9.high_ref, ...), custom_call_target="tpu_custom_call" | custom-call | flops 503316480 | bytes 4718592 | tf_op jit(solution)/shard_map/pallas_call | solution.py:279
  214.0 7.4 %all-to-all-start.4 = ((bf16[32,3,16,128]{3,2,1,0:T(8,128)(2,1)}), bf16[32,3,16,128]{3,2,1,0:T(8,128)(2,1)}, u32[]{:S(2)}, u32[]{:S(2)}) async-start(bf16[32,3,16,128]{3,2,1,0:T(8,128)(2,1)} %bitcast.25), calls=%async_computation.4 | async-start | bytes 786432 | tf_op jit(solution)/shard_map/all_to_all | solution.py:321
  221.4 1.9 reduce_sum.80
  223.4 1.4 shard_map.49.refs_1_
  224.8 6.8 %all-to-all-done.4 = bf16[32,3,16,128]{3,2,1,0:T(8,128)(2,1)} async-done(((bf16[32,3,16,128]{3,2,1,0:T(8,128)(2,1)}), bf16[32,3,16,128]{3,2,1,0:T(8,128)(2,1)}, u32[]{:S(2)}, u32[]{:S(2)}) %all-to-all-start.4) | async-done | bytes 393248 | tf_op jit(solution)/shard_map/all_to_all | solution.py:321
  231.6 1.0 bitcast_reduce_fusion
  232.8 2.9 %collective-permute-done.12 = bf16[4,3,16,128]{3,2,1,0:T(8,128)(2,1)S(1)} collective-permute-done((bf16[4,3,16,128]{3,2,1,0:T(8,128)(2,1)S(1)}, bf16[4,3,16,128]{3,2,1,0:T(8,128)(2,1)S(1)}, u32[]{:S(2)}, u32[]{:S(2)}) %collective-permute-start.12) | collective-permute-done | bytes 49184 | tf_op jit(solution)/shard_map/ppermute | solution.py:413
  235.7 2.1 shard_map.50
  (33 shorter events, 5.2 us)
Async XLA Ops:
  0.0 18.4 %copy-start = (bf16[64,128,128]{2,1,0:T(8,128)(2,1)S(1)}, bf16[64,128,128]{2,1,0:T(8,128)(2,1)}, u32[]{:S(2)}) copy-start(bf16[64,128,128]{2,1,0:T(8,128)(2,1)} %param.4) | copy-start | bytes 6291460
  0.0 62.2 %collective-permute-start = (bf16[5,16,128,128]{3,2,1,0:T(8,128)(2,1)}, bf16[5,16,128,128]{3,2,1,0:T(8,128)(2,1)}, u32[]{:S(2)}, u32[]{:S(2)}) collective-permute-start(bf16[5,16,128,128]{3,2,1,0:T(8,128)(2,1)} %refs_6_.1), channel_id=1, source_target_pairs={{0,32},{1,225},{32,64},{33,1},{64,96},{65,33},{96,128},{97,65},{12... | collective-permute-start | bytes 7864328 | tf_op jit(solution)/shard_map/ppermute | solution.py:340
  6.4 59.2 %collective-permute-start.2 = (bf16[5,16,128,128]{3,2,1,0:T(8,128)(2,1)}, bf16[5,16,128,128]{3,2,1,0:T(8,128)(2,1)}, u32[]{:S(2)}, u32[]{:S(2)}) collective-permute-start(bf16[5,16,128,128]{3,2,1,0:T(8,128)(2,1)} %refs_6_.1), channel_id=1, source_target_pairs={{0,224},{1,33},{32,0},{33,65},{64,32},{65,97},{96,64},{97,129},{12... | collective-permute-start | bytes 7864328 | tf_op jit(solution)/shard_map/ppermute | solution.py:340
  15.3 51.6 %collective-permute-start.6 = (bf16[5,16,128,128]{3,2,1,0:T(8,128)(2,1)}, bf16[5,16,128,128]{3,2,1,0:T(8,128)(2,1)}, u32[]{:S(2)}, u32[]{:S(2)}) collective-permute-start(bf16[5,16,128,128]{3,2,1,0:T(8,128)(2,1)} %refs_2_), channel_id=1, source_target_pairs={{0,8},{1,25},{8,16},{9,1},{16,24},{17,9},{24,0},{25,17},{2,10},{3,... | collective-permute-start | bytes 7864328 | tf_op jit(solution)/shard_map/ppermute | solution.py:340
  20.4 48.0 %all-to-all-start.1 = ((bf16[4,12,128,128]{3,2,1,0:T(8,128)(2,1)}), bf16[4,12,128,128]{3,2,1,0:T(8,128)(2,1)}, u32[]{:S(2)}, u32[]{:S(2)}) async-start(bf16[4,12,128,128]{3,2,1,0:T(8,128)(2,1)} %bitcast.21), calls=%async_computation.1 | async-start | bytes 3145728 | tf_op jit(solution)/shard_map/all_to_all | solution.py:382
  62.2 58.2 %collective-permute-start.1 = (bf16[5,16,128,128]{3,2,1,0:T(8,128)(2,1)}, bf16[5,16,128,128]{3,2,1,0:T(8,128)(2,1)}, u32[]{:S(2)}, u32[]{:S(2)}) collective-permute-start(bf16[5,16,128,128]{3,2,1,0:T(8,128)(2,1)} %collective-permute-done.refs_7_), channel_id=1, source_target_pairs={{0,32},{1,225},{32,64},{33,1},{64,96},{65,33},{96,128},{97,65},{12... | collective-permute-start | bytes 7864328 | tf_op jit(solution)/shard_map/ppermute | solution.py:340
  65.6 59.1 %collective-permute-start.3 = (bf16[5,16,128,128]{3,2,1,0:T(8,128)(2,1)}, bf16[5,16,128,128]{3,2,1,0:T(8,128)(2,1)}, u32[]{:S(2)}, u32[]{:S(2)}) collective-permute-start(bf16[5,16,128,128]{3,2,1,0:T(8,128)(2,1)} %collective-permute-done.2.refs_8_), channel_id=1, source_target_pairs={{0,224},{1,33},{32,0},{33,65},{64,32},{65,97},{96,64},{97,129},{12... | collective-permute-start | bytes 7864328 | tf_op jit(solution)/shard_map/ppermute | solution.py:340
  65.6 61.4 %collective-permute-start.5 = (bf16[5,16,128,128]{3,2,1,0:T(8,128)(2,1)}, bf16[5,16,128,128]{3,2,1,0:T(8,128)(2,1)}, u32[]{:S(2)}, u32[]{:S(2)}) collective-permute-start(bf16[5,16,128,128]{3,2,1,0:T(8,128)(2,1)} %refs_2_), channel_id=1, source_target_pairs={{0,24},{1,9},{8,0},{9,17},{16,8},{17,25},{24,16},{25,1},{2,26},{3,... | collective-permute-start | bytes 7864328 | tf_op jit(solution)/shard_map/ppermute | solution.py:340
  66.9 60.1 %collective-permute-start.7 = (bf16[5,16,128,128]{3,2,1,0:T(8,128)(2,1)}, bf16[5,16,128,128]{3,2,1,0:T(8,128)(2,1)}, u32[]{:S(2)}, u32[]{:S(2)}) collective-permute-start(bf16[5,16,128,128]{3,2,1,0:T(8,128)(2,1)} %collective-permute-done.6.refs_5_), channel_id=1, source_target_pairs={{0,8},{1,25},{8,16},{9,1},{16,24},{17,9},{24,0},{25,17},{2,10},{3,... | collective-permute-start | bytes 7864328 | tf_op jit(solution)/shard_map/ppermute | solution.py:340
  68.4 5.6 %collective-permute-start.4 = (bf16[4,12,128,128]{3,2,1,0:T(8,128)(2,1)}, bf16[4,12,128,128]{3,2,1,0:T(8,128)(2,1)}, u32[]{:S(2)}, u32[]{:S(2)}) collective-permute-start(bf16[4,12,128,128]{3,2,1,0:T(8,128)(2,1)} %all-to-all-done.1), channel_id=1, source_target_pairs={{0,1},{1,0},{2,3},{3,2},{4,5},{5,4},{6,7},{7,6},{8,9},{9,8},{10,11... | collective-permute-start | bytes 4718600 | tf_op jit(solution)/shard_map/ppermute | solution.py:384
  124.7 59.1 %collective-permute-start.10 = (bf16[5,16,128,128]{3,2,1,0:T(8,128)(2,1)}, bf16[5,16,128,128]{3,2,1,0:T(8,128)(2,1)}, u32[]{:S(2)}, u32[]{:S(2)}) collective-permute-start(bf16[5,16,128,128]{3,2,1,0:T(8,128)(2,1)} %collective-permute-done.1.refs_9_), channel_id=1, source_target_pairs={{0,32},{1,225},{32,64},{33,1},{64,96},{65,33},{96,128},{97,65},{12... | collective-permute-start | bytes 7864328 | tf_op jit(solution)/shard_map/ppermute | solution.py:340
  124.7 60.3 %collective-permute-start.11 = (bf16[5,16,128,128]{3,2,1,0:T(8,128)(2,1)}, bf16[5,16,128,128]{3,2,1,0:T(8,128)(2,1)}, u32[]{:S(2)}, u32[]{:S(2)}) collective-permute-start(bf16[5,16,128,128]{3,2,1,0:T(8,128)(2,1)} %collective-permute-done.3.refs_10_), channel_id=1, source_target_pairs={{0,224},{1,33},{32,0},{33,65},{64,32},{65,97},{96,64},{97,129},{12... | collective-permute-start | bytes 7864328 | tf_op jit(solution)/shard_map/ppermute | solution.py:340
  152.3 38.9 %all-to-all-start.2 = ((bf16[32,15,16,128]{3,2,1,0:T(8,128)(2,1)}), bf16[32,15,16,128]{3,2,1,0:T(8,128)(2,1)}, u32[]{:S(2)}, u32[]{:S(2)}) async-start(bf16[32,15,16,128]{3,2,1,0:T(8,128)(2,1)} %bitcast.24), calls=%async_computation.2 | async-start | bytes 3932160 | tf_op jit(solution)/shard_map/all_to_all | solution.py:321
  160.2 45.8 %collective-permute-start.8 = (bf16[2,3,656,128]{3,2,1,0:T(8,128)(2,1)}, bf16[2,3,656,128]{3,2,1,0:T(8,128)(2,1)}, u32[]{:S(2)}, u32[]{:S(2)}) collective-permute-start(bf16[2,3,656,128]{3,2,1,0:T(8,128)(2,1)} %get-tuple-element.27), channel_id=1, source_target_pairs={{0,32},{32,64},{64,96},{96,128},{128,160},{160,192},{192,224},{224... | collective-permute-start | bytes 3022856 | tf_op jit(solution)/shard_map/ppermute | solution.py:391
  160.3 47.2 %collective-permute-start.9 = (bf16[2,3,656,128]{3,2,1,0:T(8,128)(2,1)}, bf16[2,3,656,128]{3,2,1,0:T(8,128)(2,1)}, u32[]{:S(2)}, u32[]{:S(2)}) collective-permute-start(bf16[2,3,656,128]{3,2,1,0:T(8,128)(2,1)} %get-tuple-element.28), channel_id=1, source_target_pairs={{0,224},{32,0},{64,32},{96,64},{128,96},{160,128},{192,160},{224,1... | collective-permute-start | bytes 3022856 | tf_op jit(solution)/shard_map/ppermute | solution.py:392
  191.2 22.8 %all-to-all-start.3 = ((bf16[32,6,16,128]{3,2,1,0:T(8,128)(2,1)}), bf16[32,6,16,128]{3,2,1,0:T(8,128)(2,1)S(1)}, u32[]{:S(2)}, u32[]{:S(2)}) async-start(bf16[32,6,16,128]{3,2,1,0:T(8,128)(2,1)} %bitcast.22), calls=%async_computation.3 | async-start | bytes 1572864 | tf_op jit(solution)/shard_map/all_to_all | solution.py:321
  214.0 17.6 %all-to-all-start.4 = ((bf16[32,3,16,128]{3,2,1,0:T(8,128)(2,1)}), bf16[32,3,16,128]{3,2,1,0:T(8,128)(2,1)}, u32[]{:S(2)}, u32[]{:S(2)}) async-start(bf16[32,3,16,128]{3,2,1,0:T(8,128)(2,1)} %bitcast.25), calls=%async_computation.4 | async-start | bytes 786432 | tf_op jit(solution)/shard_map/all_to_all | solution.py:321
  232.7 3.0 %collective-permute-start.12 = (bf16[4,3,16,128]{3,2,1,0:T(8,128)(2,1)S(1)}, bf16[4,3,16,128]{3,2,1,0:T(8,128)(2,1)S(1)}, u32[]{:S(2)}, u32[]{:S(2)}) collective-permute-start(bf16[4,3,16,128]{3,2,1,0:T(8,128)(2,1)S(1)} %bitcast_reduce_fusion), channel_id=1, source_target_pairs={{0,224},{8,232},{16,48},{24,56},{32,0},{40,8},{48,80},{56,88},{64,... | collective-permute-start | bytes 147464 | tf_op jit(solution)/shard_map/ppermute | solution.py:413

commit v5 on v4

--- a/solution.py
+++ b/solution.py
@@ -56,9 +56,9 @@
 
 def right_times(chosen, turned):
     wide = jnp.concatenate([chosen[w, 0] for w in range(chosen.shape[0])], axis=1)
-    total = jnp.dot(wide, turned, preferred_element_type=jnp.float32).T
+    total = jnp.dot(wide, turned, preferred_element_type=jnp.float32).astype(jnp.bfloat16).T
     width = total.shape[0]
-    return total.astype(jnp.bfloat16).reshape(M, width // M, width)
+    return total.reshape(M, width // M, width)
 
 
 def middle_kernel(near, info_ref, *refs):
@@ -157,46 +157,35 @@
             out_ref[h, :, pl.ds(to, 1)] = right_times(held[i], held_mixed[h, s])[:, None]
 
 
-def guest_kernel(
-    info_ref, low_index, high_index, low_ref, high_ref, one_ref, other_ref,
-    out_ref, held, guests, sems, guest_sems,
-):
+def guest_kernel(index_ref, low_ref, high_ref, one_ref, other_ref, out_ref, held, sems):
     half = Y // 2 * CAP
     rows = low_ref.shape[2] - TILE
-    sides = [
-        pltpu.make_async_copy(side, guests.at[pl.ds(n * (Y // 2), Y // 2)], guest_sems.at[n])
-        for n, side in enumerate((low_ref, high_ref))
-    ]
-    for side in sides:
-        side.start()
 
     def start(low_source, high_source):
         for i in range(Y * CAP):
             source = low_source if i < half else high_source
-            index = low_index if i < half else high_index
-            sector = index[i % half // CAP, i % CAP]
             pltpu.make_async_copy(
-                source.at[:, pl.ds(sector, 1)], held.at[i], sems.at[i]
+                source.at[:, pl.ds(index_ref[i], 1)], held.at[i], sems.at[i]
             ).start()
 
-    @pl.when(info_ref[Y * SLOTS + 1] == 1)
+    @pl.when(index_ref[Y * CAP] == 1)
     def _():
         start(other_ref, one_ref)
 
-    @pl.when(info_ref[Y * SLOTS + 1] != 1)
+    @pl.when(index_ref[Y * CAP] != 1)
     def _():
         start(one_ref, other_ref)
 
+    for i in range(Y * CAP):
+        pltpu.make_async_copy(one_ref.at[:, pl.ds(0, 1)], held.at[i], sems.at[i]).wait()
     for h in range(Y):
-        if h % (Y // 2) == 0:
-            sides[h // (Y // 2)].wait()
-        slots = range(h * CAP, (h + 1) * CAP)
-        for i in slots:
-            pltpu.make_async_copy(one_ref.at[:, pl.ds(0, 1)], held.at[i], sems.at[i]).wait()
-        for s, i in enumerate(slots):
-            out_ref[h, :, s] = right_times(held[i], guests[h, s, :rows])
-
-
+        guests = low_ref if h < Y // 2 else high_ref
+        for s in range(CAP):
+            mixed = guests[h % (Y // 2), s, :rows]
+            out_ref[h, :, s] = right_times(held[h * CAP + s], mixed)
+
+
+MIDDLE = pltpu.CompilerParams(vmem_limit_bytes=56 * 1024 * 1024)
 LARGE = pltpu.CompilerParams(vmem_limit_bytes=60 * 1024 * 1024)
 
 
@@ -269,27 +258,25 @@
             pltpu.SemaphoreType.DMA((Y * slots,)),
             pltpu.SemaphoreType.DMA((Y,)),
         ],
-        compiler_params=LARGE,
+        compiler_params=MIDDLE,
         cost_estimate=cost(Y * slots, 2, terms, width),
     )(info, mixed, *arrived)
 
 
-def guest_products(info, low_index, high_index, low, high, arrived):
+def guest_products(index, low, high, arrived):
     terms, _, width, _ = arrived[0].shape
     return pl.pallas_call(
         guest_kernel,
         out_shape=jax.ShapeDtypeStruct((Y, M, CAP, width // M, width), jnp.bfloat16),
-        in_specs=[pl.BlockSpec(memory_space=pltpu.SMEM)] * 3 + [IN_HBM] * 4,
+        in_specs=[pl.BlockSpec(memory_space=pltpu.SMEM), IN_VMEM, IN_VMEM] + [IN_HBM] * 2,
         out_specs=IN_VMEM,
         scratch_shapes=[
             pltpu.VMEM((Y * CAP, terms, 1, width, width), jnp.bfloat16),
-            pltpu.VMEM((Y,) + low.shape[1:], jnp.bfloat16),
             pltpu.SemaphoreType.DMA((Y * CAP,)),
-            pltpu.SemaphoreType.DMA((2,)),
         ],
-        compiler_params=LARGE,
+        compiler_params=SMALL,
         cost_estimate=cost(Y * CAP, 2, terms, width),
-    )(info, low_index, high_index, low, high, *arrived)
+    )(index, low, high, *arrived)
 
 
 def settle_kernel(place_ref, *refs):
@@ -314,6 +301,30 @@
         out_specs=IN_VMEM,
         compiler_params=SMALL,
     )(place, *parts)
+
+
+def finish_kernel(target_ref, end_ref, settled_ref, out_ref, sems):
+    del settled_ref
+    copies = [
+        pltpu.make_async_copy(end_ref.at[i], out_ref.at[target_ref[i]], sems.at[i])
+        for i in range(end_ref.shape[0])
+    ]
+    for i, copy in enumerate(copies):
+        pl.when(target_ref[i] >= 0)(copy.start)
+    for i, copy in enumerate(copies):
+        pl.when(target_ref[i] >= 0)(copy.wait)
+
+
+def finish(target, end, settled):
+    return pl.pallas_call(
+        finish_kernel,
+        out_shape=jax.ShapeDtypeStruct(settled.shape, settled.dtype),
+        in_specs=[pl.BlockSpec(memory_space=pltpu.SMEM), IN_VMEM, IN_HBM],
+        out_specs=IN_HBM,
+        scratch_shapes=[pltpu.SemaphoreType.DMA(target.shape)],
+        input_output_aliases={2: 0},
+        compiler_params=SMALL,
+    )(target, end, settled)
 
 
 def exchange(part):
@@ -392,8 +403,9 @@
     high = lax.ppermute(high, "z", [(i, (i - 1) % Z) for i in range(Z)])
     far = far_products(info, far_mixed, third)
     far, near = tie((far, exchange(near)))
-    sectors = [g[:, :, -1, 0].astype(jnp.int32) for g in (low, high)]
-    guests = guest_products(info, *sectors, low, high, third)
+    sectors = [g[:, :, -1, 0].reshape(-1).astype(jnp.int32) for g in (low, high)]
+    sectors = jnp.concatenate(sectors + [way[None].astype(jnp.int32)])
+    guests = guest_products(sectors, low, high, third)
     guests, far = tie((guests, exchange(far)))
     guests = add_up(exchange(guests))
     flat = lambda part: part.reshape((-1,) + part.shape[2:])
@@ -412,9 +424,11 @@
     ]
     end = lax.ppermute(guests, ("z", "y"), home)
 
-    end = flat(end)
-    place = jnp.where(at < first_end, end.shape[0] + index, column * CAP + at - first_end)
-    return settle(place, (end, settled))
+    hit = (at >= first_end) & (
+        column * CAP + at - first_end == jnp.arange(Y * CAP, dtype=jnp.int32)[:, None]
+    )
+    target = jnp.max(jnp.where(hit, index, -1), axis=1)
+    return finish(target, flat(end), settled)
 
 
 def solution(mesh):

time: 239 us -> 235 us (0.983)
  transfers between devices with their start and end apart: 17 -> 17, of which waited for: 9 -> 10; matrix products, arithmetic and copies ran while one was open for 6% -> 6% of each run, Pallas kernels for 16% -> 16%
where the time goes in v5:
time: 235 us; the launch traced here: 234 us
  waiting for transfers between devices  125 us (53%)
  starting transfers between devices  46.2 us (20%)
  Pallas kernels  39.5 us (17%)
  other arithmetic  11.6 us (5%)
  blocking collectives  8.18 us (3%)
  local copies, waits for them, and re-layouts  2.87 us (1%)
    ppermute x9, waiting for transfers between devices, hop(): return lax.ppermute(moved, (axis, 'c'), ring(size, direction))  106 us
    pallas_call x1, Pallas kernels, middle_products(): pl.pallas_call(functools.partial(middle_kernel, near), out_shape=[out, tu...  25.6 us
    all_to_all x3, starting transfers between devices, exchange(): lax.all_to_all(part, ('y', 'x', 'c'), split_axis=0, concat_axis=0, tiled=...  21.4 us
    ppermute x9, starting transfers between devices, hop(): return lax.ppermute(moved, (axis, 'c'), ring(size, direction))  14.9 us
    all_to_all x1, blocking collectives, on_device(): lax.all_to_all(sectors, 'y', split_axis=0, concat_axis=0, tiled=True)  8.18 us
    ppermute x1, waiting for transfers between devices, on_device(): low = lax.ppermute(low, 'z', [(i, (i + 1) % Z) for i in range(Z)])  8.06 us
    pallas_call x1, Pallas kernels, far_products(): pl.pallas_call(functools.partial(far_kernel, len(arrived)), out_shape=jax...  6.05 us
    all_to_all x3, waiting for transfers between devices, exchange(): lax.all_to_all(part, ('y', 'x', 'c'), split_axis=0, concat_axis=0, tiled=...  5.36 us
  transfers between devices with their start and end apart: 17, of which 10 were waited for; matrix products, arithmetic and copies ran while one was open for 6% of the time, Pallas kernels for 16%

profile of v5, /device:TPU:1, one launch (start us, length us, event | category | flops | bytes accessed | tf_op | source)
XLA Modules:
  0.0 233.8 jit_solution(4944668592179126256)
XLA Ops:
  0.0 6.4 %collective-permute-start = (bf16[5,16,128,128]{3,2,1,0:T(8,128)(2,1)}, bf16[5,16,128,128]{3,2,1,0:T(8,128)(2,1)}, u32[]{:S(2)}, u32[]{:S(2)}) collective-permute-start(bf16[5,16,128,128]{3,2,1,0:T(8,128)(2,1)} %refs_6_.1), channel_id=1, source_target_pairs={{0,32},{1,225},{32,64},{33,1},{64,96},{65,33},{96,128},{97,65},{12... | collective-permute-start | bytes 7864328 | tf_op jit(solution)/shard_map/ppermute | solution.py:351
  7.1 8.2 %all_to_all.29 = s32[4,1,64]{2,1,0:T(1,128)S(1)} all-to-all(s32[4,1,64]{2,1,0:T(1,128)S(1)} %broadcast_in_dim.122), channel_id=1, replica_groups=mesh['z'=8,'y'=4,'x'=4,'c'=2] {'y'}, dimensions={0} | all-to-all | bytes 2048 | tf_op jit(solution)/shard_map/all_to_all | solution.py:384
  15.3 0.8 collective-permute-start.6
  18.4 2.0 gather_fusion
  20.4 4.4 %all-to-all-start.1 = ((bf16[4,12,128,128]{3,2,1,0:T(8,128)(2,1)}), bf16[4,12,128,128]{3,2,1,0:T(8,128)(2,1)}, u32[]{:S(2)}, u32[]{:S(2)}) async-start(bf16[4,12,128,128]{3,2,1,0:T(8,128)(2,1)} %bitcast.21), calls=%async_computation.1 | async-start | bytes 3145728 | tf_op jit(solution)/shard_map/all_to_all | solution.py:393
  24.8 37.4 %collective-permute-done.refs_7_ = bf16[5,16,128,128]{3,2,1,0:T(8,128)(2,1)} collective-permute-done((bf16[5,16,128,128]{3,2,1,0:T(8,128)(2,1)}, bf16[5,16,128,128]{3,2,1,0:T(8,128)(2,1)}, u32[]{:S(2)}, u32[]{:S(2)}) %collective-permute-start) | collective-permute-done | bytes 2621472 | tf_op jit(solution)/shard_map/ppermute | solution.py:351
  62.2 3.4 %collective-permute-start.1 = (bf16[5,16,128,128]{3,2,1,0:T(8,128)(2,1)}, bf16[5,16,128,128]{3,2,1,0:T(8,128)(2,1)}, u32[]{:S(2)}, u32[]{:S(2)}) collective-permute-start(bf16[5,16,128,128]{3,2,1,0:T(8,128)(2,1)} %collective-permute-done.refs_7_), channel_id=1, source_target_pairs={{0,32},{1,225},{32,64},{33,1},{64,96},{65,33},{96,128},{97,65},{12... | collective-permute-start | bytes 7864328 | tf_op jit(solution)/shard_map/ppermute | solution.py:351
  65.6 1.3 collective-permute-start.5
  66.9 1.5 collective-permute-start.7
  68.4 2.2 collective-permute-start.4
  70.9 3.1 %collective-permute-done.4 = bf16[4,12,128,128]{3,2,1,0:T(8,128)(2,1)} collective-permute-done((bf16[4,12,128,128]{3,2,1,0:T(8,128)(2,1)}, bf16[4,12,128,128]{3,2,1,0:T(8,128)(2,1)}, u32[]{:S(2)}, u32[]{:S(2)}) %collective-permute-start.4) | collective-permute-done | bytes 1572896 | tf_op jit(solution)/shard_map/ppermute | solution.py:395
  74.0 3.7 %broadcast_select_fusion = (bf16[4,12,128,128]{3,2,1,0:T(8,128)(2,1)}, bf16[4,12,128,128]{3,2,1,0:T(8,128)(2,1)}) fusion(bf16[4,12,128,128]{3,2,1,0:T(8,128)(2,1)} %collective-permute-done.4, bf16[4,12,128,128]{3,2,1,0:T(8,128)(2,1)} %all-to-all-done.1, pred[]{:T(512)S(6)} %eq.228), kind=kLoop, calls=%fused_computation.1 | loop fusion | flops 1572864 | bytes 6291457 | tf_op jit(solution)/shard_map/jit(_where)/select_n | solution.py:396
  77.7 42.7 %collective-permute-done.1.refs_9_ = bf16[5,16,128,128]{3,2,1,0:T(8,128)(2,1)} collective-permute-done((bf16[5,16,128,128]{3,2,1,0:T(8,128)(2,1)}, bf16[5,16,128,128]{3,2,1,0:T(8,128)(2,1)}, u32[]{:S(2)}, u32[]{:S(2)}) %collective-permute-start.1) | collective-permute-done | bytes 2621472 | tf_op jit(solution)/shard_map/ppermute | solution.py:351
  120.4 4.2 %collective-permute-done.3.refs_10_ = bf16[5,16,128,128]{3,2,1,0:T(8,128)(2,1)} collective-permute-done((bf16[5,16,128,128]{3,2,1,0:T(8,128)(2,1)}, bf16[5,16,128,128]{3,2,1,0:T(8,128)(2,1)}, u32[]{:S(2)}, u32[]{:S(2)}) %collective-permute-start.3) | collective-permute-done | bytes 2621472 | tf_op jit(solution)/shard_map/ppermute | solution.py:351
  124.7 1.5 collective-permute-start.11
  127.0 25.6 %shard_map.46 = (bf16[4,8,15,16,128]{4,3,2,1,0:T(8,128)(2,1)}, bf16[4,6,640,128]{3,2,1,0:T(8,128)(2,1)}, bf16[2,3,656,128]{3,2,1,0:T(8,128)(2,1)}, bf16[2,3,656,128]{3,2,1,0:T(8,128)(2,1)}) custom-call(s32[98]{0:T(128)} %pad_add_fusion.info_ref, bf16[4,12,128,128]{3,2,1,0:T(8,128)(2,1)} %get-tuple-element.22.refs_0_, ...), custom_call_target="tpu_custom_call" | custom-call | flops 4026531840 | bytes 37748736 | tf_op jit(solution)/shard_map/pallas_call | solution.py:210
  152.6 7.5 %all-to-all-start.2 = ((bf16[32,15,16,128]{3,2,1,0:T(8,128)(2,1)}), bf16[32,15,16,128]{3,2,1,0:T(8,128)(2,1)}, u32[]{:S(2)}, u32[]{:S(2)}) async-start(bf16[32,15,16,128]{3,2,1,0:T(8,128)(2,1)} %bitcast.23), calls=%async_computation.2 | async-start | bytes 3932160 | tf_op jit(solution)/shard_map/all_to_all | solution.py:332
  160.2 2.7 %collective-permute-start.9 = (bf16[2,3,656,128]{3,2,1,0:T(8,128)(2,1)}, bf16[2,3,656,128]{3,2,1,0:T(8,128)(2,1)}, u32[]{:S(2)}, u32[]{:S(2)}) collective-permute-start(bf16[2,3,656,128]{3,2,1,0:T(8,128)(2,1)} %get-tuple-element.28), channel_id=1, source_target_pairs={{0,224},{32,0},{64,32},{96,64},{128,96},{160,128},{192,160},{224,1... | collective-permute-start | bytes 3022856 | tf_op jit(solution)/shard_map/ppermute | solution.py:403
  162.9 20.9 %collective-permute-done.10.one_ref.refs_0_ = bf16[5,16,128,128]{3,2,1,0:T(8,128)(2,1)} collective-permute-done((bf16[5,16,128,128]{3,2,1,0:T(8,128)(2,1)}, bf16[5,16,128,128]{3,2,1,0:T(8,128)(2,1)}, u32[]{:S(2)}, u32[]{:S(2)}) %collective-permute-start.10) | collective-permute-done | bytes 2621472 | tf_op jit(solution)/shard_map/ppermute | solution.py:351
  183.8 1.1 collective-permute-done.11.other_ref.refs_1_
  184.9 6.1 %shard_map.48 = bf16[4,8,6,16,128]{4,3,2,1,0:T(8,128)(2,1)} custom-call(s32[98]{0:T(128)} %pad_add_fusion.info_ref, bf16[4,6,640,128]{3,2,1,0:T(8,128)(2,1)} %get-tuple-element.29.mixed_ref, bf16[5,16,128,128]{3,2,1,0:T(8,128)(2,1)} %collective-permute-done.10.one_ref.refs_0_, bf16[5,16,128,128]{3,2,1,0:T(8,128)(2,1)} %collective-permute-done.11.other_ref.refs_1_), custom_call_target="tpu_custom_call" | custom-call | flops 1006632960 | bytes 9437184 | tf_op jit(solution)/shard_map/pallas_call | solution.py:250
  191.0 7.1 %all-to-all-start.3 = ((bf16[32,6,16,128]{3,2,1,0:T(8,128)(2,1)}), bf16[32,6,16,128]{3,2,1,0:T(8,128)(2,1)}, u32[]{:S(2)}, u32[]{:S(2)}) async-start(bf16[32,6,16,128]{3,2,1,0:T(8,128)(2,1)} %bitcast.22), calls=%async_computation.3 | async-start | bytes 1572864 | tf_op jit(solution)/shard_map/all_to_all | solution.py:332
  198.1 8.1 %collective-permute-done.8.low_ref = bf16[2,3,656,128]{3,2,1,0:T(8,128)(2,1)S(1)} collective-permute-done((bf16[2,3,656,128]{3,2,1,0:T(8,128)(2,1)}, bf16[2,3,656,128]{3,2,1,0:T(8,128)(2,1)S(1)}, u32[]{:S(2)}, u32[]{:S(2)}) %collective-permute-start.8) | collective-permute-done | bytes 1007648 | tf_op jit(solution)/shard_map/ppermute | solution.py:402
  206.4 0.9 fusion.2
  207.5 4.4 %shard_map.47 = bf16[4,8,3,16,128]{4,3,2,1,0:T(8,128)(2,1)} custom-call(s32[13]{0:T(128)S(1)} %pad_add_fusion.1.index_ref, bf16[2,3,656,128]{3,2,1,0:T(8,128)(2,1)S(1)} %collective-permute-done.8.low_ref, bf16[2,3,656,128]{3,2,1,0:T(8,128)(2,1)} %collective-permute-done.9.high_ref, bf16[5,16,128,128]{3,2,1,0:T(8,128)(2,1)} %collective-permute-done.10.one_ref.refs_0_, ...), custom_call_target="tpu_custom_call" | custom-call | flops 503316480 | bytes 4718592 | tf_op jit(solution)/shard_map/pallas_call | solution.py:268
  212.3 6.8 %all-to-all-start.4 = ((bf16[32,3,16,128]{3,2,1,0:T(8,128)(2,1)}), bf16[32,3,16,128]{3,2,1,0:T(8,128)(2,1)S(1)}, u32[]{:S(2)}, u32[]{:S(2)}) async-start(bf16[32,3,16,128]{3,2,1,0:T(8,128)(2,1)} %bitcast.10), calls=%async_computation.4 | async-start | bytes 786432 | tf_op jit(solution)/shard_map/all_to_all | solution.py:332
  219.2 1.9 reduce_sum.80
  221.0 1.2 reduce_sum.81
  222.3 2.1 shard_map.49.settled_ref
  224.4 4.9 %all-to-all-done.4 = bf16[32,3,16,128]{3,2,1,0:T(8,128)(2,1)S(1)} async-done(((bf16[32,3,16,128]{3,2,1,0:T(8,128)(2,1)}), bf16[32,3,16,128]{3,2,1,0:T(8,128)(2,1)S(1)}, u32[]{:S(2)}, u32[]{:S(2)}) %all-to-all-start.4) | async-done | bytes 393248 | tf_op jit(solution)/shard_map/all_to_all | solution.py:332
  230.1 2.3 collective-permute-done.12
  232.4 1.3 shard_map.50
  (38 shorter events, 5.9 us)
Async XLA Ops:
  0.0 18.4 %copy-start = (bf16[64,128,128]{2,1,0:T(8,128)(2,1)S(1)}, bf16[64,128,128]{2,1,0:T(8,128)(2,1)}, u32[]{:S(2)}) copy-start(bf16[64,128,128]{2,1,0:T(8,128)(2,1)} %param.4) | copy-start | bytes 6291460
  0.0 62.2 %collective-permute-start = (bf16[5,16,128,128]{3,2,1,0:T(8,128)(2,1)}, bf16[5,16,128,128]{3,2,1,0:T(8,128)(2,1)}, u32[]{:S(2)}, u32[]{:S(2)}) collective-permute-start(bf16[5,16,128,128]{3,2,1,0:T(8,128)(2,1)} %refs_6_.1), channel_id=1, source_target_pairs={{0,32},{1,225},{32,64},{33,1},{64,96},{65,33},{96,128},{97,65},{12... | collective-permute-start | bytes 7864328 | tf_op jit(solution)/shard_map/ppermute | solution.py:351
  6.4 59.2 %collective-permute-start.2 = (bf16[5,16,128,128]{3,2,1,0:T(8,128)(2,1)}, bf16[5,16,128,128]{3,2,1,0:T(8,128)(2,1)}, u32[]{:S(2)}, u32[]{:S(2)}) collective-permute-start(bf16[5,16,128,128]{3,2,1,0:T(8,128)(2,1)} %refs_6_.1), channel_id=1, source_target_pairs={{0,224},{1,33},{32,0},{33,65},{64,32},{65,97},{96,64},{97,129},{12... | collective-permute-start | bytes 7864328 | tf_op jit(solution)/shard_map/ppermute | solution.py:351
  15.3 51.6 %collective-permute-start.6 = (bf16[5,16,128,128]{3,2,1,0:T(8,128)(2,1)}, bf16[5,16,128,128]{3,2,1,0:T(8,128)(2,1)}, u32[]{:S(2)}, u32[]{:S(2)}) collective-permute-start(bf16[5,16,128,128]{3,2,1,0:T(8,128)(2,1)} %refs_2_), channel_id=1, source_target_pairs={{0,8},{1,25},{8,16},{9,1},{16,24},{17,9},{24,0},{25,17},{2,10},{3,... | collective-permute-start | bytes 7864328 | tf_op jit(solution)/shard_map/ppermute | solution.py:351
  20.4 48.0 %all-to-all-start.1 = ((bf16[4,12,128,128]{3,2,1,0:T(8,128)(2,1)}), bf16[4,12,128,128]{3,2,1,0:T(8,128)(2,1)}, u32[]{:S(2)}, u32[]{:S(2)}) async-start(bf16[4,12,128,128]{3,2,1,0:T(8,128)(2,1)} %bitcast.21), calls=%async_computation.1 | async-start | bytes 3145728 | tf_op jit(solution)/shard_map/all_to_all | solution.py:393
  62.2 58.2 %collective-permute-start.1 = (bf16[5,16,128,128]{3,2,1,0:T(8,128)(2,1)}, bf16[5,16,128,128]{3,2,1,0:T(8,128)(2,1)}, u32[]{:S(2)}, u32[]{:S(2)}) collective-permute-start(bf16[5,16,128,128]{3,2,1,0:T(8,128)(2,1)} %collective-permute-done.refs_7_), channel_id=1, source_target_pairs={{0,32},{1,225},{32,64},{33,1},{64,96},{65,33},{96,128},{97,65},{12... | collective-permute-start | bytes 7864328 | tf_op jit(solution)/shard_map/ppermute | solution.py:351
  65.6 59.1 %collective-permute-start.3 = (bf16[5,16,128,128]{3,2,1,0:T(8,128)(2,1)}, bf16[5,16,128,128]{3,2,1,0:T(8,128)(2,1)}, u32[]{:S(2)}, u32[]{:S(2)}) collective-permute-start(bf16[5,16,128,128]{3,2,1,0:T(8,128)(2,1)} %collective-permute-done.2.refs_8_), channel_id=1, source_target_pairs={{0,224},{1,33},{32,0},{33,65},{64,32},{65,97},{96,64},{97,129},{12... | collective-permute-start | bytes 7864328 | tf_op jit(solution)/shard_map/ppermute | solution.py:351
  65.6 61.4 %collective-permute-start.5 = (bf16[5,16,128,128]{3,2,1,0:T(8,128)(2,1)}, bf16[5,16,128,128]{3,2,1,0:T(8,128)(2,1)}, u32[]{:S(2)}, u32[]{:S(2)}) collective-permute-start(bf16[5,16,128,128]{3,2,1,0:T(8,128)(2,1)} %refs_2_), channel_id=1, source_target_pairs={{0,24},{1,9},{8,0},{9,17},{16,8},{17,25},{24,16},{25,1},{2,26},{3,... | collective-permute-start | bytes 7864328 | tf_op jit(solution)/shard_map/ppermute | solution.py:351
  66.9 60.1 %collective-permute-start.7 = (bf16[5,16,128,128]{3,2,1,0:T(8,128)(2,1)}, bf16[5,16,128,128]{3,2,1,0:T(8,128)(2,1)}, u32[]{:S(2)}, u32[]{:S(2)}) collective-permute-start(bf16[5,16,128,128]{3,2,1,0:T(8,128)(2,1)} %collective-permute-done.6.refs_5_), channel_id=1, source_target_pairs={{0,8},{1,25},{8,16},{9,1},{16,24},{17,9},{24,0},{25,17},{2,10},{3,... | collective-permute-start | bytes 7864328 | tf_op jit(solution)/shard_map/ppermute | solution.py:351
  68.4 5.6 %collective-permute-start.4 = (bf16[4,12,128,128]{3,2,1,0:T(8,128)(2,1)}, bf16[4,12,128,128]{3,2,1,0:T(8,128)(2,1)}, u32[]{:S(2)}, u32[]{:S(2)}) collective-permute-start(bf16[4,12,128,128]{3,2,1,0:T(8,128)(2,1)} %all-to-all-done.1), channel_id=1, source_target_pairs={{0,1},{1,0},{2,3},{3,2},{4,5},{5,4},{6,7},{7,6},{8,9},{9,8},{10,11... | collective-permute-start | bytes 4718600 | tf_op jit(solution)/shard_map/ppermute | solution.py:395
  124.7 59.1 %collective-permute-start.10 = (bf16[5,16,128,128]{3,2,1,0:T(8,128)(2,1)}, bf16[5,16,128,128]{3,2,1,0:T(8,128)(2,1)}, u32[]{:S(2)}, u32[]{:S(2)}) collective-permute-start(bf16[5,16,128,128]{3,2,1,0:T(8,128)(2,1)} %collective-permute-done.1.refs_9_), channel_id=1, source_target_pairs={{0,32},{1,225},{32,64},{33,1},{64,96},{65,33},{96,128},{97,65},{12... | collective-permute-start | bytes 7864328 | tf_op jit(solution)/shard_map/ppermute | solution.py:351
  124.7 60.2 %collective-permute-start.11 = (bf16[5,16,128,128]{3,2,1,0:T(8,128)(2,1)}, bf16[5,16,128,128]{3,2,1,0:T(8,128)(2,1)}, u32[]{:S(2)}, u32[]{:S(2)}) collective-permute-start(bf16[5,16,128,128]{3,2,1,0:T(8,128)(2,1)} %collective-permute-done.3.refs_10_), channel_id=1, source_target_pairs={{0,224},{1,33},{32,0},{33,65},{64,32},{65,97},{96,64},{97,129},{12... | collective-permute-start | bytes 7864328 | tf_op jit(solution)/shard_map/ppermute | solution.py:351
  152.6 38.4 %all-to-all-start.2 = ((bf16[32,15,16,128]{3,2,1,0:T(8,128)(2,1)}), bf16[32,15,16,128]{3,2,1,0:T(8,128)(2,1)}, u32[]{:S(2)}, u32[]{:S(2)}) async-start(bf16[32,15,16,128]{3,2,1,0:T(8,128)(2,1)} %bitcast.23), calls=%async_computation.2 | async-start | bytes 3932160 | tf_op jit(solution)/shard_map/all_to_all | solution.py:332
  160.1 46.0 %collective-permute-start.8 = (bf16[2,3,656,128]{3,2,1,0:T(8,128)(2,1)}, bf16[2,3,656,128]{3,2,1,0:T(8,128)(2,1)S(1)}, u32[]{:S(2)}, u32[]{:S(2)}) collective-permute-start(bf16[2,3,656,128]{3,2,1,0:T(8,128)(2,1)} %get-tuple-element.27), channel_id=1, source_target_pairs={{0,32},{32,64},{64,96},{96,128},{128,160},{160,192},{192,224},{224... | collective-permute-start | bytes 3022856 | tf_op jit(solution)/shard_map/ppermute | solution.py:402
  160.2 46.2 %collective-permute-start.9 = (bf16[2,3,656,128]{3,2,1,0:T(8,128)(2,1)}, bf16[2,3,656,128]{3,2,1,0:T(8,128)(2,1)}, u32[]{:S(2)}, u32[]{:S(2)}) collective-permute-start(bf16[2,3,656,128]{3,2,1,0:T(8,128)(2,1)} %get-tuple-element.28), channel_id=1, source_target_pairs={{0,224},{32,0},{64,32},{96,64},{128,96},{160,128},{192,160},{224,1... | collective-permute-start | bytes 3022856 | tf_op jit(solution)/shard_map/ppermute | solution.py:403
  191.0 21.4 %all-to-all-start.3 = ((bf16[32,6,16,128]{3,2,1,0:T(8,128)(2,1)}), bf16[32,6,16,128]{3,2,1,0:T(8,128)(2,1)}, u32[]{:S(2)}, u32[]{:S(2)}) async-start(bf16[32,6,16,128]{3,2,1,0:T(8,128)(2,1)} %bitcast.22), calls=%async_computation.3 | async-start | bytes 1572864 | tf_op jit(solution)/shard_map/all_to_all | solution.py:332
  212.3 17.0 %all-to-all-start.4 = ((bf16[32,3,16,128]{3,2,1,0:T(8,128)(2,1)}), bf16[32,3,16,128]{3,2,1,0:T(8,128)(2,1)S(1)}, u32[]{:S(2)}, u32[]{:S(2)}) async-start(bf16[32,3,16,128]{3,2,1,0:T(8,128)(2,1)} %bitcast.10), calls=%async_computation.4 | async-start | bytes 786432 | tf_op jit(solution)/shard_map/all_to_all | solution.py:332
  229.4 3.0 %collective-permute-start.12 = (bf16[4,3,16,128]{3,2,1,0:T(8,128)(2,1)S(1)}, bf16[4,3,16,128]{3,2,1,0:T(8,128)(2,1)S(1)}, u32[]{:S(2)}, u32[]{:S(2)}) collective-permute-start(bf16[4,3,16,128]{3,2,1,0:T(8,128)(2,1)S(1)} %bitcast_reduce_fusion), channel_id=1, source_target_pairs={{0,224},{8,232},{16,48},{24,56},{32,0},{40,8},{48,80},{56,88},{64,... | collective-permute-start | bytes 147464 | tf_op jit(solution)/shard_map/ppermute | solution.py:425

commit v6 on v5

--- a/solution.py
+++ b/solution.py
@@ -157,32 +157,23 @@
             out_ref[h, :, pl.ds(to, 1)] = right_times(held[i], held_mixed[h, s])[:, None]
 
 
-def guest_kernel(index_ref, low_ref, high_ref, one_ref, other_ref, out_ref, held, sems):
-    half = Y // 2 * CAP
+def guest_kernel(index_ref, low_ref, high_ref, one_ref, other_ref, out_ref):
     rows = low_ref.shape[2] - TILE
 
-    def start(low_source, high_source):
-        for i in range(Y * CAP):
-            source = low_source if i < half else high_source
-            pltpu.make_async_copy(
-                source.at[:, pl.ds(index_ref[i], 1)], held.at[i], sems.at[i]
-            ).start()
+    def products(low_source, high_source):
+        for h in range(Y):
+            guests, source = (low_ref, low_source) if h < Y // 2 else (high_ref, high_source)
+            for s in range(CAP):
+                chosen = source[:, pl.ds(index_ref[h * CAP + s], 1)]
+                out_ref[h, :, s] = right_times(chosen, guests[h % (Y // 2), s, :rows])
 
     @pl.when(index_ref[Y * CAP] == 1)
     def _():
-        start(other_ref, one_ref)
+        products(other_ref, one_ref)
 
     @pl.when(index_ref[Y * CAP] != 1)
     def _():
-        start(one_ref, other_ref)
-
-    for i in range(Y * CAP):
-        pltpu.make_async_copy(one_ref.at[:, pl.ds(0, 1)], held.at[i], sems.at[i]).wait()
-    for h in range(Y):
-        guests = low_ref if h < Y // 2 else high_ref
-        for s in range(CAP):
-            mixed = guests[h % (Y // 2), s, :rows]
-            out_ref[h, :, s] = right_times(held[h * CAP + s], mixed)
+        products(one_ref, other_ref)
 
 
 MIDDLE = pltpu.CompilerParams(vmem_limit_bytes=56 * 1024 * 1024)
@@ -268,12 +259,8 @@
     return pl.pallas_call(
         guest_kernel,
         out_shape=jax.ShapeDtypeStruct((Y, M, CAP, width // M, width), jnp.bfloat16),
-        in_specs=[pl.BlockSpec(memory_space=pltpu.SMEM), IN_VMEM, IN_VMEM] + [IN_HBM] * 2,
+        in_specs=[pl.BlockSpec(memory_space=pltpu.SMEM)] + [IN_VMEM] * 4,
         out_specs=IN_VMEM,
-        scratch_shapes=[
-            pltpu.VMEM((Y * CAP, terms, 1, width, width), jnp.bfloat16),
-            pltpu.SemaphoreType.DMA((Y * CAP,)),
-        ],
         compiler_params=SMALL,
         cost_estimate=cost(Y * CAP, 2, terms, width),
     )(index, low, high, *arrived)
@@ -306,7 +293,9 @@
 def finish_kernel(target_ref, end_ref, settled_ref, out_ref, sems):
     del settled_ref
     copies = [
-        pltpu.make_async_copy(end_ref.at[i], out_ref.at[target_ref[i]], sems.at[i])
+        pltpu.make_async_copy(
+            end_ref.at[i], out_ref.at[jnp.maximum(target_ref[i], 0)], sems.at[i]
+        )
         for i in range(end_ref.shape[0])
     ]
     for i, copy in enumerate(copies):

time: 235 us -> 234 us (level)
  no operation moved by 1% of the time
where the time goes in v6:
time: 234 us
  waiting for transfers between devices  125 us (53%)
  starting transfers between devices  46.5 us (20%)
  Pallas kernels  39.1 us (17%)
  other arithmetic  11.6 us (5%)
  blocking collectives  8.18 us (3%)
  local copies, waits for them, and re-layouts  2.87 us (1%)
    ppermute x9, waiting for transfers between devices, hop(): return lax.ppermute(moved, (axis, 'c'), ring(size, direction))  106 us
    pallas_call x1, Pallas kernels, middle_products(): pl.pallas_call(functools.partial(middle_kernel, near), out_shape=[out, tu...  25.3 us
    all_to_all x3, starting transfers between devices, exchange(): lax.all_to_all(part, ('y', 'x', 'c'), split_axis=0, concat_axis=0, tiled=...  21.5 us
    ppermute x9, starting transfers between devices, hop(): return lax.ppermute(moved, (axis, 'c'), ring(size, direction))  14.9 us
    all_to_all x1, blocking collectives, on_device(): lax.all_to_all(sectors, 'y', split_axis=0, concat_axis=0, tiled=True)  8.18 us
    ppermute x1, waiting for transfers between devices, on_device(): low = lax.ppermute(low, 'z', [(i, (i + 1) % Z) for i in range(Z)])  8.06 us
    pallas_call x1, Pallas kernels, far_products(): pl.pallas_call(functools.partial(far_kernel, len(arrived)), out_shape=jax...  6.07 us
    all_to_all x3, waiting for transfers between devices, exchange(): lax.all_to_all(part, ('y', 'x', 'c'), split_axis=0, concat_axis=0, tiled=...  5.44 us
  transfers between devices with their start and end apart: 17, of which 10 were waited for; matrix products, arithmetic and copies ran while one was open for 6% of the time, Pallas kernels for 16%

profile of v6, /device:TPU:1, one launch (start us, length us, event | category | flops | bytes accessed | tf_op | source)
XLA Modules:
  0.0 233.7 jit_solution(16543339732002044812)
XLA Ops:
  0.0 6.4 %collective-permute-start = (bf16[5,16,128,128]{3,2,1,0:T(8,128)(2,1)}, bf16[5,16,128,128]{3,2,1,0:T(8,128)(2,1)}, u32[]{:S(2)}, u32[]{:S(2)}) collective-permute-start(bf16[5,16,128,128]{3,2,1,0:T(8,128)(2,1)} %refs_6_.1), channel_id=1, source_target_pairs={{0,32},{1,225},{32,64},{33,1},{64,96},{65,33},{96,128},{97,65},{12... | collective-permute-start | bytes 7864328 | tf_op jit(solution)/shard_map/ppermute | solution.py:340
  7.1 8.2 %all_to_all.29 = s32[4,1,64]{2,1,0:T(1,128)S(1)} all-to-all(s32[4,1,64]{2,1,0:T(1,128)S(1)} %broadcast_in_dim.122), channel_id=1, replica_groups=mesh['z'=8,'y'=4,'x'=4,'c'=2] {'y'}, dimensions={0} | all-to-all | bytes 2048 | tf_op jit(solution)/shard_map/all_to_all | solution.py:373
  15.3 0.8 collective-permute-start.6
  18.4 2.0 gather_fusion
  20.4 4.4 %all-to-all-start.1 = ((bf16[4,12,128,128]{3,2,1,0:T(8,128)(2,1)}), bf16[4,12,128,128]{3,2,1,0:T(8,128)(2,1)}, u32[]{:S(2)}, u32[]{:S(2)}) async-start(bf16[4,12,128,128]{3,2,1,0:T(8,128)(2,1)} %bitcast.21), calls=%async_computation.1 | async-start | bytes 3145728 | tf_op jit(solution)/shard_map/all_to_all | solution.py:382
  24.8 37.4 %collective-permute-done.refs_7_ = bf16[5,16,128,128]{3,2,1,0:T(8,128)(2,1)} collective-permute-done((bf16[5,16,128,128]{3,2,1,0:T(8,128)(2,1)}, bf16[5,16,128,128]{3,2,1,0:T(8,128)(2,1)}, u32[]{:S(2)}, u32[]{:S(2)}) %collective-permute-start) | collective-permute-done | bytes 2621472 | tf_op jit(solution)/shard_map/ppermute | solution.py:340
  62.2 3.4 %collective-permute-start.1 = (bf16[5,16,128,128]{3,2,1,0:T(8,128)(2,1)}, bf16[5,16,128,128]{3,2,1,0:T(8,128)(2,1)}, u32[]{:S(2)}, u32[]{:S(2)}) collective-permute-start(bf16[5,16,128,128]{3,2,1,0:T(8,128)(2,1)} %collective-permute-done.refs_7_), channel_id=1, source_target_pairs={{0,32},{1,225},{32,64},{33,1},{64,96},{65,33},{96,128},{97,65},{12... | collective-permute-start | bytes 7864328 | tf_op jit(solution)/shard_map/ppermute | solution.py:340
  65.6 1.3 collective-permute-start.5
  66.9 1.5 collective-permute-start.7
  68.4 2.2 collective-permute-start.4
  70.9 3.1 %collective-permute-done.4 = bf16[4,12,128,128]{3,2,1,0:T(8,128)(2,1)} collective-permute-done((bf16[4,12,128,128]{3,2,1,0:T(8,128)(2,1)}, bf16[4,12,128,128]{3,2,1,0:T(8,128)(2,1)}, u32[]{:S(2)}, u32[]{:S(2)}) %collective-permute-start.4) | collective-permute-done | bytes 1572896 | tf_op jit(solution)/shard_map/ppermute | solution.py:384
  74.0 3.7 %broadcast_select_fusion = (bf16[4,12,128,128]{3,2,1,0:T(8,128)(2,1)}, bf16[4,12,128,128]{3,2,1,0:T(8,128)(2,1)}) fusion(bf16[4,12,128,128]{3,2,1,0:T(8,128)(2,1)} %collective-permute-done.4, bf16[4,12,128,128]{3,2,1,0:T(8,128)(2,1)} %all-to-all-done.1, pred[]{:T(512)S(6)} %eq.228), kind=kLoop, calls=%fused_computation.1 | loop fusion | flops 1572864 | bytes 6291457 | tf_op jit(solution)/shard_map/jit(_where)/select_n | solution.py:385
  77.7 42.7 %collective-permute-done.1.refs_9_ = bf16[5,16,128,128]{3,2,1,0:T(8,128)(2,1)} collective-permute-done((bf16[5,16,128,128]{3,2,1,0:T(8,128)(2,1)}, bf16[5,16,128,128]{3,2,1,0:T(8,128)(2,1)}, u32[]{:S(2)}, u32[]{:S(2)}) %collective-permute-start.1) | collective-permute-done | bytes 2621472 | tf_op jit(solution)/shard_map/ppermute | solution.py:340
  120.4 4.2 %collective-permute-done.3.refs_10_ = bf16[5,16,128,128]{3,2,1,0:T(8,128)(2,1)} collective-permute-done((bf16[5,16,128,128]{3,2,1,0:T(8,128)(2,1)}, bf16[5,16,128,128]{3,2,1,0:T(8,128)(2,1)}, u32[]{:S(2)}, u32[]{:S(2)}) %collective-permute-start.3) | collective-permute-done | bytes 2621472 | tf_op jit(solution)/shard_map/ppermute | solution.py:340
  124.7 1.5 collective-permute-start.11
  127.0 25.3 %shard_map.46 = (bf16[4,8,15,16,128]{4,3,2,1,0:T(8,128)(2,1)}, bf16[4,6,640,128]{3,2,1,0:T(8,128)(2,1)}, bf16[2,3,656,128]{3,2,1,0:T(8,128)(2,1)}, bf16[2,3,656,128]{3,2,1,0:T(8,128)(2,1)}) custom-call(s32[98]{0:T(128)} %pad_add_fusion.info_ref, bf16[4,12,128,128]{3,2,1,0:T(8,128)(2,1)} %get-tuple-element.22.refs_0_, ...), custom_call_target="tpu_custom_call" | custom-call | flops 4026531840 | bytes 37748736 | tf_op jit(solution)/shard_map/pallas_call | solution.py:201
  152.3 7.8 %all-to-all-start.2 = ((bf16[32,15,16,128]{3,2,1,0:T(8,128)(2,1)}), bf16[32,15,16,128]{3,2,1,0:T(8,128)(2,1)}, u32[]{:S(2)}, u32[]{:S(2)}) async-start(bf16[32,15,16,128]{3,2,1,0:T(8,128)(2,1)} %bitcast.23), calls=%async_computation.2 | async-start | bytes 3932160 | tf_op jit(solution)/shard_map/all_to_all | solution.py:321
  160.2 2.7 %collective-permute-start.9 = (bf16[2,3,656,128]{3,2,1,0:T(8,128)(2,1)}, bf16[2,3,656,128]{3,2,1,0:T(8,128)(2,1)}, u32[]{:S(2)}, u32[]{:S(2)}) collective-permute-start(bf16[2,3,656,128]{3,2,1,0:T(8,128)(2,1)} %get-tuple-element.28), channel_id=1, source_target_pairs={{0,224},{32,0},{64,32},{96,64},{128,96},{160,128},{192,160},{224,1... | collective-permute-start | bytes 3022856 | tf_op jit(solution)/shard_map/ppermute | solution.py:392
  162.8 21.0 %collective-permute-done.10.one_ref.refs_0_ = bf16[5,16,128,128]{3,2,1,0:T(8,128)(2,1)} collective-permute-done((bf16[5,16,128,128]{3,2,1,0:T(8,128)(2,1)}, bf16[5,16,128,128]{3,2,1,0:T(8,128)(2,1)}, u32[]{:S(2)}, u32[]{:S(2)}) %collective-permute-start.10) | collective-permute-done | bytes 2621472 | tf_op jit(solution)/shard_map/ppermute | solution.py:340
  183.8 1.1 collective-permute-done.11.other_ref.refs_1_
  184.9 6.1 %shard_map.48 = bf16[4,8,6,16,128]{4,3,2,1,0:T(8,128)(2,1)} custom-call(s32[98]{0:T(128)} %pad_add_fusion.info_ref, bf16[4,6,640,128]{3,2,1,0:T(8,128)(2,1)} %get-tuple-element.29.mixed_ref, bf16[5,16,128,128]{3,2,1,0:T(8,128)(2,1)} %collective-permute-done.10.one_ref.refs_0_, bf16[5,16,128,128]{3,2,1,0:T(8,128)(2,1)} %collective-permute-done.11.other_ref.refs_1_), custom_call_target="tpu_custom_call" | custom-call | flops 1006632960 | bytes 9437184 | tf_op jit(solution)/shard_map/pallas_call | solution.py:241
  191.0 7.1 %all-to-all-start.3 = ((bf16[32,6,16,128]{3,2,1,0:T(8,128)(2,1)}), bf16[32,6,16,128]{3,2,1,0:T(8,128)(2,1)}, u32[]{:S(2)}, u32[]{:S(2)}) async-start(bf16[32,6,16,128]{3,2,1,0:T(8,128)(2,1)} %bitcast.22), calls=%async_computation.3 | async-start | bytes 1572864 | tf_op jit(solution)/shard_map/all_to_all | solution.py:321
  198.1 8.1 %collective-permute-done.8.low_ref = bf16[2,3,656,128]{3,2,1,0:T(8,128)(2,1)S(1)} collective-permute-done((bf16[2,3,656,128]{3,2,1,0:T(8,128)(2,1)}, bf16[2,3,656,128]{3,2,1,0:T(8,128)(2,1)S(1)}, u32[]{:S(2)}, u32[]{:S(2)}) %collective-permute-start.8) | collective-permute-done | bytes 1007648 | tf_op jit(solution)/shard_map/ppermute | solution.py:391
  206.4 0.9 fusion.2
  207.5 4.4 %shard_map.47 = bf16[4,8,3,16,128]{4,3,2,1,0:T(8,128)(2,1)} custom-call(s32[13]{0:T(128)S(1)} %pad_add_fusion.1.index_ref, bf16[2,3,656,128]{3,2,1,0:T(8,128)(2,1)S(1)} %collective-permute-done.8.low_ref, bf16[2,3,656,128]{3,2,1,0:T(8,128)(2,1)} %collective-permute-done.9.high_ref, bf16[5,16,128,128]{3,2,1,0:T(8,128)(2,1)} %collective-permute-done.10.one_ref.refs_0_, ...), custom_call_target="tpu_custom_call" | custom-call | flops 503316480 | bytes 4718592 | tf_op jit(solution)/shard_map/pallas_call | solution.py:259
  212.3 6.7 %all-to-all-start.4 = ((bf16[32,3,16,128]{3,2,1,0:T(8,128)(2,1)}), bf16[32,3,16,128]{3,2,1,0:T(8,128)(2,1)S(1)}, u32[]{:S(2)}, u32[]{:S(2)}) async-start(bf16[32,3,16,128]{3,2,1,0:T(8,128)(2,1)} %bitcast.10), calls=%async_computation.4 | async-start | bytes 786432 | tf_op jit(solution)/shard_map/all_to_all | solution.py:321
  219.0 1.9 reduce_sum.80
  220.9 1.2 reduce_sum.81
  222.2 2.1 shard_map.49.settled_ref
  224.3 4.9 %all-to-all-done.4 = bf16[32,3,16,128]{3,2,1,0:T(8,128)(2,1)S(1)} async-done(((bf16[32,3,16,128]{3,2,1,0:T(8,128)(2,1)}), bf16[32,3,16,128]{3,2,1,0:T(8,128)(2,1)S(1)}, u32[]{:S(2)}, u32[]{:S(2)}) %all-to-all-start.4) | async-done | bytes 393248 | tf_op jit(solution)/shard_map/all_to_all | solution.py:321
  230.1 2.2 collective-permute-done.12
  232.3 1.3 shard_map.50
  (38 shorter events, 6.1 us)
Async XLA Ops:
  0.0 18.4 %copy-start = (bf16[64,128,128]{2,1,0:T(8,128)(2,1)S(1)}, bf16[64,128,128]{2,1,0:T(8,128)(2,1)}, u32[]{:S(2)}) copy-start(bf16[64,128,128]{2,1,0:T(8,128)(2,1)} %param.4) | copy-start | bytes 6291460
  0.0 62.2 %collective-permute-start = (bf16[5,16,128,128]{3,2,1,0:T(8,128)(2,1)}, bf16[5,16,128,128]{3,2,1,0:T(8,128)(2,1)}, u32[]{:S(2)}, u32[]{:S(2)}) collective-permute-start(bf16[5,16,128,128]{3,2,1,0:T(8,128)(2,1)} %refs_6_.1), channel_id=1, source_target_pairs={{0,32},{1,225},{32,64},{33,1},{64,96},{65,33},{96,128},{97,65},{12... | collective-permute-start | bytes 7864328 | tf_op jit(solution)/shard_map/ppermute | solution.py:340
  6.4 59.2 %collective-permute-start.2 = (bf16[5,16,128,128]{3,2,1,0:T(8,128)(2,1)}, bf16[5,16,128,128]{3,2,1,0:T(8,128)(2,1)}, u32[]{:S(2)}, u32[]{:S(2)}) collective-permute-start(bf16[5,16,128,128]{3,2,1,0:T(8,128)(2,1)} %refs_6_.1), channel_id=1, source_target_pairs={{0,224},{1,33},{32,0},{33,65},{64,32},{65,97},{96,64},{97,129},{12... | collective-permute-start | bytes 7864328 | tf_op jit(solution)/shard_map/ppermute | solution.py:340
  15.3 51.6 %collective-permute-start.6 = (bf16[5,16,128,128]{3,2,1,0:T(8,128)(2,1)}, bf16[5,16,128,128]{3,2,1,0:T(8,128)(2,1)}, u32[]{:S(2)}, u32[]{:S(2)}) collective-permute-start(bf16[5,16,128,128]{3,2,1,0:T(8,128)(2,1)} %refs_2_), channel_id=1, source_target_pairs={{0,8},{1,25},{8,16},{9,1},{16,24},{17,9},{24,0},{25,17},{2,10},{3,... | collective-permute-start | bytes 7864328 | tf_op jit(solution)/shard_map/ppermute | solution.py:340
  20.4 48.0 %all-to-all-start.1 = ((bf16[4,12,128,128]{3,2,1,0:T(8,128)(2,1)}), bf16[4,12,128,128]{3,2,1,0:T(8,128)(2,1)}, u32[]{:S(2)}, u32[]{:S(2)}) async-start(bf16[4,12,128,128]{3,2,1,0:T(8,128)(2,1)} %bitcast.21), calls=%async_computation.1 | async-start | bytes 3145728 | tf_op jit(solution)/shard_map/all_to_all | solution.py:382
  62.2 58.2 %collective-permute-start.1 = (bf16[5,16,128,128]{3,2,1,0:T(8,128)(2,1)}, bf16[5,16,128,128]{3,2,1,0:T(8,128)(2,1)}, u32[]{:S(2)}, u32[]{:S(2)}) collective-permute-start(bf16[5,16,128,128]{3,2,1,0:T(8,128)(2,1)} %collective-permute-done.refs_7_), channel_id=1, source_target_pairs={{0,32},{1,225},{32,64},{33,1},{64,96},{65,33},{96,128},{97,65},{12... | collective-permute-start | bytes 7864328 | tf_op jit(solution)/shard_map/ppermute | solution.py:340
  65.6 59.1 %collective-permute-start.3 = (bf16[5,16,128,128]{3,2,1,0:T(8,128)(2,1)}, bf16[5,16,128,128]{3,2,1,0:T(8,128)(2,1)}, u32[]{:S(2)}, u32[]{:S(2)}) collective-permute-start(bf16[5,16,128,128]{3,2,1,0:T(8,128)(2,1)} %collective-permute-done.2.refs_8_), channel_id=1, source_target_pairs={{0,224},{1,33},{32,0},{33,65},{64,32},{65,97},{96,64},{97,129},{12... | collective-permute-start | bytes 7864328 | tf_op jit(solution)/shard_map/ppermute | solution.py:340
  65.6 61.4 %collective-permute-start.5 = (bf16[5,16,128,128]{3,2,1,0:T(8,128)(2,1)}, bf16[5,16,128,128]{3,2,1,0:T(8,128)(2,1)}, u32[]{:S(2)}, u32[]{:S(2)}) collective-permute-start(bf16[5,16,128,128]{3,2,1,0:T(8,128)(2,1)} %refs_2_), channel_id=1, source_target_pairs={{0,24},{1,9},{8,0},{9,17},{16,8},{17,25},{24,16},{25,1},{2,26},{3,... | collective-permute-start | bytes 7864328 | tf_op jit(solution)/shard_map/ppermute | solution.py:340
  66.9 60.1 %collective-permute-start.7 = (bf16[5,16,128,128]{3,2,1,0:T(8,128)(2,1)}, bf16[5,16,128,128]{3,2,1,0:T(8,128)(2,1)}, u32[]{:S(2)}, u32[]{:S(2)}) collective-permute-start(bf16[5,16,128,128]{3,2,1,0:T(8,128)(2,1)} %collective-permute-done.6.refs_5_), channel_id=1, source_target_pairs={{0,8},{1,25},{8,16},{9,1},{16,24},{17,9},{24,0},{25,17},{2,10},{3,... | collective-permute-start | bytes 7864328 | tf_op jit(solution)/shard_map/ppermute | solution.py:340
  68.4 5.6 %collective-permute-start.4 = (bf16[4,12,128,128]{3,2,1,0:T(8,128)(2,1)}, bf16[4,12,128,128]{3,2,1,0:T(8,128)(2,1)}, u32[]{:S(2)}, u32[]{:S(2)}) collective-permute-start(bf16[4,12,128,128]{3,2,1,0:T(8,128)(2,1)} %all-to-all-done.1), channel_id=1, source_target_pairs={{0,1},{1,0},{2,3},{3,2},{4,5},{5,4},{6,7},{7,6},{8,9},{9,8},{10,11... | collective-permute-start | bytes 4718600 | tf_op jit(solution)/shard_map/ppermute | solution.py:384
  124.7 59.1 %collective-permute-start.10 = (bf16[5,16,128,128]{3,2,1,0:T(8,128)(2,1)}, bf16[5,16,128,128]{3,2,1,0:T(8,128)(2,1)}, u32[]{:S(2)}, u32[]{:S(2)}) collective-permute-start(bf16[5,16,128,128]{3,2,1,0:T(8,128)(2,1)} %collective-permute-done.1.refs_9_), channel_id=1, source_target_pairs={{0,32},{1,225},{32,64},{33,1},{64,96},{65,33},{96,128},{97,65},{12... | collective-permute-start | bytes 7864328 | tf_op jit(solution)/shard_map/ppermute | solution.py:340
  124.7 60.2 %collective-permute-start.11 = (bf16[5,16,128,128]{3,2,1,0:T(8,128)(2,1)}, bf16[5,16,128,128]{3,2,1,0:T(8,128)(2,1)}, u32[]{:S(2)}, u32[]{:S(2)}) collective-permute-start(bf16[5,16,128,128]{3,2,1,0:T(8,128)(2,1)} %collective-permute-done.3.refs_10_), channel_id=1, source_target_pairs={{0,224},{1,33},{32,0},{33,65},{64,32},{65,97},{96,64},{97,129},{12... | collective-permute-start | bytes 7864328 | tf_op jit(solution)/shard_map/ppermute | solution.py:340
  152.3 38.7 %all-to-all-start.2 = ((bf16[32,15,16,128]{3,2,1,0:T(8,128)(2,1)}), bf16[32,15,16,128]{3,2,1,0:T(8,128)(2,1)}, u32[]{:S(2)}, u32[]{:S(2)}) async-start(bf16[32,15,16,128]{3,2,1,0:T(8,128)(2,1)} %bitcast.23), calls=%async_computation.2 | async-start | bytes 3932160 | tf_op jit(solution)/shard_map/all_to_all | solution.py:321
  160.1 46.1 %collective-permute-start.8 = (bf16[2,3,656,128]{3,2,1,0:T(8,128)(2,1)}, bf16[2,3,656,128]{3,2,1,0:T(8,128)(2,1)S(1)}, u32[]{:S(2)}, u32[]{:S(2)}) collective-permute-start(bf16[2,3,656,128]{3,2,1,0:T(8,128)(2,1)} %get-tuple-element.27), channel_id=1, source_target_pairs={{0,32},{32,64},{64,96},{96,128},{128,160},{160,192},{192,224},{224... | collective-permute-start | bytes 3022856 | tf_op jit(solution)/shard_map/ppermute | solution.py:391
  160.2 46.3 %collective-permute-start.9 = (bf16[2,3,656,128]{3,2,1,0:T(8,128)(2,1)}, bf16[2,3,656,128]{3,2,1,0:T(8,128)(2,1)}, u32[]{:S(2)}, u32[]{:S(2)}) collective-permute-start(bf16[2,3,656,128]{3,2,1,0:T(8,128)(2,1)} %get-tuple-element.28), channel_id=1, source_target_pairs={{0,224},{32,0},{64,32},{96,64},{128,96},{160,128},{192,160},{224,1... | collective-permute-start | bytes 3022856 | tf_op jit(solution)/shard_map/ppermute | solution.py:392
  191.0 21.4 %all-to-all-start.3 = ((bf16[32,6,16,128]{3,2,1,0:T(8,128)(2,1)}), bf16[32,6,16,128]{3,2,1,0:T(8,128)(2,1)}, u32[]{:S(2)}, u32[]{:S(2)}) async-start(bf16[32,6,16,128]{3,2,1,0:T(8,128)(2,1)} %bitcast.22), calls=%async_computation.3 | async-start | bytes 1572864 | tf_op jit(solution)/shard_map/all_to_all | solution.py:321
  212.3 16.9 %all-to-all-start.4 = ((bf16[32,3,16,128]{3,2,1,0:T(8,128)(2,1)}), bf16[32,3,16,128]{3,2,1,0:T(8,128)(2,1)S(1)}, u32[]{:S(2)}, u32[]{:S(2)}) async-start(bf16[32,3,16,128]{3,2,1,0:T(8,128)(2,1)} %bitcast.10), calls=%async_computation.4 | async-start | bytes 786432 | tf_op jit(solution)/shard_map/all_to_all | solution.py:321
  229.3 3.0 %collective-permute-start.12 = (bf16[4,3,16,128]{3,2,1,0:T(8,128)(2,1)S(1)}, bf16[4,3,16,128]{3,2,1,0:T(8,128)(2,1)S(1)}, u32[]{:S(2)}, u32[]{:S(2)}) collective-permute-start(bf16[4,3,16,128]{3,2,1,0:T(8,128)(2,1)S(1)} %bitcast_reduce_fusion), channel_id=1, source_target_pairs={{0,224},{8,232},{16,48},{24,56},{32,0},{40,8},{48,80},{56,88},{64,... | collective-permute-start | bytes 147464 | tf_op jit(solution)/shard_map/ppermute | solution.py:414

commit v7 on v6

--- a/solution.py
+++ b/solution.py
@@ -125,7 +125,7 @@
 
 
 def far_kernel(count, info_ref, mixed_ref, *refs):
-    rights, (out_ref, held, held_mixed, sems, mixed_sems) = refs[:count], refs[count:]
+    rights, (keep_ref, give_ref, held, held_mixed, sems, mixed_sems) = refs[:count], refs[count:]
     flipped = (1 - info_ref[Y * SLOTS + 1]) // 2
     copies = []
     mixed_copies = [
@@ -154,7 +154,10 @@
             copies[i].wait()
         for s, i in enumerate(slots):
             to = s + flipped * (CAP if s < CAP else -CAP)
-            out_ref[h, :, pl.ds(to, 1)] = right_times(held[i], held_mixed[h, s])[:, None]
+            total = right_times(held[i], held_mixed[h, s])
+            total = total.reshape((X, C) + total.shape[1:])
+            keep_ref[h, :, pl.ds(to, 1)] = jnp.where(flipped == 0, total[:, 0], total[:, 1])[:, None]
+            give_ref[h, :, pl.ds(to, 1)] = jnp.where(flipped == 0, total[:, 1], total[:, 0])[:, None]
 
 
 def guest_kernel(index_ref, low_ref, high_ref, one_ref, other_ref, out_ref):
@@ -238,11 +241,12 @@
 def far_products(info, mixed, arrived):
     slots, width = mixed.shape[1], mixed.shape[3]
     terms = mixed.shape[2] // width
+    out = jax.ShapeDtypeStruct((Y, X, slots, width // M, width), jnp.bfloat16)
     return pl.pallas_call(
         functools.partial(far_kernel, len(arrived)),
-        out_shape=jax.ShapeDtypeStruct((Y, M, slots, width // M, width), jnp.bfloat16),
+        out_shape=[out, out],
         in_specs=[pl.BlockSpec(memory_space=pltpu.SMEM)] + [IN_HBM] * (1 + len(arrived)),
-        out_specs=IN_VMEM,
+        out_specs=[IN_VMEM, IN_VMEM],
         scratch_shapes=[
             pltpu.VMEM((Y * slots, terms, 1, width, width), jnp.bfloat16),
             pltpu.VMEM(mixed.shape, jnp.bfloat16),
@@ -316,10 +320,11 @@
     )(target, end, settled)
 
 
-def exchange(part):
-    part = part.reshape((Y * M,) + part.shape[2:])
-    part = lax.all_to_all(part, ("y", "x", "c"), split_axis=0, concat_axis=0, tiled=True)
-    return part.reshape((Y, M) + part.shape[1:])
+def exchange(part, axes=("y", "x", "c")):
+    shape = part.shape
+    part = part.reshape((-1,) + shape[2:])
+    part = lax.all_to_all(part, axes, split_axis=0, concat_axis=0, tiled=True)
+    return part.reshape(shape)
 
 
 def add_up(part):
@@ -383,19 +388,21 @@
     far_left = hop(near_left[0], "y", 1)
     other = lax.ppermute(psi, "c", [(0, 1), (1, 0)])
     psi = (jnp.where(core == 0, psi, other), jnp.where(core == 0, other, psi))
-    second, psi = tie((second, psi))
+    second[1], psi = tie((second[1], psi))
     third = step(second)
     lefts = (left_environment, near_left[1], far_left, near_left[0])
     arrived = [right_environment] + first + second
     near, far_mixed, low, high = middle_products(info, psi, lefts, arrived)
     low = lax.ppermute(low, "z", [(i, (i + 1) % Z) for i in range(Z)])
     high = lax.ppermute(high, "z", [(i, (i - 1) % Z) for i in range(Z)])
-    far = far_products(info, far_mixed, third)
+    keep, give = far_products(info, far_mixed, third)
+    given = lax.ppermute(give, "c", [(0, 1), (1, 0)])
+    far = (keep.astype(jnp.float32) + given.astype(jnp.float32)).astype(jnp.bfloat16)
     far, near = tie((far, exchange(near)))
     sectors = [g[:, :, -1, 0].reshape(-1).astype(jnp.int32) for g in (low, high)]
     sectors = jnp.concatenate(sectors + [way[None].astype(jnp.int32)])
     guests = guest_products(sectors, low, high, third)
-    guests, far = tie((guests, exchange(far)))
+    guests, far = tie((guests, exchange(far, ("y", "x"))))
     guests = add_up(exchange(guests))
     flat = lambda part: part.reshape((-1,) + part.shape[2:])
     column, at = slot[0] // SLOTS, slot[0] % SLOTS

time: 234 us -> 234 us (level)
  waiting for transfers between devices: 125 us -> 122 us
  starting transfers between devices: 46.5 us -> 49.1 us
    ppermute x1, waiting for transfers between devices: 8.06 us -> 4.39 us  [on_device(): low = lax.ppermute(low, 'z', [(i, (i + 1) % Z) for i in range(Z)])]
    ppermute x1, waiting for transfers between devices: 3.12 us -> 0.62 us  [on_device(): other = lax.ppermute(psi, 'c', [(0, 1), (1, 0)])]
  transfers between devices with their start and end apart: 17 -> 18, of which waited for: 10 -> 12; matrix products, arithmetic and copies ran while one was open for 6% -> 6% of each run, Pallas kernels for 16% -> 16%
where the time goes in v7:
time: 234 us
  waiting for transfers between devices  122 us (52%)
  starting transfers between devices  49.1 us (21%)
  Pallas kernels  38.9 us (17%)
  other arithmetic  12.2 us (5%)
  blocking collectives  8.18 us (3%)
  local copies, waits for them, and re-layouts  2.9 us (1%)
    ppermute x9, waiting for transfers between devices, hop(): return lax.ppermute(moved, (axis, 'c'), ring(size, direction))  107 us
    pallas_call x1, Pallas kernels, middle_products(): pl.pallas_call(functools.partial(middle_kernel, near), out_shape=[out, tu...  25.1 us
    all_to_all x3, starting transfers between devices, exchange(): part = lax.all_to_all(part, axes, split_axis=0, concat_axis=0, tiled=True)  22.5 us
    ppermute x9, starting transfers between devices, hop(): return lax.ppermute(moved, (axis, 'c'), ring(size, direction))  16.9 us
    all_to_all x1, blocking collectives, on_device(): lax.all_to_all(sectors, 'y', split_axis=0, concat_axis=0, tiled=True)  8.18 us
    all_to_all x3, waiting for transfers between devices, exchange(): part = lax.all_to_all(part, axes, split_axis=0, concat_axis=0, tiled=True)  6.13 us
    pallas_call x1, Pallas kernels, far_products(): pl.pallas_call(functools.partial(far_kernel, len(arrived)), out_shape=[ou...  6.07 us
  transfers between devices with their start and end apart: 18, of which 12 were waited for; matrix products, arithmetic and copies ran while one was open for 6% of the time, Pallas kernels for 16%

profile of v7, /device:TPU:1, one launch (start us, length us, event | category | flops | bytes accessed | tf_op | source)
XLA Modules:
  0.0 233.6 jit_solution(678211409077016763)
XLA Ops:
  0.0 2.5 %collective-permute-start = (bf16[5,16,128,128]{3,2,1,0:T(8,128)(2,1)}, bf16[5,16,128,128]{3,2,1,0:T(8,128)(2,1)}, u32[]{:S(2)}, u32[]{:S(2)}) collective-permute-start(bf16[5,16,128,128]{3,2,1,0:T(8,128)(2,1)} %refs_6_.1), channel_id=1, source_target_pairs={{0,224},{1,33},{32,0},{33,65},{64,32},{65,97},{96,64},{97,129},{12... | collective-permute-start | bytes 7864328 | tf_op jit(solution)/shard_map/ppermute | solution.py:345
  2.5 4.0 %collective-permute-start.6 = (bf16[5,16,128,128]{3,2,1,0:T(8,128)(2,1)}, bf16[5,16,128,128]{3,2,1,0:T(8,128)(2,1)}, u32[]{:S(2)}, u32[]{:S(2)}) collective-permute-start(bf16[5,16,128,128]{3,2,1,0:T(8,128)(2,1)} %refs_6_.1), channel_id=1, source_target_pairs={{0,32},{1,225},{32,64},{33,1},{64,96},{65,33},{96,128},{97,65},{12... | collective-permute-start | bytes 7864328 | tf_op jit(solution)/shard_map/ppermute | solution.py:345
  7.1 8.2 %all_to_all.29 = s32[4,1,64]{2,1,0:T(1,128)S(1)} all-to-all(s32[4,1,64]{2,1,0:T(1,128)S(1)} %broadcast_in_dim.122), channel_id=1, replica_groups=mesh['z'=8,'y'=4,'x'=4,'c'=2] {'y'}, dimensions={0} | all-to-all | bytes 2048 | tf_op jit(solution)/shard_map/all_to_all | solution.py:378
  18.5 2.0 gather_fusion
  20.5 4.4 %all-to-all-start.1 = ((bf16[4,12,128,128]{3,2,1,0:T(8,128)(2,1)}), bf16[4,12,128,128]{3,2,1,0:T(8,128)(2,1)}, u32[]{:S(2)}, u32[]{:S(2)}) async-start(bf16[4,12,128,128]{3,2,1,0:T(8,128)(2,1)} %bitcast.21), calls=%async_computation.1 | async-start | bytes 3145728 | tf_op jit(solution)/shard_map/all_to_all | solution.py:387
  24.9 35.1 %collective-permute-done.refs_8_ = bf16[5,16,128,128]{3,2,1,0:T(8,128)(2,1)} collective-permute-done((bf16[5,16,128,128]{3,2,1,0:T(8,128)(2,1)}, bf16[5,16,128,128]{3,2,1,0:T(8,128)(2,1)}, u32[]{:S(2)}, u32[]{:S(2)}) %collective-permute-start) | collective-permute-done | bytes 2621472 | tf_op jit(solution)/shard_map/ppermute | solution.py:345
  60.0 2.4 %collective-permute-done.6.refs_7_ = bf16[5,16,128,128]{3,2,1,0:T(8,128)(2,1)} collective-permute-done((bf16[5,16,128,128]{3,2,1,0:T(8,128)(2,1)}, bf16[5,16,128,128]{3,2,1,0:T(8,128)(2,1)}, u32[]{:S(2)}, u32[]{:S(2)}) %collective-permute-start.6) | collective-permute-done | bytes 2621472 | tf_op jit(solution)/shard_map/ppermute | solution.py:345
  62.4 3.4 %collective-permute-start.7 = (bf16[5,16,128,128]{3,2,1,0:T(8,128)(2,1)}, bf16[5,16,128,128]{3,2,1,0:T(8,128)(2,1)}, u32[]{:S(2)}, u32[]{:S(2)}) collective-permute-start(bf16[5,16,128,128]{3,2,1,0:T(8,128)(2,1)} %collective-permute-done.6.refs_7_), channel_id=1, source_target_pairs={{0,32},{1,225},{32,64},{33,1},{64,96},{65,33},{96,128},{97,65},{12... | collective-permute-start | bytes 7864328 | tf_op jit(solution)/shard_map/ppermute | solution.py:345
  65.8 1.8 collective-permute-start.2
  67.7 1.3 collective-permute-start.3
  69.0 1.5 collective-permute-start.5
  71.1 3.7 %broadcast_select_fusion = (bf16[4,12,128,128]{3,2,1,0:T(8,128)(2,1)}, bf16[4,12,128,128]{3,2,1,0:T(8,128)(2,1)}) fusion(bf16[4,12,128,128]{3,2,1,0:T(8,128)(2,1)} %collective-permute-done.2, bf16[4,12,128,128]{3,2,1,0:T(8,128)(2,1)} %all-to-all-done.1, pred[]{:T(512)S(6)} %eq.228), kind=kLoop, calls=%fused_computation.1 | loop fusion | flops 1572864 | bytes 6291457 | tf_op jit(solution)/shard_map/jit(_where)/select_n | solution.py:390
  74.8 39.0 %collective-permute-done.1.refs_10_ = bf16[5,16,128,128]{3,2,1,0:T(8,128)(2,1)} collective-permute-done((bf16[5,16,128,128]{3,2,1,0:T(8,128)(2,1)}, bf16[5,16,128,128]{3,2,1,0:T(8,128)(2,1)}, u32[]{:S(2)}, u32[]{:S(2)}) %collective-permute-start.1) | collective-permute-done | bytes 2621472 | tf_op jit(solution)/shard_map/ppermute | solution.py:345
  113.8 7.1 %collective-permute-done.7.refs_9_ = bf16[5,16,128,128]{3,2,1,0:T(8,128)(2,1)} collective-permute-done((bf16[5,16,128,128]{3,2,1,0:T(8,128)(2,1)}, bf16[5,16,128,128]{3,2,1,0:T(8,128)(2,1)}, u32[]{:S(2)}, u32[]{:S(2)}) %collective-permute-start.7) | collective-permute-done | bytes 2621472 | tf_op jit(solution)/shard_map/ppermute | solution.py:345
  120.9 3.4 %collective-permute-start.10 = (bf16[5,16,128,128]{3,2,1,0:T(8,128)(2,1)}, bf16[5,16,128,128]{3,2,1,0:T(8,128)(2,1)}, u32[]{:S(2)}, u32[]{:S(2)}) collective-permute-start(bf16[5,16,128,128]{3,2,1,0:T(8,128)(2,1)} %collective-permute-done.7.refs_9_), channel_id=1, source_target_pairs={{0,32},{1,225},{32,64},{33,1},{64,96},{65,33},{96,128},{97,65},{12... | collective-permute-start | bytes 7864328 | tf_op jit(solution)/shard_map/ppermute | solution.py:345
  125.4 2.0 collective-permute-done.5.refs_4_
  127.4 25.1 %shard_map.46 = (bf16[4,8,15,16,128]{4,3,2,1,0:T(8,128)(2,1)}, bf16[4,6,640,128]{3,2,1,0:T(8,128)(2,1)}, bf16[2,3,656,128]{3,2,1,0:T(8,128)(2,1)}, bf16[2,3,656,128]{3,2,1,0:T(8,128)(2,1)}) custom-call(s32[98]{0:T(128)} %pad_add_fusion.info_ref, bf16[4,12,128,128]{3,2,1,0:T(8,128)(2,1)} %get-tuple-element.23.refs_0_, ...), custom_call_target="tpu_custom_call" | custom-call | flops 4026531840 | bytes 37748736 | tf_op jit(solution)/shard_map/pallas_call | solution.py:204
  152.5 8.3 %all-to-all-start.2 = ((bf16[32,15,16,128]{3,2,1,0:T(8,128)(2,1)}), bf16[32,15,16,128]{3,2,1,0:T(8,128)(2,1)}, u32[]{:S(2)}, u32[]{:S(2)}) async-start(bf16[32,15,16,128]{3,2,1,0:T(8,128)(2,1)} %bitcast.22), calls=%async_computation.2 | async-start | bytes 3932160 | tf_op jit(solution)/shard_map/all_to_all | solution.py:326
  160.8 2.7 %collective-permute-start.9 = (bf16[2,3,656,128]{3,2,1,0:T(8,128)(2,1)}, bf16[2,3,656,128]{3,2,1,0:T(8,128)(2,1)S(1)}, u32[]{:S(2)}, u32[]{:S(2)}) collective-permute-start(bf16[2,3,656,128]{3,2,1,0:T(8,128)(2,1)} %get-tuple-element.28), channel_id=1, source_target_pairs={{0,224},{32,0},{64,32},{96,64},{128,96},{160,128},{192,160},{224,1... | collective-permute-start | bytes 3022856 | tf_op jit(solution)/shard_map/ppermute | solution.py:397
  163.6 14.8 %collective-permute-done.10.one_ref.refs_0_ = bf16[5,16,128,128]{3,2,1,0:T(8,128)(2,1)} collective-permute-done((bf16[5,16,128,128]{3,2,1,0:T(8,128)(2,1)}, bf16[5,16,128,128]{3,2,1,0:T(8,128)(2,1)}, u32[]{:S(2)}, u32[]{:S(2)}) %collective-permute-start.10) | collective-permute-done | bytes 2621472 | tf_op jit(solution)/shard_map/ppermute | solution.py:345
  178.4 6.3 %collective-permute-done.11.other_ref.refs_1_ = bf16[5,16,128,128]{3,2,1,0:T(8,128)(2,1)} collective-permute-done((bf16[5,16,128,128]{3,2,1,0:T(8,128)(2,1)}, bf16[5,16,128,128]{3,2,1,0:T(8,128)(2,1)}, u32[]{:S(2)}, u32[]{:S(2)}) %collective-permute-start.11) | collective-permute-done | bytes 2621472 | tf_op jit(solution)/shard_map/ppermute | solution.py:345
  184.7 6.1 %shard_map.48 = (bf16[4,4,6,16,128]{4,3,2,1,0:T(8,128)(2,1)}, bf16[4,4,6,16,128]{4,3,2,1,0:T(8,128)(2,1)}) custom-call(s32[98]{0:T(128)} %pad_add_fusion.info_ref, bf16[4,6,640,128]{3,2,1,0:T(8,128)(2,1)} %get-tuple-element.29.mixed_ref, bf16[5,16,128,128]{3,2,1,0:T(8,128)(2,1)} %collective-permute-done.10.one_ref.refs_0_, ...), custom_call_target="tpu_custom_call" | custom-call | flops 1006632960 | bytes 9437184 | tf_op jit(solution)/shard_map/pallas_call | solution.py:245
  191.1 1.7 collective-permute-done.12
  192.8 1.8 add_convert_fusion
  194.6 6.7 %all-to-all-start.3 = ((bf16[16,6,16,128]{3,2,1,0:T(8,128)(2,1)}), bf16[16,6,16,128]{3,2,1,0:T(8,128)(2,1)S(1)}, u32[]{:S(2)}, u32[]{:S(2)}) async-start(bf16[16,6,16,128]{3,2,1,0:T(8,128)(2,1)} %bitcast.24), calls=%async_computation.3 | async-start | bytes 786432 | tf_op jit(solution)/shard_map/all_to_all | solution.py:326
  201.7 4.4 %collective-permute-done.8.low_ref = bf16[2,3,656,128]{3,2,1,0:T(8,128)(2,1)} collective-permute-done((bf16[2,3,656,128]{3,2,1,0:T(8,128)(2,1)}, bf16[2,3,656,128]{3,2,1,0:T(8,128)(2,1)}, u32[]{:S(2)}, u32[]{:S(2)}) %collective-permute-start.8) | collective-permute-done | bytes 1007648 | tf_op jit(solution)/shard_map/ppermute | solution.py:396
  207.1 4.4 %shard_map.47 = bf16[4,8,3,16,128]{4,3,2,1,0:T(8,128)(2,1)} custom-call(s32[13]{0:T(128)S(1)} %pad_add_fusion.1.index_ref, bf16[2,3,656,128]{3,2,1,0:T(8,128)(2,1)} %collective-permute-done.8.low_ref, bf16[2,3,656,128]{3,2,1,0:T(8,128)(2,1)S(1)} %collective-permute-done.9.high_ref, bf16[5,16,128,128]{3,2,1,0:T(8,128)(2,1)} %collective-permute-done.10.one_ref.refs_0_, ...), custom_call_target="tpu_custom_call" | custom-call | flops 503316480 | bytes 4718592 | tf_op jit(solution)/shard_map/pallas_call | solution.py:263
  211.5 7.5 %all-to-all-start.4 = ((bf16[32,3,16,128]{3,2,1,0:T(8,128)(2,1)}), bf16[32,3,16,128]{3,2,1,0:T(8,128)(2,1)S(1)}, u32[]{:S(2)}, u32[]{:S(2)}) async-start(bf16[32,3,16,128]{3,2,1,0:T(8,128)(2,1)} %bitcast.10), calls=%async_computation.4 | async-start | bytes 786432 | tf_op jit(solution)/shard_map/all_to_all | solution.py:326
  219.0 1.9 reduce_sum.80
  220.9 2.1 shard_map.49.settled_ref
  223.0 6.1 %all-to-all-done.4 = bf16[32,3,16,128]{3,2,1,0:T(8,128)(2,1)S(1)} async-done(((bf16[32,3,16,128]{3,2,1,0:T(8,128)(2,1)}), bf16[32,3,16,128]{3,2,1,0:T(8,128)(2,1)S(1)}, u32[]{:S(2)}, u32[]{:S(2)}) %all-to-all-start.4) | async-done | bytes 393248 | tf_op jit(solution)/shard_map/all_to_all | solution.py:326
  229.8 2.4 %collective-permute-done.13 = bf16[4,3,16,128]{3,2,1,0:T(8,128)(2,1)S(1)} collective-permute-done((bf16[4,3,16,128]{3,2,1,0:T(8,128)(2,1)S(1)}, bf16[4,3,16,128]{3,2,1,0:T(8,128)(2,1)S(1)}, u32[]{:S(2)}, u32[]{:S(2)}) %collective-permute-start.13) | collective-permute-done | bytes 49184 | tf_op jit(solution)/shard_map/ppermute | solution.py:421
  (41 shorter events, 9.2 us)
Async XLA Ops:
  0.0 18.5 %copy-start = (bf16[64,128,128]{2,1,0:T(8,128)(2,1)S(1)}, bf16[64,128,128]{2,1,0:T(8,128)(2,1)}, u32[]{:S(2)}) copy-start(bf16[64,128,128]{2,1,0:T(8,128)(2,1)} %param.4) | copy-start | bytes 6291460
  0.0 60.0 %collective-permute-start = (bf16[5,16,128,128]{3,2,1,0:T(8,128)(2,1)}, bf16[5,16,128,128]{3,2,1,0:T(8,128)(2,1)}, u32[]{:S(2)}, u32[]{:S(2)}) collective-permute-start(bf16[5,16,128,128]{3,2,1,0:T(8,128)(2,1)} %refs_6_.1), channel_id=1, source_target_pairs={{0,224},{1,33},{32,0},{33,65},{64,32},{65,97},{96,64},{97,129},{12... | collective-permute-start | bytes 7864328 | tf_op jit(solution)/shard_map/ppermute | solution.py:345
  2.5 60.0 %collective-permute-start.6 = (bf16[5,16,128,128]{3,2,1,0:T(8,128)(2,1)}, bf16[5,16,128,128]{3,2,1,0:T(8,128)(2,1)}, u32[]{:S(2)}, u32[]{:S(2)}) collective-permute-start(bf16[5,16,128,128]{3,2,1,0:T(8,128)(2,1)} %refs_6_.1), channel_id=1, source_target_pairs={{0,32},{1,225},{32,64},{33,1},{64,96},{65,33},{96,128},{97,65},{12... | collective-permute-start | bytes 7864328 | tf_op jit(solution)/shard_map/ppermute | solution.py:345
  15.3 53.6 %collective-permute-start.4 = (bf16[5,16,128,128]{3,2,1,0:T(8,128)(2,1)}, bf16[5,16,128,128]{3,2,1,0:T(8,128)(2,1)}, u32[]{:S(2)}, u32[]{:S(2)}) collective-permute-start(bf16[5,16,128,128]{3,2,1,0:T(8,128)(2,1)} %refs_2_), channel_id=1, source_target_pairs={{0,8},{1,25},{8,16},{9,1},{16,24},{17,9},{24,0},{25,17},{2,10},{3,... | collective-permute-start | bytes 7864328 | tf_op jit(solution)/shard_map/ppermute | solution.py:345
  20.5 45.4 %all-to-all-start.1 = ((bf16[4,12,128,128]{3,2,1,0:T(8,128)(2,1)}), bf16[4,12,128,128]{3,2,1,0:T(8,128)(2,1)}, u32[]{:S(2)}, u32[]{:S(2)}) async-start(bf16[4,12,128,128]{3,2,1,0:T(8,128)(2,1)} %bitcast.21), calls=%async_computation.1 | async-start | bytes 3145728 | tf_op jit(solution)/shard_map/all_to_all | solution.py:387
  60.0 53.8 %collective-permute-start.1 = (bf16[5,16,128,128]{3,2,1,0:T(8,128)(2,1)}, bf16[5,16,128,128]{3,2,1,0:T(8,128)(2,1)}, u32[]{:S(2)}, u32[]{:S(2)}) collective-permute-start(bf16[5,16,128,128]{3,2,1,0:T(8,128)(2,1)} %collective-permute-done.refs_8_), channel_id=1, source_target_pairs={{0,224},{1,33},{32,0},{33,65},{64,32},{65,97},{96,64},{97,129},{12... | collective-permute-start | bytes 7864328 | tf_op jit(solution)/shard_map/ppermute | solution.py:345
  62.4 58.4 %collective-permute-start.7 = (bf16[5,16,128,128]{3,2,1,0:T(8,128)(2,1)}, bf16[5,16,128,128]{3,2,1,0:T(8,128)(2,1)}, u32[]{:S(2)}, u32[]{:S(2)}) collective-permute-start(bf16[5,16,128,128]{3,2,1,0:T(8,128)(2,1)} %collective-permute-done.6.refs_7_), channel_id=1, source_target_pairs={{0,32},{1,225},{32,64},{33,1},{64,96},{65,33},{96,128},{97,65},{12... | collective-permute-start | bytes 7864328 | tf_op jit(solution)/shard_map/ppermute | solution.py:345
  65.8 5.2 %collective-permute-start.2 = (bf16[4,12,128,128]{3,2,1,0:T(8,128)(2,1)}, bf16[4,12,128,128]{3,2,1,0:T(8,128)(2,1)}, u32[]{:S(2)}, u32[]{:S(2)}) collective-permute-start(bf16[4,12,128,128]{3,2,1,0:T(8,128)(2,1)} %all-to-all-done.1), channel_id=1, source_target_pairs={{0,1},{1,0},{2,3},{3,2},{4,5},{5,4},{6,7},{7,6},{8,9},{9,8},{10,11... | collective-permute-start | bytes 4718600 | tf_op jit(solution)/shard_map/ppermute | solution.py:389
  67.7 57.7 %collective-permute-start.3 = (bf16[5,16,128,128]{3,2,1,0:T(8,128)(2,1)}, bf16[5,16,128,128]{3,2,1,0:T(8,128)(2,1)}, u32[]{:S(2)}, u32[]{:S(2)}) collective-permute-start(bf16[5,16,128,128]{3,2,1,0:T(8,128)(2,1)} %refs_2_), channel_id=1, source_target_pairs={{0,24},{1,9},{8,0},{9,17},{16,8},{17,25},{24,16},{25,1},{2,26},{3,... | collective-permute-start | bytes 7864328 | tf_op jit(solution)/shard_map/ppermute | solution.py:345
  69.0 58.5 %collective-permute-start.5 = (bf16[5,16,128,128]{3,2,1,0:T(8,128)(2,1)}, bf16[5,16,128,128]{3,2,1,0:T(8,128)(2,1)}, u32[]{:S(2)}, u32[]{:S(2)}) collective-permute-start(bf16[5,16,128,128]{3,2,1,0:T(8,128)(2,1)} %collective-permute-done.4.refs_5_), channel_id=1, source_target_pairs={{0,8},{1,25},{8,16},{9,1},{16,24},{17,9},{24,0},{25,17},{2,10},{3,... | collective-permute-start | bytes 7864328 | tf_op jit(solution)/shard_map/ppermute | solution.py:345
  120.9 57.5 %collective-permute-start.10 = (bf16[5,16,128,128]{3,2,1,0:T(8,128)(2,1)}, bf16[5,16,128,128]{3,2,1,0:T(8,128)(2,1)}, u32[]{:S(2)}, u32[]{:S(2)}) collective-permute-start(bf16[5,16,128,128]{3,2,1,0:T(8,128)(2,1)} %collective-permute-done.7.refs_9_), channel_id=1, source_target_pairs={{0,32},{1,225},{32,64},{33,1},{64,96},{65,33},{96,128},{97,65},{12... | collective-permute-start | bytes 7864328 | tf_op jit(solution)/shard_map/ppermute | solution.py:345
  124.3 60.4 %collective-permute-start.11 = (bf16[5,16,128,128]{3,2,1,0:T(8,128)(2,1)}, bf16[5,16,128,128]{3,2,1,0:T(8,128)(2,1)}, u32[]{:S(2)}, u32[]{:S(2)}) collective-permute-start(bf16[5,16,128,128]{3,2,1,0:T(8,128)(2,1)} %collective-permute-done.1.refs_10_), channel_id=1, source_target_pairs={{0,224},{1,33},{32,0},{33,65},{64,32},{65,97},{96,64},{97,129},{12... | collective-permute-start | bytes 7864328 | tf_op jit(solution)/shard_map/ppermute | solution.py:345
  152.5 42.1 %all-to-all-start.2 = ((bf16[32,15,16,128]{3,2,1,0:T(8,128)(2,1)}), bf16[32,15,16,128]{3,2,1,0:T(8,128)(2,1)}, u32[]{:S(2)}, u32[]{:S(2)}) async-start(bf16[32,15,16,128]{3,2,1,0:T(8,128)(2,1)} %bitcast.22), calls=%async_computation.2 | async-start | bytes 3932160 | tf_op jit(solution)/shard_map/all_to_all | solution.py:326
  160.8 40.5 %collective-permute-start.9 = (bf16[2,3,656,128]{3,2,1,0:T(8,128)(2,1)}, bf16[2,3,656,128]{3,2,1,0:T(8,128)(2,1)S(1)}, u32[]{:S(2)}, u32[]{:S(2)}) collective-permute-start(bf16[2,3,656,128]{3,2,1,0:T(8,128)(2,1)} %get-tuple-element.28), channel_id=1, source_target_pairs={{0,224},{32,0},{64,32},{96,64},{128,96},{160,128},{192,160},{224,1... | collective-permute-start | bytes 3022856 | tf_op jit(solution)/shard_map/ppermute | solution.py:397
  163.6 42.5 %collective-permute-start.8 = (bf16[2,3,656,128]{3,2,1,0:T(8,128)(2,1)}, bf16[2,3,656,128]{3,2,1,0:T(8,128)(2,1)}, u32[]{:S(2)}, u32[]{:S(2)}) collective-permute-start(bf16[2,3,656,128]{3,2,1,0:T(8,128)(2,1)} %get-tuple-element.27), channel_id=1, source_target_pairs={{0,32},{32,64},{64,96},{96,128},{128,160},{160,192},{192,224},{224... | collective-permute-start | bytes 3022856 | tf_op jit(solution)/shard_map/ppermute | solution.py:396
  190.8 2.0 collective-permute-start.12
  194.6 16.8 %all-to-all-start.3 = ((bf16[16,6,16,128]{3,2,1,0:T(8,128)(2,1)}), bf16[16,6,16,128]{3,2,1,0:T(8,128)(2,1)S(1)}, u32[]{:S(2)}, u32[]{:S(2)}) async-start(bf16[16,6,16,128]{3,2,1,0:T(8,128)(2,1)} %bitcast.24), calls=%async_computation.3 | async-start | bytes 786432 | tf_op jit(solution)/shard_map/all_to_all | solution.py:326
  211.5 17.7 %all-to-all-start.4 = ((bf16[32,3,16,128]{3,2,1,0:T(8,128)(2,1)}), bf16[32,3,16,128]{3,2,1,0:T(8,128)(2,1)S(1)}, u32[]{:S(2)}, u32[]{:S(2)}) async-start(bf16[32,3,16,128]{3,2,1,0:T(8,128)(2,1)} %bitcast.10), calls=%async_computation.4 | async-start | bytes 786432 | tf_op jit(solution)/shard_map/all_to_all | solution.py:326
  229.2 3.0 %collective-permute-start.13 = (bf16[4,3,16,128]{3,2,1,0:T(8,128)(2,1)S(1)}, bf16[4,3,16,128]{3,2,1,0:T(8,128)(2,1)S(1)}, u32[]{:S(2)}, u32[]{:S(2)}) collective-permute-start(bf16[4,3,16,128]{3,2,1,0:T(8,128)(2,1)S(1)} %bitcast_reduce_fusion), channel_id=1, source_target_pairs={{0,224},{8,232},{16,48},{24,56},{32,0},{40,8},{48,80},{56,88},{64,... | collective-permute-start | bytes 147464 | tf_op jit(solution)/shard_map/ppermute | solution.py:421
